TPU v7x, 256 devices: a whole 4x4x8 slice. The times are simulated.
256 devices in a mesh: enc: 32 (over z_lo, x, core), seq: 8 (over z_hi, y).
Axes of the slice: x: 4, y: 4, z: 8 (z_hi: 2, z_lo: 4; z = z_hi * 4 + z_lo), core: 2. Of those that a mesh axis runs over, the one named last changes fastest.
Arguments:
- acts_clip: bfloat16 [8192, 1024], P('seq'), may hold values from -6 to 6
- acts_convnext: bfloat16 [8192, 3072], P('seq'), may hold values from -6 to 6
- acts_eva: bfloat16 [8192, 1024], P('seq'), may hold values from -6 to 6
- acts_sam: bfloat16 [8192, 1024], P('seq'), may hold values from -6 to 6
- cotangent: bfloat16 [8192, 5120], P('seq'), may hold values from -6 to 6
- weight_clip: bfloat16 [1024, 1024], P('seq', 'enc'), may hold values from -0.1875 to 0.1875
- weight_convnext: bfloat16 [3072, 3072], P('seq', 'enc'), may hold values from -0.109375 to 0.109375
- weight_eva: bfloat16 [1024, 1024], P('seq', 'enc'), may hold values from -0.1875 to 0.1875
- weight_sam: bfloat16 [1024, 1024], P('seq', 'enc'), may hold values from -0.1875 to 0.1875
- proj_clip: bfloat16 [5120, 1024], P('seq', 'enc'), may hold values from -0.078125 to 0.078125
- proj_convnext: bfloat16 [5120, 3072], P('seq', 'enc'), may hold values from -0.078125 to 0.078125
- proj_eva: bfloat16 [5120, 1024], P('seq', 'enc'), may hold values from -0.078125 to 0.078125
- proj_sam: bfloat16 [5120, 1024], P('seq', 'enc'), may hold values from -0.078125 to 0.078125
Outputs:
- grad_acts_clip: bfloat16 [8192, 1024], P('seq', 'enc')
- grad_acts_convnext: bfloat16 [8192, 3072], P('seq', 'enc')
- grad_acts_eva: bfloat16 [8192, 1024], P('seq', 'enc')
- grad_acts_sam: bfloat16 [8192, 1024], P('seq', 'enc')
- grad_weight_clip: float32 [1024, 1024], P('seq', 'enc')
- grad_weight_convnext: float32 [3072, 3072], P('seq', 'enc')
- grad_weight_eva: float32 [1024, 1024], P('seq', 'enc')
- grad_weight_sam: float32 [1024, 1024], P('seq', 'enc')
- grad_proj_clip: float32 [5120, 1024], P('seq', 'enc')
- grad_proj_convnext: float32 [5120, 3072], P('seq', 'enc')
- grad_proj_eva: float32 [5120, 1024], P('seq', 'enc')
- grad_proj_sam: float32 [5120, 1024], P('seq', 'enc')
All inputs are finite; a program needn't handle non-finite values.
Results may differ from a plain program's by a relative error of at most 0.0035.
Values may be sent and summed in bfloat16 or wider, within the bound.
No kernel may reach another device: no remote copies, remote signals or barrier semaphores. Data moves between devices by JAX's collectives and lax.ppermute only.
A program may use at most 128 MiB of HBM per device.

v0:
```python
import jax
import jax.numpy as jnp
from jax import lax
from jax.sharding import PartitionSpec as P

ROOT_HALF = 0.7071067811865476
INV_ROOT_TAU = 0.3989422804014327


def normal_cdf(values):
    return 0.5 * (1.0 + lax.erf(values * ROOT_HALF))


def slope_of(values):
    return normal_cdf(values) + values * jnp.exp(-0.5 * values * values) * INV_ROOT_TAU


def contract_rows(left, right):
    return lax.dot_general(
        left, right, (((0,), (0,)), ((), ())), preferred_element_type=jnp.float32
    )


def contract_cols(left, right):
    return lax.dot_general(
        left, right, (((1,), (1,)), ((), ())), preferred_element_type=jnp.float32
    )


def body(
    acts_clip,
    acts_convnext,
    acts_eva,
    acts_sam,
    cotangent,
    weight_clip,
    weight_convnext,
    weight_eva,
    weight_sam,
    proj_clip,
    proj_convnext,
    proj_eva,
    proj_sam,
):
    layer_inputs = (acts_clip, acts_convnext, acts_eva, acts_sam)
    group_pos = lax.axis_index("enc")
    seq_count = lax.axis_size("seq")
    token_count = cotangent.shape[0]
    factor = float(seq_count * token_count) ** (-0.5)
    gathered = (
        lax.all_gather(weight_clip, "seq", axis=0, tiled=True),
        lax.all_gather(weight_convnext, "seq", axis=0, tiled=True),
        lax.all_gather(weight_eva, "seq", axis=0, tiled=True),
        lax.all_gather(weight_sam, "seq", axis=0, tiled=True),
        lax.all_gather(proj_clip, "seq", axis=0, tiled=True),
        lax.all_gather(proj_convnext, "seq", axis=0, tiled=True),
        lax.all_gather(proj_eva, "seq", axis=0, tiled=True),
        lax.all_gather(proj_sam, "seq", axis=0, tiled=True),
    )
    weight_cols = gathered[:4]
    proj_cols = gathered[4:]
    back_grads = []
    hidden_grads = []
    partial_terms = []
    weight_grads = []
    proj_grads = []
    for encoder in range(4):
        layer_input = layer_inputs[encoder]
        col_width = weight_cols[encoder].shape[1]
        own_input = lax.dynamic_slice_in_dim(layer_input, group_pos * col_width, col_width, 1)
        pre_act = jnp.dot(layer_input, weight_cols[encoder], preferred_element_type=jnp.float32)
        feature = (own_input.astype(jnp.float32) + pre_act * normal_cdf(pre_act)).astype(
            jnp.bfloat16
        )
        back_grad = jnp.dot(cotangent, proj_cols[encoder], preferred_element_type=jnp.float32)
        hidden_grad = (back_grad * slope_of(pre_act)).astype(jnp.bfloat16)

        def weight_term(start, count, source=layer_input, hidden=hidden_grad):
            return contract_rows(source, hidden)

        def proj_term(start, count, feats=feature):
            return contract_rows(cotangent, feats)

        weight_sum = lax.psum_scatter(
            weight_term(jnp.int32(0), lax.axis_size("seq") * (layer_input.shape[1] // seq_count)),
            "seq",
            scatter_dimension=0,
            tiled=True,
        )
        proj_sum = lax.psum_scatter(
            proj_term(jnp.int32(0), lax.axis_size("seq") * (cotangent.shape[1] // seq_count)),
            "seq",
            scatter_dimension=0,
            tiled=True,
        )
        weight_grads.append(weight_sum * factor)
        proj_grads.append(proj_sum * factor)
        back_grads.append(back_grad)
        hidden_grads.append(hidden_grad)
        partial_terms.append(contract_cols(hidden_grad, weight_cols[encoder]))
    input_grads = []
    summed = (
        lax.psum_scatter(partial_terms[0], "enc", scatter_dimension=1, tiled=True),
        lax.psum_scatter(partial_terms[1], "enc", scatter_dimension=1, tiled=True),
        lax.psum_scatter(partial_terms[2], "enc", scatter_dimension=1, tiled=True),
        lax.psum_scatter(partial_terms[3], "enc", scatter_dimension=1, tiled=True),
    )
    for encoder in range(4):
        input_grads.append((back_grads[encoder] + summed[encoder]).astype(jnp.bfloat16))
    return (
        input_grads[0],
        input_grads[1],
        input_grads[2],
        input_grads[3],
        weight_grads[0],
        weight_grads[1],
        weight_grads[2],
        weight_grads[3],
        proj_grads[0],
        proj_grads[1],
        proj_grads[2],
        proj_grads[3],
    )


def solution(mesh):
    placed = (
        P("seq", None),
        P("seq", None),
        P("seq", None),
        P("seq", None),
        P("seq", None),
        P("seq", "enc"),
        P("seq", "enc"),
        P("seq", "enc"),
        P("seq", "enc"),
        P("seq", "enc"),
        P("seq", "enc"),
        P("seq", "enc"),
        P("seq", "enc"),
    )
    return jax.shard_map(
        body,
        mesh=mesh,
        in_specs=placed,
        out_specs=(
            P("seq", "enc"),
            P("seq", "enc"),
            P("seq", "enc"),
            P("seq", "enc"),
            P("seq", "enc"),
            P("seq", "enc"),
            P("seq", "enc"),
            P("seq", "enc"),
            P("seq", "enc"),
            P("seq", "enc"),
            P("seq", "enc"),
            P("seq", "enc"),
        ),
        check_vma=False,
    )
```

profile of v0, /device:TPU:1, one launch (start us, length us, event | category | flops | bytes accessed | tf_op | source)
XLA Modules:
  0.0 1423.2 jit_solution(11041867211965298147)
XLA Ops:
  7.2 41.4 %all_gather.24 = bf16[5120,32]{0,1:T(8,128)(2,1)S(1)} all-gather(bf16[640,32]{0,1:T(8,128)(2,1)} %param.22), channel_id=1, replica_groups=mesh['enc'=32,'seq'=8] {'seq'}, dimensions={0}, use_global_device_ids=true | all-gather | bytes 368640 | tf_op jit(solution)/shard_map/all_gather | solution.py:55
  48.6 35.2 %all_gather.25 = bf16[1024,32]{0,1:T(8,128)(2,1)S(1)} all-gather(bf16[128,32]{0,1:T(8,128)(2,1)} %param.18), channel_id=1, replica_groups=mesh['enc'=32,'seq'=8] {'seq'}, dimensions={0}, use_global_device_ids=true | all-gather | bytes 73728 | tf_op jit(solution)/shard_map/all_gather | solution.py:51
  83.8 7.2 fusion.36
  93.0 38.4 %all_gather.28 = bf16[5120,32]{0,1:T(8,128)(2,1)S(1)} all-gather(bf16[640,32]{0,1:T(8,128)(2,1)S(1)} %copy-done.17), channel_id=1, replica_groups=mesh['enc'=32,'seq'=8] {'seq'}, dimensions={0}, use_global_device_ids=true | all-gather | bytes 368640 | tf_op jit(solution)/shard_map/all_gather | solution.py:57
  131.3 7.2 fusion.40
  138.6 35.0 %all_gather.29 = bf16[1024,32]{0,1:T(8,128)(2,1)S(1)} all-gather(bf16[128,32]{0,1:T(8,128)(2,1)S(1)} %copy-done.19), channel_id=1, replica_groups=mesh['enc'=32,'seq'=8] {'seq'}, dimensions={0}, use_global_device_ids=true | all-gather | bytes 73728 | tf_op jit(solution)/shard_map/all_gather | solution.py:53
  175.6 38.5 %all_gather.30 = bf16[5120,32]{0,1:T(8,128)(2,1)S(1)} all-gather(bf16[640,32]{0,1:T(8,128)(2,1)S(1)} %copy-done.18), channel_id=1, replica_groups=mesh['enc'=32,'seq'=8] {'seq'}, dimensions={0}, use_global_device_ids=true | all-gather | bytes 368640 | tf_op jit(solution)/shard_map/all_gather | solution.py:58
  214.1 7.2 fusion.42
  221.3 35.0 %all_gather.31 = bf16[1024,32]{0,1:T(8,128)(2,1)S(1)} all-gather(bf16[128,32]{0,1:T(8,128)(2,1)S(1)} %copy-done.20), channel_id=1, replica_groups=mesh['enc'=32,'seq'=8] {'seq'}, dimensions={0}, use_global_device_ids=true | all-gather | bytes 73728 | tf_op jit(solution)/shard_map/all_gather | solution.py:54
  266.7 6.8 convolution_bitcast_fusion.2
  274.8 6.7 convolution_bitcast_fusion.1
  281.6 38.4 %all_gather.27 = bf16[3072,96]{0,1:T(8,128)(2,1)S(1)} all-gather(bf16[384,96]{0,1:T(8,128)(2,1)S(1)} %copy-done.16), channel_id=1, replica_groups=mesh['enc'=32,'seq'=8] {'seq'}, dimensions={0}, use_global_device_ids=true | all-gather | bytes 663552 | tf_op jit(solution)/shard_map/all_gather | solution.py:52
  324.9 41.4 %all_gather.26 = bf16[5120,96]{0,1:T(8,128)(2,1)S(1)} all-gather(bf16[640,96]{0,1:T(8,128)(2,1)S(1)} %copy-done.15), channel_id=1, replica_groups=mesh['enc'=32,'seq'=8] {'seq'}, dimensions={0}, use_global_device_ids=true | all-gather | bytes 1105920 | tf_op jit(solution)/shard_map/all_gather | solution.py:56
  366.3 7.6 fusion.38
  380.1 7.3 convolution_bitcast_fusion
  409.3 43.9 %reduce-scatter.29.cloned.1.call-done = f32[640,32]{0,1:T(8,128)} async-done(((f32[5120,32]{0,1:T(8,128)}), f32[640,32]{0,1:T(8,128)}) %reduce-scatter.29.cloned.1.call-update) | async-done | bytes 81936 | tf_op jit(solution)/shard_map/reduce_scatter | solution.py:90
  454.7 83.2 %reduce-scatter.33.cloned.1.call-done = f32[640,32]{0,1:T(8,128)} async-done(((f32[5120,32]{0,1:T(8,128)}), f32[640,32]{0,1:T(8,128)}) %reduce-scatter.33.cloned.1.call-update) | async-done | bytes 81936 | tf_op jit(solution)/shard_map/reduce_scatter | solution.py:90
  539.5 83.2 %reduce-scatter.35.cloned.1.call-done = f32[640,32]{0,1:T(8,128)} async-done(((f32[5120,32]{0,1:T(8,128)}), f32[640,32]{0,1:T(8,128)}) %reduce-scatter.35.cloned.1.call-update) | async-done | bytes 81936 | tf_op jit(solution)/shard_map/reduce_scatter | solution.py:90
  624.2 87.1 %reduce-scatter.23.cloned.1.call-done = f32[384,96]{0,1:T(8,128)} async-done(((f32[3072,96]{0,1:T(8,128)}), f32[384,96]{0,1:T(8,128)}) %reduce-scatter.23.cloned.1.call-update) | async-done | bytes 147472 | tf_op jit(solution)/shard_map/reduce_scatter | solution.py:84
  712.9 93.6 %reduce-scatter.31.cloned.1.call-done = f32[640,96]{0,1:T(8,128)} async-done(((f32[5120,96]{0,1:T(8,128)}), f32[640,96]{0,1:T(8,128)}) %reduce-scatter.31.cloned.1.call-update) | async-done | bytes 245776 | tf_op jit(solution)/shard_map/reduce_scatter | solution.py:90
  808.1 143.4 %reduce-scatter.13.cloned.1.call-done = f32[1024,32]{0,1:T(8,128)} async-done(((f32[1024,1024]{0,1:T(8,128)}), f32[1024,32]{0,1:T(8,128)}) %reduce-scatter.13.cloned.1.call-update) | async-done | bytes 131088 | tf_op jit(solution)/shard_map/reduce_scatter | solution.py:103
  953.1 148.2 %reduce-scatter.17.cloned.1.call-done = f32[1024,32]{0,1:T(8,128)} async-done(((f32[1024,1024]{0,1:T(8,128)}), f32[1024,32]{0,1:T(8,128)}) %reduce-scatter.17.cloned.1.call-update) | async-done | bytes 131088 | tf_op jit(solution)/shard_map/reduce_scatter | solution.py:105
  1102.8 148.3 %reduce-scatter.19.cloned.1.call-done = f32[1024,32]{0,1:T(8,128)} async-done(((f32[1024,1024]{0,1:T(8,128)}), f32[1024,32]{0,1:T(8,128)}) %reduce-scatter.19.cloned.1.call-update) | async-done | bytes 131088 | tf_op jit(solution)/shard_map/reduce_scatter | solution.py:106
  1252.7 162.0 %reduce-scatter.15.cloned.1.call-done = f32[1024,96]{0,1:T(8,128)} async-done(((f32[1024,3072]{0,1:T(8,128)}), f32[1024,96]{0,1:T(8,128)}) %reduce-scatter.15.cloned.1.call-update) | async-done | bytes 393232 | tf_op jit(solution)/shard_map/reduce_scatter | solution.py:104
  (107 shorter events, 62.6 us)
Async XLA Ops:
  7.2 83.8 %copy-start = (bf16[1024,1024]{1,0:T(8,128)(2,1)S(1)}, bf16[1024,1024]{1,0:T(8,128)(2,1)}, u32[]{:S(2)}) copy-start(bf16[1024,1024]{1,0:T(8,128)(2,1)} %param.13) | copy-start | bytes 6291460
  7.2 398.0 %reduce-scatter.21.cloned.1.call-start = ((), (), s32[]{:S(2)}) async-start(), calls=%async_computation.16 | async-start | bytes 147456 | tf_op jit(solution)/shard_map/reduce_scatter | solution.py:84
  91.8 166.9 %copy-start.3 = (f32[1024,32]{0,1:T(8,128)}, f32[1024,32]{0,1:T(8,128)S(1)}, u32[]{:S(2)}) copy-start(f32[1024,32]{0,1:T(8,128)S(1)} %fusion.37) | copy-start | bytes 393220
  92.9 45.7 %copy-start.19 = (bf16[128,32]{0,1:T(8,128)(2,1)S(1)}, bf16[128,32]{0,1:T(8,128)(2,1)}, u32[]{:S(2)}) copy-start(bf16[128,32]{0,1:T(8,128)(2,1)} %param.20) | copy-start | bytes 24580
  92.9 313.7 %reduce-scatter.25.cloned.1.call-start = ((), (), s32[]{:S(2)}) async-start(), calls=%async_computation.18 | async-start | bytes 147456 | tf_op jit(solution)/shard_map/reduce_scatter | solution.py:84
  93.0 80.7 %copy-start.1 = (bf16[1024,1024]{1,0:T(8,128)(2,1)S(1)}, bf16[1024,1024]{1,0:T(8,128)(2,1)}, u32[]{:S(2)}) copy-start(bf16[1024,1024]{1,0:T(8,128)(2,1)} %param.15) | copy-start | bytes 6291460
  173.6 47.7 %copy-start.12 = (bf16[1024,32]{0,1:T(8,128)(2,1)}, bf16[1024,32]{0,1:T(8,128)(2,1)S(1)}, u32[]{:S(2)}) copy-start(bf16[1024,32]{0,1:T(8,128)(2,1)S(1)} %all_gather.29) | copy-start | bytes 196612
  174.4 92.3 %copy-start.4 = (f32[1024,32]{0,1:T(8,128)}, f32[1024,32]{0,1:T(8,128)S(1)}, u32[]{:S(2)}) copy-start(f32[1024,32]{0,1:T(8,128)S(1)} %fusion.41) | copy-start | bytes 393220
  175.5 45.8 %copy-start.20 = (bf16[128,32]{0,1:T(8,128)(2,1)S(1)}, bf16[128,32]{0,1:T(8,128)(2,1)}, u32[]{:S(2)}) copy-start(bf16[128,32]{0,1:T(8,128)(2,1)} %param.21) | copy-start | bytes 24580
  175.5 232.5 %reduce-scatter.27.cloned.1.call-start = ((), (), s32[]{:S(2)}) async-start(), calls=%async_computation.19 | async-start | bytes 147456 | tf_op jit(solution)/shard_map/reduce_scatter | solution.py:84
  175.6 80.7 %copy-start.2 = (bf16[1024,1024]{1,0:T(8,128)(2,1)S(1)}, bf16[1024,1024]{1,0:T(8,128)(2,1)}, u32[]{:S(2)}) copy-start(bf16[1024,1024]{1,0:T(8,128)(2,1)} %param.16) | copy-start | bytes 6291460
  258.2 195.1 %reduce-scatter.29.cloned.1.call-start = ((), (), s32[]{:S(2)}) async-start(), calls=%async_computation.20 | async-start | bytes 737280 | tf_op jit(solution)/shard_map/reduce_scatter | solution.py:90
  265.4 272.5 %reduce-scatter.33.cloned.1.call-start = ((), (), s32[]{:S(2)}) async-start(), calls=%async_computation.22 | async-start | bytes 737280 | tf_op jit(solution)/shard_map/reduce_scatter | solution.py:90
  273.5 349.2 %reduce-scatter.35.cloned.1.call-start = ((), (), s32[]{:S(2)}) async-start(), calls=%async_computation.23 | async-start | bytes 737280 | tf_op jit(solution)/shard_map/reduce_scatter | solution.py:90
  281.6 429.7 %reduce-scatter.23.cloned.1.call-start = ((), (), s32[]{:S(2)}) async-start(), calls=%async_computation.17 | async-start | bytes 1327104 | tf_op jit(solution)/shard_map/reduce_scatter | solution.py:84
  324.9 49.0 %slice-start = ((s8[6291456]{0:T(1024)(128)(4,1)}), s8[4194304]{0:T(1024)(128)(4,1)S(1)}, s32[]{:S(2)}) async-start(s8[6291456]{0:T(1024)(128)(4,1)} %bitcast.44), calls=%async_computation.24 | async-start | bytes 8388608
  376.2 430.3 %reduce-scatter.31.cloned.1.call-start = ((), (), s32[]{:S(2)}) async-start(), calls=%async_computation.21 | async-start | bytes 2211840 | tf_op jit(solution)/shard_map/reduce_scatter | solution.py:90
  387.4 564.1 %reduce-scatter.13.cloned.1.call-start = ((), (), s32[]{:S(2)}) async-start(), calls=%async_computation.12 | async-start | bytes 4325376 | tf_op jit(solution)/shard_map/reduce_scatter | solution.py:103
  391.3 710.0 %reduce-scatter.17.cloned.1.call-start = ((), (), s32[]{:S(2)}) async-start(), calls=%async_computation.14 | async-start | bytes 4325376 | tf_op jit(solution)/shard_map/reduce_scatter | solution.py:105
  395.0 856.1 %reduce-scatter.19.cloned.1.call-start = ((), (), s32[]{:S(2)}) async-start(), calls=%async_computation.15 | async-start | bytes 4325376 | tf_op jit(solution)/shard_map/reduce_scatter | solution.py:106
  398.7 1015.9 %reduce-scatter.15.cloned.1.call-start = ((), (), s32[]{:S(2)}) async-start(), calls=%async_computation.13 | async-start | bytes 12976128 | tf_op jit(solution)/shard_map/reduce_scatter | solution.py:104
  405.2 546.4 %copy-start.7 = (f32[1024,32]{0,1:T(8,128)S(1)}, f32[1024,32]{0,1:T(8,128)}, u32[]{:S(2)}) copy-start(f32[1024,32]{0,1:T(8,128)} %copy-done.6) | copy-start | bytes 393220
  405.2 696.1 %copy-start.9 = (f32[1024,32]{0,1:T(8,128)S(1)}, f32[1024,32]{0,1:T(8,128)}, u32[]{:S(2)}) copy-start(f32[1024,32]{0,1:T(8,128)} %copy-done.8) | copy-start | bytes 393220
  405.2 846.0 %copy-start.11 = (f32[1024,32]{0,1:T(8,128)S(1)}, f32[1024,32]{0,1:T(8,128)}, u32[]{:S(2)}) copy-start(f32[1024,32]{0,1:T(8,128)} %copy-done.10) | copy-start | bytes 393220
  (11 other events, 207.0 us)
Sparse Core Ops, SparseCore 0:
  93.0 89.8 reduce-scatter.20
  186.7 88.4 reduce-scatter.24
  279.0 89.1 reduce-scatter.26
  372.0 81.1 reduce-scatter.28
  457.0 80.9 reduce-scatter.32
  541.7 80.9 reduce-scatter.34
  626.7 84.5 reduce-scatter.22
  716.0 90.4 reduce-scatter.30
  809.2 142.3 reduce-scatter.12
  954.1 147.1 reduce-scatter.16
  1104.0 147.1 reduce-scatter.18
  1253.7 160.9 reduce-scatter.14
where the time goes:
time: 1430 us; the launch traced here: 1420 us
  waiting for transfers between devices  993 us (69%)
  blocking collectives  303 us (21%)
  matrix products  86.7 us (6%)
  other arithmetic  18.3 us (1%)
  between operations  14.6 us (1%)
    reduce_scatter x4, waiting for transfers between devices, body(): lax.psum_scatter(proj_term(jnp.int32(0), lax.axis_size('seq') * (cotangen...  304 us
    reduce_scatter x1, waiting for transfers between devices, body(): lax.psum_scatter(partial_terms[1], 'enc', scatter_dimension=1, tiled=True)  162 us
    reduce_scatter x1, waiting for transfers between devices, body(): lax.psum_scatter(partial_terms[3], 'enc', scatter_dimension=1, tiled=True)  148 us
    reduce_scatter x1, waiting for transfers between devices, body(): lax.psum_scatter(partial_terms[2], 'enc', scatter_dimension=1, tiled=True)  148 us
    reduce_scatter x1, waiting for transfers between devices, body(): lax.psum_scatter(partial_terms[0], 'enc', scatter_dimension=1, tiled=True)  143 us
    reduce_scatter x4, waiting for transfers between devices, body(): lax.psum_scatter(weight_term(jnp.int32(0), lax.axis_size('seq') * (layer_...  87.1 us
    all_gather x1, blocking collectives, body(): lax.all_gather(proj_convnext, 'seq', axis=0, tiled=True)  41.4 us
    all_gather x1, blocking collectives, body(): lax.all_gather(proj_clip, 'seq', axis=0, tiled=True)  41.4 us
  transfers between devices with their start and end apart: 12, of which 9 were waited for; matrix products, arithmetic and copies ran while one was open for 7% of the time, Pallas kernels for 0%

commit v1 on v0

v1 whole, which is shorter than its diff:
```python
import jax
import jax.numpy as jnp
from jax import lax
from jax.sharding import Mesh, PartitionSpec as P

ROOT_HALF = 0.7071067811865476
INV_ROOT_TAU = 0.3989422804014327
LANES = 128
ENC = ("zl", "x", "core")
BF16 = jnp.bfloat16
F32 = jnp.float32


def normal_cdf(values):
    return 0.5 * (1.0 + lax.erf(values * ROOT_HALF))


def slope_of(values):
    return normal_cdf(values) + values * jnp.exp(-0.5 * values * values) * INV_ROOT_TAU


def dot(left, right, left_dim, right_dim):
    return lax.dot_general(
        left, right, (((left_dim,), (right_dim,)), ((), ())), preferred_element_type=F32
    )


def lane_chunks(block):
    cols, width = block.shape
    count = width // LANES
    return block.reshape(cols, count, LANES).transpose(1, 0, 2).reshape(count * cols, LANES)


def pack(blocks):
    return jnp.concatenate([lane_chunks(block.T) for block in blocks], axis=0)


def unpack(gathered, widths, counts):
    out = []
    start = 0
    for cols, count in zip(widths, counts):
        rows = cols * count
        piece = gathered[:, :, start : start + rows].reshape(4, 2, count, cols, LANES)
        out.append(piece.transpose(3, 1, 0, 2, 4).reshape(cols, 8 * count * LANES))
        start += rows
    return out


def spread(grads, counts):
    pieces = []
    for grad, count in zip(grads, counts):
        cols = grad.shape[0]
        piece = grad.reshape(cols, 2, 4, count, LANES).transpose(1, 2, 3, 0, 4)
        pieces.append(piece.reshape(2, 4, count * cols, LANES))
    return jnp.concatenate(pieces, axis=2)


def body(
    acts_clip,
    acts_convnext,
    acts_eva,
    acts_sam,
    cotangent,
    weight_clip,
    weight_convnext,
    weight_eva,
    weight_sam,
    proj_clip,
    proj_convnext,
    proj_eva,
    proj_sam,
):
    acts = (acts_clip, acts_convnext, acts_eva, acts_sam)
    zh = lax.axis_index("zh")
    enc = lax.axis_index(ENC)
    tokens = cotangent.shape[0]
    factor = float(8 * tokens) ** (-0.5)
    proj = jnp.concatenate([proj_clip, proj_convnext, proj_eva, proj_sam], axis=1)
    blocks = (weight_clip, weight_convnext, weight_eva, weight_sam, proj)
    widths = tuple(block.shape[1] for block in blocks)
    counts = tuple(block.shape[0] // LANES for block in blocks)
    swap = [(0, 1), (1, 0)]

    own = pack(blocks)
    other = lax.ppermute(own, "zh", swap)
    both = jnp.where(zh == 0, jnp.stack([own, other]), jnp.stack([other, own]))
    gathered = lax.all_gather(both, "y", axis=0)
    weight_t = unpack(gathered, widths, counts)
    proj_t = weight_t.pop()

    back_t = dot(proj_t, cotangent, 1, 1)
    pres = []
    owns = []
    for layer_input, weight in zip(acts, weight_t):
        cols = weight.shape[0]
        pres.append(dot(weight, layer_input, 1, 1))
        owns.append(lax.dynamic_slice_in_dim(layer_input, enc * cols, cols, 1).T)
    pre_t = jnp.concatenate(pres, axis=0)
    own_t = jnp.concatenate(owns, axis=0)
    feature_t = (own_t.astype(F32) + pre_t * normal_cdf(pre_t)).astype(BF16)
    hidden_t = (back_t * slope_of(pre_t)).astype(BF16)

    hidden_all = lax.all_gather(hidden_t, ENC, axis=0, tiled=True)

    narrow = jnp.concatenate([weight_t[0], weight_t[2], weight_t[3]], axis=0)
    small = widths[0]
    wide = widths[1]
    send = jnp.concatenate(
        [
            weight_t[1].reshape(wide, 32, wide).transpose(1, 0, 2),
            narrow.reshape(3 * small, 32, small).transpose(1, 0, 2),
        ],
        axis=2,
    )
    rows = lax.all_to_all(send, ENC, split_axis=0, concat_axis=0, tiled=True)

    def placed(block, left):
        return jnp.pad(block, ((0, 0), (0, 0), (left, sum(widths[:4]) - left - block.shape[2])))

    rows_t = jnp.concatenate(
        [
            placed(rows[:, :small, wide:], 0),
            placed(rows[:, :, :wide], small),
            placed(rows[:, small : 2 * small, wide:], small + wide),
            placed(rows[:, 2 * small :, wide:], 2 * small + wide),
        ],
        axis=1,
    ).reshape(hidden_all.shape[0], -1)

    grads = []
    start = 0
    for layer_input, cols in zip(acts, widths):
        grads.append(dot(hidden_t[start : start + cols], layer_input, 1, 0).astype(BF16))
        start += cols
    grads.append(dot(feature_t, cotangent, 1, 0).astype(BF16))
    parts = spread(grads, counts)
    parts = lax.all_to_all(parts, "y", split_axis=1, concat_axis=1, tiled=True)
    sums = jnp.sum(parts.astype(F32), axis=1)
    mine = lax.dynamic_index_in_dim(sums, zh, 0, keepdims=False)
    away = lax.dynamic_index_in_dim(sums, 1 - zh, 0, keepdims=False).astype(BF16)
    total = (mine + lax.ppermute(away, "zh", swap).astype(F32)) * factor
    finals = []
    start = 0
    for cols, count in zip(widths, counts):
        piece = total[start : start + cols * count].reshape(count, cols, LANES)
        finals.append(piece.transpose(0, 2, 1).reshape(count * LANES, cols))
        start += cols * count
    proj_grad = finals.pop()

    input_t = (back_t + dot(rows_t, hidden_all, 0, 0)).astype(BF16)
    bounds = []
    start = 0
    for cols in widths[:4]:
        bounds.append((start, start + cols))
        start += cols
    return (
        *[input_t[low:high].T for low, high in bounds],
        *finals,
        *[proj_grad[:, low:high] for low, high in bounds],
    )


def solution(mesh):
    split = Mesh(mesh.devices.reshape(4, 4, 2, 2, 4), ("zl", "x", "core", "zh", "y"))
    seq = ("zh", "y")
    whole = P(seq, None)
    tiled = P(seq, ENC)
    return jax.shard_map(
        body,
        mesh=split,
        in_specs=(whole,) * 5 + (tiled,) * 8,
        out_specs=(tiled,) * 12,
        check_vma=False,
    )
```

time: 1430 us -> 253 us (0.18)
  waiting for transfers between devices: 993 us -> 119 us
  blocking collectives: 303 us -> 0 us
  matrix products: 86.7 us -> 41.8 us
  local copies, waits for them, and re-layouts: 6.5 us -> 47.1 us
  starting transfers between devices: 0.9 us -> 21.2 us
    reduce_scatter x12 -> x0, waiting for transfers between devices: 993 us -> none  [the longest x4 304 us: body(): lax.psum_scatter(proj_term(jnp.int32(0), lax.axis_size('seq') * (cotangen...]
    all_gather x8 -> x0, blocking collectives: 303 us -> none  [the longest x1 41.4 us: body(): lax.all_gather(proj_convnext, 'seq', axis=0, tiled=True)]
    all_gather x0 -> x2, waiting for transfers between devices: none -> 47.4 us  [the longest x1 47.4 us: body(): gathered = lax.all_gather(both, 'y', axis=0)]
    all_to_all x0 -> x2, waiting for transfers between devices: none -> 47 us  [the longest x1 33.1 us: body(): parts = lax.all_to_all(parts, 'y', split_axis=1, concat_axis=1, tiled=True)]
    dot_general x20 -> x11, matrix products: 86.7 us -> 41.8 us  [dot(): lax.dot_general(left, right, (((left_dim,), (right_dim,)), ((), ())), pre...]
    ppermute x0 -> x2, waiting for transfers between devices: none -> 25 us  [the longest x1 16.8 us: body(): total = (mine + lax.ppermute(away, 'zh', swap).astype(F32)) * factor]
  transfers between devices with their start and end apart: 12 -> 6, of which waited for: 9 -> 5; matrix products, arithmetic and copies ran while one was open for 7% -> 20% of each run, Pallas kernels for 0% -> 0%
where the time goes in v1:
time: 253 us; the launch traced here: 252 us
  waiting for transfers between devices  119 us (47%)
  local copies, waits for them, and re-layouts  47.1 us (19%)
  matrix products  41.8 us (17%)
  starting transfers between devices  21.2 us (8%)
  between operations  14.6 us (6%)
  other arithmetic  8.08 us (3%)
    all_gather x1, waiting for transfers between devices, body(): gathered = lax.all_gather(both, 'y', axis=0)  47.4 us
    dot_general x11, matrix products, dot(): lax.dot_general(left, right, (((left_dim,), (right_dim,)), ((), ())), pre...  41.8 us
    all_to_all x1, waiting for transfers between devices, body(): parts = lax.all_to_all(parts, 'y', split_axis=1, concat_axis=1, tiled=True)  33.1 us
    ppermute x1, waiting for transfers between devices, body(): total = (mine + lax.ppermute(away, 'zh', swap).astype(F32)) * factor  16.8 us
    all_to_all x1, waiting for transfers between devices, body(): rows = lax.all_to_all(send, ENC, split_axis=0, concat_axis=0, tiled=True)  13.9 us
    unnamed x63, local copies, waits for them, and re-layouts  9.47 us
    ppermute x1, waiting for transfers between devices, body(): other = lax.ppermute(own, 'zh', swap)  8.23 us
    all_to_all x1, starting transfers between devices, body(): rows = lax.all_to_all(send, ENC, split_axis=0, concat_axis=0, tiled=True)  8.09 us
  transfers between devices with their start and end apart: 6, of which 5 were waited for; matrix products, arithmetic and copies ran while one was open for 20% of the time, Pallas kernels for 0%

profile of v1, /device:TPU:1, one launch (start us, length us, event | category | flops | bytes accessed | tf_op | source)
XLA Modules:
  0.0 252.2 jit_solution(3494805495836968173)
XLA Ops:
  11.9 7.8 %collective-permute-start = (bf16[1344,128]{1,0:T(8,128)(2,1)S(1)}, bf16[1344,128]{1,0:T(8,128)(2,1)S(1)}, u32[]{:S(2)}, u32[]{:S(2)}) collective-permute-start(bf16[1344,128]{1,0:T(8,128)(2,1)S(1)} %constant_dynamic-update-slice_fusion), channel_id=1, source_target_pairs={{0,4},{4,0},{1,5},{5,1},{2,6},{6,2},{3,7},{7,3},{8,12},{12,8},{9,1... | collective-permute-start | bytes 1032200 | tf_op jit(solution)/shard_map/ppermute | solution.py:85
  19.7 8.2 %collective-permute-done = bf16[1344,128]{1,0:T(8,128)(2,1)S(1)} collective-permute-done((bf16[1344,128]{1,0:T(8,128)(2,1)S(1)}, bf16[1344,128]{1,0:T(8,128)(2,1)S(1)}, u32[]{:S(2)}, u32[]{:S(2)}) %collective-permute-start) | collective-permute-done | bytes 344096 | tf_op jit(solution)/shard_map/ppermute | solution.py:85
  28.9 47.4 %all-gather.3.cloned.1.call-done = bf16[4,2,1344,128]{3,2,1,0:T(8,128)(2,1)} async-done(((bf16[1,2,1344,128]{3,2,1,0:T(8,128)(2,1)}), bf16[4,2,1344,128]{3,2,1,0:T(8,128)(2,1)}) %all-gather.3.cloned.1.call-update) | async-done | bytes 2752528 | tf_op jit(solution)/shard_map/all_gather | solution.py:87
  82.3 3.0 %slice.104 = bf16[4,2,960,128]{3,2,1,0:T(8,128)(2,1)} slice(bf16[4,2,1344,128]{3,2,1,0:T(8,128)(2,1)} %all-gather.3.cloned.1.call-done), slice={[0:4], [0:2], [384:1344], [0:128]} | slice | bytes 3932160 | tf_op jit(solution)/shard_map/slice | solution.py:43
  85.3 4.3 %copy.102 = bf16[4,2,5,192,128]{3,4,2,0,1:T(8,128)(2,1)} copy(bf16[4,2,5,192,128]{4,3,2,1,0:T(8,128)(2,1)} %bitcast.138) | data formatting | bytes 3932160 | tf_op jit(solution)/shard_map/reshape | solution.py:43
  90.4 2.4 fusion.35
  93.5 5.0 %fusion.34 = f32[96,1024]{1,0:T(8,128)S(1)} fusion(bf16[96,3072]{1,0:T(8,128)(2,1)S(1)} %copy-done.5, bf16[1024,3072]{1,0:T(8,128)(2,1)} %param.14), kind=kOutput, calls=%fused_computation.82 | convolution fusion | flops 603979776 | bytes 7274496 | tf_op jit(solution)/shard_map/dot_general | solution.py:23
  98.6 8.9 %fusion.15 = (bf16[192,1024]{1,0:T(8,128)(2,1)}, f32[192,1024]{1,0:T(8,128)}) fusion(f32[32,1024]{1,0:T(8,128)S(1)} %fusion.36, f32[32,1024]{1,0:T(8,128)S(1)} %fusion.35, f32[96,1024]{1,0:T(8,128)S(1)} %fusion.34, f32[32,1024]{1,0:T(8,128)S(1)} %fusion.33, bf16[192,5120]{0,1:T(8,128)(2,1)S(1)} %bitcast.146, bf16[1024,5120]{1,0:T(8,128)(2,1)} %param.17), kind=kOutput, calls=%fused_computation.30 | convolution fusion | flops 2015821824 | bytes 14417920 | tf_op jit(solution)/shard_map/dot_general | solution.py:23
  117.5 4.3 %convolution_convert_fusion.1 = bf16[96,3072]{1,0:T(8,128)(2,1)S(1)} fusion(bf16[1024,3072]{1,0:T(8,128)(2,1)} %param.14, bf16[192,1024]{1,0:T(8,128)(2,1)} %get-tuple-element.63), kind=kOutput, calls=%fused_computation.14 | convolution fusion | flops 604274688 | bytes 7077888 | tf_op jit(solution)/shard_map/dot_general | solution.py:23
  121.8 1.6 reshape.213
  123.5 2.3 copy.117
  127.1 2.1 convolution_convert_fusion.2
  132.1 8.1 %all-to-all-start = ((bf16[32,96,128]{2,1,0:T(8,128)(2,1)}), bf16[32,96,128]{2,1,0:T(8,128)(2,1)S(1)}, u32[]{:S(2)}, u32[]{:S(2)}) async-start(bf16[32,96,128]{2,1,0:T(8,128)(2,1)} %copy.110), calls=%async_computation | async-start | bytes 1572864 | tf_op jit(solution)/shard_map/all_to_all | solution.py:115
  140.2 6.8 %convolution_convert_fusion = bf16[192,5120]{1,0:T(8,128)(2,1)S(1)} fusion(bf16[1024,5120]{1,0:T(8,128)(2,1)} %param.17, bf16[32,1024]{1,0:T(8,128)(2,1)} %bitcast.164, bf16[32,1024]{1,0:T(8,128)(2,1)} %bitcast.163, bf16[96,1024]{1,0:T(8,128)(2,1)S(1)} %bitcast.160, bf16[32,1024]{1,0:T(8,128)(2,1)} %bitcast.165, f32[32,1024]{1,0:T(8,128)} %copy-done.22, ...), kind=kOutput, calls=%fused_computation.12 | convolution fusion | flops 2017591296 | bytes 13631488 | tf_op jit(solution)/shard_map/dot_general | solution.py:23
  147.0 2.6 %copy.124 = bf16[192,5120]{0,1:T(8,128)(2,1)} copy(bf16[192,5120]{1,0:T(8,128)(2,1)S(1)} %convolution_convert_fusion) | data formatting | bytes 3932160 | tf_op jit(solution)/shard_map/convert_element_type | solution.py:135
  149.6 3.2 %copy.125 = bf16[2,4,5,192,128]{4,3,2,1,0:T(8,128)(2,1)S(1)} copy(bf16[2,4,5,192,128]{3,4,2,1,0:T(8,128)(2,1)} %bitcast.136) | data formatting | bytes 3932160 | tf_op jit(solution)/shard_map/transpose | solution.py:53
  153.3 1.7 copy.126
  154.9 13.9 %all-to-all-done = bf16[32,96,128]{2,1,0:T(8,128)(2,1)S(1)} async-done(((bf16[32,96,128]{2,1,0:T(8,128)(2,1)}), bf16[32,96,128]{2,1,0:T(8,128)(2,1)S(1)}, u32[]{:S(2)}, u32[]{:S(2)}) %all-to-all-start) | async-done | bytes 786464 | tf_op jit(solution)/shard_map/all_to_all | solution.py:115
  168.9 4.6 %all-to-all-start.1 = ((bf16[2,4,1344,128]{3,2,0,1:T(8,128)(2,1)}), bf16[2,4,1344,128]{3,2,0,1:T(8,128)(2,1)}, u32[]{:S(2)}, u32[]{:S(2)}) async-start(bf16[2,4,1344,128]{3,2,0,1:T(8,128)(2,1)} %copy.126), calls=%async_computation.1 | async-start | bytes 5505024 | tf_op jit(solution)/shard_map/all_to_all | solution.py:137
  173.8 33.1 %all-to-all-done.1 = bf16[2,4,1344,128]{3,2,0,1:T(8,128)(2,1)} async-done(((bf16[2,4,1344,128]{3,2,0,1:T(8,128)(2,1)}), bf16[2,4,1344,128]{3,2,0,1:T(8,128)(2,1)}, u32[]{:S(2)}, u32[]{:S(2)}) %all-to-all-start.1) | async-done | bytes 2752544 | tf_op jit(solution)/shard_map/all_to_all | solution.py:137
  206.9 2.3 convert_reduce_fusion
  209.8 2.2 fusion.7
  212.1 16.8 %collective-permute-done.1 = bf16[1344,128]{1,0:T(8,128)(2,1)S(1)} collective-permute-done((bf16[1344,128]{1,0:T(8,128)(2,1)S(1)}, bf16[1344,128]{1,0:T(8,128)(2,1)S(1)}, u32[]{:S(2)}, u32[]{:S(2)}) %collective-permute-start.1) | collective-permute-done | bytes 344096 | tf_op jit(solution)/shard_map/ppermute | solution.py:141
  235.7 8.3 %fusion.9 = bf16[192,1024]{1,0:T(8,128)(2,1)S(1)} fusion(f32[192,1024]{1,0:T(8,128)S(1)} %copy-done.9, bf16[6144,192]{1,0:T(8,128)(2,1)} %bitcast.135, bf16[6144,1024]{1,0:T(8,128)(2,1)} %all-gather.5.cloned.1.call-done), kind=kOutput, calls=%fused_computation.19 | convolution fusion | flops 2416312320 | bytes 16121856 | tf_op jit(solution)/shard_map/dot_general | solution.py:23
  (116 shorter events, 36.6 us)
Async XLA Ops:
  7.2 82.4 %copy-start = (bf16[1024,1024]{1,0:T(8,128)(2,1)S(1)}, bf16[1024,1024]{1,0:T(8,128)(2,1)}, u32[]{:S(2)}) copy-start(bf16[1024,1024]{1,0:T(8,128)(2,1)} %param.13) | copy-start | bytes 6291460
  7.2 69.2 %all-gather.3.cloned.1.call-start = ((), (), s32[]{:S(2)}) async-start(), calls=%async_computation.2 | async-start | bytes 3440640 | tf_op jit(solution)/shard_map/all_gather | solution.py:87
  11.9 16.1 %collective-permute-start = (bf16[1344,128]{1,0:T(8,128)(2,1)S(1)}, bf16[1344,128]{1,0:T(8,128)(2,1)S(1)}, u32[]{:S(2)}, u32[]{:S(2)}) collective-permute-start(bf16[1344,128]{1,0:T(8,128)(2,1)S(1)} %constant_dynamic-update-slice_fusion), channel_id=1, source_target_pairs={{0,4},{4,0},{1,5},{5,1},{2,6},{6,2},{3,7},{7,3},{8,12},{12,8},{9,1... | collective-permute-start | bytes 1032200 | tf_op jit(solution)/shard_map/ppermute | solution.py:85
  28.9 206.8 %all-gather.5.cloned.1.call-start = ((), (), s32[]{:S(2)}) async-start(), calls=%async_computation.3 | async-start | bytes 12976128 | tf_op jit(solution)/shard_map/all_gather | solution.py:103
  85.3 4.3 %copy-start.16 = (bf16[32,1024]{1,0:T(8,128)(2,1)S(1)}, bf16[32,1024]{1,0:T(8,128)(2,1)}, u32[]{:S(2)}) copy-start(bf16[32,1024]{1,0:T(8,128)(2,1)} %reshape.207) | copy-start | bytes 196612
  85.3 5.1 %copy-start.17 = (bf16[32,1024]{1,0:T(8,128)(2,1)S(1)}, bf16[32,1024]{1,0:T(8,128)(2,1)}, u32[]{:S(2)}) copy-start(bf16[32,1024]{1,0:T(8,128)(2,1)} %reshape.209) | copy-start | bytes 196612
  90.4 8.2 %copy-start.20 = (f32[32,1024]{1,0:T(8,128)}, f32[32,1024]{1,0:T(8,128)S(1)}, u32[]{:S(2)}) copy-start(f32[32,1024]{1,0:T(8,128)S(1)} %fusion.33) | copy-start | bytes 393220
  92.8 5.8 %copy-start.21 = (f32[32,1024]{1,0:T(8,128)}, f32[32,1024]{1,0:T(8,128)S(1)}, u32[]{:S(2)}) copy-start(f32[32,1024]{1,0:T(8,128)S(1)} %fusion.35) | copy-start | bytes 393220
  93.5 5.1 %copy-start.22 = (f32[32,1024]{1,0:T(8,128)}, f32[32,1024]{1,0:T(8,128)S(1)}, u32[]{:S(2)}) copy-start(f32[32,1024]{1,0:T(8,128)S(1)} %fusion.36) | copy-start | bytes 393220
  93.5 5.0 %copy-start.4 = (bf16[4,2,5,192,128]{3,4,2,0,1:T(8,128)(2,1)S(1)}, bf16[4,2,5,192,128]{3,4,2,0,1:T(8,128)(2,1)}, u32[]{:S(2)}) copy-start(bf16[4,2,5,192,128]{3,4,2,0,1:T(8,128)(2,1)} %copy.102) | copy-start | bytes 5898244
  98.5 9.0 %copy-start.14 = (f32[96,1024]{1,0:T(8,128)}, f32[96,1024]{1,0:T(8,128)S(1)}, u32[]{:S(2)}) copy-start(f32[96,1024]{1,0:T(8,128)S(1)} %fusion.34) | copy-start | bytes 1179652
  107.5 5.7 %copy-start.13 = (bf16[32,2,4,1,128]{4,0,1,2,3:T(8,128)(2,1)S(1)}, bf16[32,2,4,1,128]{4,0,1,2,3:T(8,128)(2,1)}, u32[]{:S(2)}) copy-start(bf16[32,2,4,1,128]{4,0,1,2,3:T(8,128)(2,1)} %copy-done.12) | copy-start | bytes 196612
  107.5 6.6 %copy-start.11 = (bf16[32,2,4,1,128]{4,0,1,2,3:T(8,128)(2,1)S(1)}, bf16[32,2,4,1,128]{4,0,1,2,3:T(8,128)(2,1)}, u32[]{:S(2)}) copy-start(bf16[32,2,4,1,128]{4,0,1,2,3:T(8,128)(2,1)} %copy-done.10) | copy-start | bytes 196612
  121.8 3.9 %copy-start.2 = (bf16[1024,1024]{1,0:T(8,128)(2,1)S(1)}, bf16[1024,1024]{1,0:T(8,128)(2,1)}, u32[]{:S(2)}) copy-start(bf16[1024,1024]{1,0:T(8,128)(2,1)} %param.15) | copy-start | bytes 6291460
  123.5 5.8 %copy-start.7 = (bf16[32,2,4,1,128]{0,4,2,1,3:T(8,128)(2,1)S(1)}, bf16[32,2,4,1,128]{0,4,2,1,3:T(8,128)(2,1)}, u32[]{:S(2)}) copy-start(bf16[32,2,4,1,128]{0,4,2,1,3:T(8,128)(2,1)} %copy.133) | copy-start | bytes 196612
  123.5 5.8 %copy-start.8 = (bf16[32,2,4,1,128]{0,4,2,1,3:T(8,128)(2,1)S(1)}, bf16[32,2,4,1,128]{0,4,2,1,3:T(8,128)(2,1)}, u32[]{:S(2)}) copy-start(bf16[32,2,4,1,128]{0,4,2,1,3:T(8,128)(2,1)} %copy.134) | copy-start | bytes 196612
  130.8 9.4 %copy-start.15 = (f32[96,1024]{1,0:T(8,128)S(1)}, f32[96,1024]{1,0:T(8,128)}, u32[]{:S(2)}) copy-start(f32[96,1024]{1,0:T(8,128)} %copy-done.14) | copy-start | bytes 1179652
  130.8 9.4 %copy-start.19 = (bf16[1024,96]{0,1:T(8,128)(2,1)S(1)}, bf16[1024,96]{0,1:T(8,128)(2,1)}, u32[]{:S(2)}) copy-start(bf16[1024,96]{0,1:T(8,128)(2,1)} %copy.141) | copy-start | bytes 589828
  132.1 36.8 %all-to-all-start = ((bf16[32,96,128]{2,1,0:T(8,128)(2,1)}), bf16[32,96,128]{2,1,0:T(8,128)(2,1)S(1)}, u32[]{:S(2)}, u32[]{:S(2)}) async-start(bf16[32,96,128]{2,1,0:T(8,128)(2,1)} %copy.110), calls=%async_computation | async-start | bytes 1572864 | tf_op jit(solution)/shard_map/all_to_all | solution.py:115
  149.6 3.3 %copy-start.6 = (bf16[2,4,3,96,128]{4,3,2,1,0:T(8,128)(2,1)S(1)}, bf16[2,4,3,96,128]{4,3,2,1,0:T(8,128)(2,1)}, u32[]{:S(2)}) copy-start(bf16[2,4,3,96,128]{4,3,2,1,0:T(8,128)(2,1)} %copy.117) | copy-start | bytes 1769476
  168.9 38.0 %all-to-all-start.1 = ((bf16[2,4,1344,128]{3,2,0,1:T(8,128)(2,1)}), bf16[2,4,1344,128]{3,2,0,1:T(8,128)(2,1)}, u32[]{:S(2)}, u32[]{:S(2)}) async-start(bf16[2,4,1344,128]{3,2,0,1:T(8,128)(2,1)} %copy.126), calls=%async_computation.1 | async-start | bytes 5505024 | tf_op jit(solution)/shard_map/all_to_all | solution.py:137
  209.2 19.6 %collective-permute-start.1 = (bf16[1344,128]{1,0:T(8,128)(2,1)S(1)}, bf16[1344,128]{1,0:T(8,128)(2,1)S(1)}, u32[]{:S(2)}, u32[]{:S(2)}) collective-permute-start(bf16[1344,128]{1,0:T(8,128)(2,1)S(1)} %fusion.24), channel_id=1, source_target_pairs={{0,4},{4,0},{1,5},{5,1},{2,6},{6,2},{3,7},{7,3},{8,12},{12,8},{9,1... | collective-permute-start | bytes 1032200 | tf_op jit(solution)/shard_map/ppermute | solution.py:141
  229.9 5.8 %copy-start.9 = (f32[192,1024]{1,0:T(8,128)S(1)}, f32[192,1024]{1,0:T(8,128)}, u32[]{:S(2)}) copy-start(f32[192,1024]{1,0:T(8,128)} %get-tuple-element.64) | copy-start | bytes 2359300
  235.7 9.7 %copy-start.1 = (bf16[1024,1024]{1,0:T(8,128)(2,1)S(1)}, bf16[1024,1024]{1,0:T(8,128)(2,1)}, u32[]{:S(2)}) copy-start(bf16[1024,1024]{1,0:T(8,128)(2,1)} %param.13) | copy-start | bytes 6291460
  (5 other events, 12.5 us)
Sparse Core Ops, SparseCore 0:
  29.0 47.3 all-gather.2
  107.7 96.8 all-gather.4

commit v2 on v1

v2 whole, which is shorter than its diff:
```python
import jax
import jax.numpy as jnp
from jax import lax
from jax.experimental import pallas as pl
from jax.experimental.pallas import tpu as pltpu
from jax.sharding import Mesh, PartitionSpec as P

ROOT_HALF = 0.7071067811865476
INV_ROOT_TAU = 0.3989422804014327
LANES = 128
ENC = ("zl", "x", "core")
BF16 = jnp.bfloat16
F32 = jnp.float32
SWAP = [(0, 1), (1, 0)]
SHIFTS = (1, 3, 2)
WIDE = 96
SMALL = 32
COLS = WIDE + 3 * SMALL
SPANS = ((0, 96), (96, 128), (128, 160), (160, 192))
W_ROWS = 3 * WIDE + 3 * SMALL
ROWS = W_ROWS + 5 * COLS
TILE = 256


def normal_cdf(values):
    return 0.5 * (1.0 + lax.erf(values * ROOT_HALF))


def slope_of(values):
    return normal_cdf(values) + values * jnp.exp(-0.5 * values * values) * INV_ROOT_TAU


def dot(left, right, left_dim, right_dim):
    return lax.dot_general(
        left, right, (((left_dim,), (right_dim,)), ((), ())), preferred_element_type=F32
    )


def lanes_of(start, width=LANES):
    return pl.ds(pl.multiple_of(start, LANES), width)


def pack_kernel(wv, wc, we, ws, pv, pc, pe, ps, out):
    for j in range(3):
        out[j * WIDE : (j + 1) * WIDE, :] = wv[:, j * LANES : (j + 1) * LANES]
    row = 3 * WIDE
    for ref in (wc, we, ws):
        out[row : row + SMALL, :] = ref[...]
        row += SMALL
    for ref, (low, high) in zip((pv, pc, pe, ps), SPANS):
        for j in range(5):
            at = W_ROWS + j * COLS
            out[at + low : at + high, :] = ref[:, j * LANES : (j + 1) * LANES]


def pack(*shards):
    return pl.pallas_call(
        pack_kernel,
        out_shape=jax.ShapeDtypeStruct((ROWS, LANES), BF16),
        name="pack",
    )(*shards)


def forward_kernel(place, *refs):
    gathered = refs[:8]
    acts = refs[8:12]
    cotangent, hidden, feature, back = refs[12:16]
    weights = refs[16:20]
    proj = refs[20]
    enc = place[8]

    @pl.when(pl.program_id(0) == 0)
    def _():
        for source, ref in enumerate(gathered):
            seq = place[source]
            for j in range(3):
                weights[0][:WIDE, lanes_of(seq * (3 * LANES) + j * LANES)] = ref[
                    j * WIDE : (j + 1) * WIDE, :
                ]
            row = 3 * WIDE
            for k in range(1, 4):
                weights[k][:SMALL, lanes_of(seq * LANES)] = ref[row : row + SMALL, :]
                row += SMALL
            for j in range(5):
                at = W_ROWS + j * COLS
                proj[:, lanes_of(seq * (5 * LANES) + j * LANES)] = ref[at : at + COLS, :]
        for k in range(4):
            cols = SPANS[k][1] - SPANS[k][0]
            shape = (cols, weights[k].shape[1])
            row = lax.broadcasted_iota(jnp.int32, shape, 0) + enc * cols
            lane = lax.broadcasted_iota(jnp.int32, shape, 1)
            weights[k][cols:, :] = jnp.where(row == lane, 1.0, 0.0).astype(BF16)

    back_t = dot(proj[...], cotangent[...], 1, 1)
    back[...] = back_t
    for k in range(4):
        low, high = SPANS[k]
        both = dot(weights[k][...], acts[k][...], 1, 1)
        pre = both[: high - low]
        cdf = normal_cdf(pre)
        slope = cdf + pre * jnp.exp(-0.5 * pre * pre) * INV_ROOT_TAU
        feature[low:high, :] = (both[high - low :] + pre * cdf).astype(BF16)
        hidden[low:high, :] = (back_t[low:high] * slope).astype(BF16)


def forward(place, gathered, acts, cotangent):
    tokens = cotangent.shape[0]
    whole = pl.BlockSpec((ROWS, LANES), lambda i, p: (0, 0))
    tall = lambda a: pl.BlockSpec((TILE, a.shape[1]), lambda i, p: (i, 0))
    flat = pl.BlockSpec((COLS, TILE), lambda i, p: (0, i))
    return pl.pallas_call(
        forward_kernel,
        grid_spec=pltpu.PrefetchScalarGridSpec(
            num_scalar_prefetch=1,
            grid=(tokens // TILE,),
            in_specs=[whole] * 8 + [tall(a) for a in acts] + [tall(cotangent)],
            out_specs=[flat] * 3,
            scratch_shapes=[
                pltpu.VMEM((2 * (high - low), a.shape[1]), BF16)
                for (low, high), a in zip(SPANS, acts)
            ]
            + [pltpu.VMEM((COLS, cotangent.shape[1]), BF16)],
        ),
        out_shape=[
            jax.ShapeDtypeStruct((COLS, tokens), BF16),
            jax.ShapeDtypeStruct((COLS, tokens), BF16),
            jax.ShapeDtypeStruct((COLS, tokens), F32),
        ],
        compiler_params=pltpu.CompilerParams(vmem_limit_bytes=50 * 2**20),
        name="forward",
    )(place, *gathered, *acts, cotangent)


def send_kernel(place, *refs):
    out = refs[8]
    for source, ref in enumerate(refs[:8]):
        seq = place[source]
        line = seq // 2
        first = (seq % 2) * 4
        wide = jnp.concatenate([ref[j * WIDE : (j + 1) * WIDE, :] for j in range(3)], axis=1)
        narrow = ref[3 * WIDE : W_ROWS, :]
        for j in range(4):
            out[first + j, line] = jnp.concatenate(
                [wide[:, j * WIDE : (j + 1) * WIDE], narrow[:, j * SMALL : (j + 1) * SMALL]],
                axis=1,
            )


def send_rows(place, gathered):
    return pl.pallas_call(
        send_kernel,
        grid_spec=pltpu.PrefetchScalarGridSpec(
            num_scalar_prefetch=1,
            grid=(1,),
            in_specs=[pl.BlockSpec((W_ROWS, LANES), lambda i, p: (0, 0))] * 8,
            out_specs=pl.BlockSpec((8, 4, WIDE, LANES), lambda i, p: (0, 0, 0, 0)),
        ),
        out_shape=jax.ShapeDtypeStruct((8, 4, WIDE, LANES), BF16),
        compiler_params=pltpu.CompilerParams(vmem_limit_bytes=32 * 2**20),
        name="send_rows",
    )(place, *gathered)


def expand_kernel(rows, out):
    lane = lax.broadcasted_iota(jnp.int32, (WIDE, LANES), 1)
    zero = jnp.zeros((WIDE, LANES), BF16)
    for group in range(4):
        pieces = []
        for j in range(2):
            block = rows[group * 2 + j, 0]
            conv = jnp.where(lane < WIDE, block, zero)
            rest = jnp.where(lane < WIDE, zero, block)
            clip = jnp.concatenate([rest[:SMALL], zero[:SMALL]], axis=1)
            turned = pltpu.roll(rest[SMALL:].astype(F32), SMALL, 1).astype(BF16)
            eva = jnp.concatenate([zero[:SMALL], turned[:SMALL]], axis=1)
            later = pltpu.roll(turned[SMALL:].astype(F32), SMALL, 1).astype(BF16)
            sam = jnp.concatenate([zero[:SMALL], later], axis=1)
            conv = jnp.concatenate([conv, zero], axis=1)
            pieces += [conv, clip, eva, sam]
        both = jnp.concatenate(pieces, axis=0)
        turned = both.astype(F32).T.astype(BF16)
        out[0, :, group * 2 * COLS : (group + 1) * 2 * COLS] = turned[:COLS]


def expand(rows):
    return pl.pallas_call(
        expand_kernel,
        grid=(4,),
        in_specs=[pl.BlockSpec((8, 1, WIDE, LANES), lambda i: (0, i, 0, 0))],
        out_specs=pl.BlockSpec((1, COLS, 8 * COLS), lambda i: (i, 0, 0)),
        out_shape=jax.ShapeDtypeStruct((4, COLS, 8 * COLS), BF16),
        name="expand_rows",
    )(rows)


def grads_kernel(hidden, feature, acts_v, acts_c, acts_e, acts_s, cotangent, out):
    wide = dot(hidden[:WIDE, :], acts_v[...], 1, 0).astype(BF16)
    for j in range(3):
        out[0, j * WIDE : (j + 1) * WIDE, :] = wide[:, j * LANES : (j + 1) * LANES]
    row = 3 * WIDE
    for (low, high), ref in zip(SPANS[1:], (acts_c, acts_e, acts_s)):
        out[0, row : row + SMALL, :] = dot(hidden[low:high, :], ref[...], 1, 0).astype(BF16)
        row += SMALL
    proj = dot(feature[...], cotangent[...], 1, 0).astype(BF16)
    for j in range(5):
        at = W_ROWS + j * COLS
        out[0, at : at + COLS, :] = proj[:, j * LANES : (j + 1) * LANES]


def grads(hidden, feature, acts, cotangent):
    tokens = cotangent.shape[0]
    whole = pl.BlockSpec((COLS, tokens), lambda i: (0, 0))
    part = lambda a: pl.BlockSpec((tokens, a.shape[1] // 8), lambda i: (0, i))
    return pl.pallas_call(
        grads_kernel,
        grid=(8,),
        in_specs=[whole] * 2 + [part(a) for a in acts] + [part(cotangent)],
        out_specs=pl.BlockSpec((1, ROWS, LANES), lambda i: ((i % 4) * 2 + i // 4, 0, 0)),
        out_shape=jax.ShapeDtypeStruct((8, ROWS, LANES), BF16),
        compiler_params=pltpu.CompilerParams(vmem_limit_bytes=50 * 2**20),
        name="grads",
    )(hidden, feature, *acts, cotangent)


def away_kernel(place, parts, out):
    total = parts[0, 0].astype(F32)
    for j in range(1, 4):
        total += parts[j, 0].astype(F32)
    out[...] = total.astype(BF16)


def away_sum(place, parts):
    return pl.pallas_call(
        away_kernel,
        grid_spec=pltpu.PrefetchScalarGridSpec(
            num_scalar_prefetch=1,
            grid=(1,),
            in_specs=[pl.BlockSpec((4, 1, ROWS, LANES), lambda i, p: (0, 1 - p[9], 0, 0))],
            out_specs=pl.BlockSpec((ROWS, LANES), lambda i, p: (0, 0)),
        ),
        out_shape=jax.ShapeDtypeStruct((ROWS, LANES), BF16),
        compiler_params=pltpu.CompilerParams(vmem_limit_bytes=32 * 2**20),
        name="away_sum",
    )(place, parts)


def unpack_kernel(factor, place, parts, other, wv, wc, we, ws, pv, pc, pe, ps):
    def total(low, high):
        rows = parts[0, 0, low:high].astype(F32)
        for j in range(1, 4):
            rows += parts[j, 0, low:high].astype(F32)
        return (rows + other[low:high].astype(F32)) * factor

    for j in range(3):
        wv[:, j * LANES : (j + 1) * LANES] = total(j * WIDE, (j + 1) * WIDE)
    row = 3 * WIDE
    for ref in (wc, we, ws):
        ref[...] = total(row, row + SMALL)
        row += SMALL
    for j in range(5):
        at = W_ROWS + j * COLS
        for ref, (low, high) in zip((pv, pc, pe, ps), SPANS):
            ref[:, j * LANES : (j + 1) * LANES] = total(at + low, at + high)


def unpack(place, parts, other, factor):
    sizes = [(WIDE, 384)] + [(SMALL, 128)] * 3 + [(WIDE, 640)] + [(SMALL, 640)] * 3
    return pl.pallas_call(
        lambda *refs: unpack_kernel(factor, *refs),
        grid_spec=pltpu.PrefetchScalarGridSpec(
            num_scalar_prefetch=1,
            grid=(1,),
            in_specs=[
                pl.BlockSpec((4, 1, ROWS, LANES), lambda i, p: (0, p[9], 0, 0)),
                pl.BlockSpec((ROWS, LANES), lambda i, p: (0, 0)),
            ],
            out_specs=[pl.BlockSpec(size, lambda i, p: (0, 0)) for size in sizes],
        ),
        out_shape=[jax.ShapeDtypeStruct(size, F32) for size in sizes],
        compiler_params=pltpu.CompilerParams(vmem_limit_bytes=32 * 2**20),
        name="unpack",
    )(place, parts, other)


def partial_kernel(rows, hidden, out):
    out[0] = dot(rows[0], hidden[...], 1, 0).astype(BF16)


def partial_inputs(rows, hidden):
    depth, tokens = hidden.shape
    return pl.pallas_call(
        partial_kernel,
        grid=(4,),
        in_specs=[
            pl.BlockSpec((1, COLS, depth), lambda i: (i, 0, 0)),
            pl.BlockSpec((depth, tokens), lambda i: (0, 0)),
        ],
        out_specs=pl.BlockSpec((1, COLS, tokens), lambda i: (i, 0, 0)),
        out_shape=jax.ShapeDtypeStruct((4, COLS, tokens), BF16),
        compiler_params=pltpu.CompilerParams(vmem_limit_bytes=32 * 2**20),
        name="partial_inputs",
    )(rows, hidden)


def finish_kernel(parts, back, *outs):
    for (low, high), ref in zip(SPANS, outs):
        total = parts[0, low:high].astype(F32)
        for j in range(1, 4):
            total += parts[j, low:high].astype(F32)
        ref[...] = (back[low:high, :] + total).astype(BF16)


def finish(parts, back):
    tokens = back.shape[1]
    return pl.pallas_call(
        finish_kernel,
        out_shape=[jax.ShapeDtypeStruct((high - low, tokens), BF16) for low, high in SPANS],
        compiler_params=pltpu.CompilerParams(vmem_limit_bytes=32 * 2**20),
        name="finish",
    )(parts, back)


def body(
    acts_clip,
    acts_convnext,
    acts_eva,
    acts_sam,
    cotangent,
    weight_clip,
    weight_convnext,
    weight_eva,
    weight_sam,
    proj_clip,
    proj_convnext,
    proj_eva,
    proj_sam,
):
    acts = (acts_convnext, acts_clip, acts_eva, acts_sam)
    zh = lax.axis_index("zh")
    y = lax.axis_index("y")
    enc = lax.axis_index(ENC)
    factor = float(8 * cotangent.shape[0]) ** (-0.5)

    def around(block):
        return [block] + [
            lax.ppermute(block, "y", [(i, (i + shift) % 4) for i in range(4)]) for shift in SHIFTS
        ]

    own = pack(
        weight_convnext.T,
        weight_clip.T,
        weight_eva.T,
        weight_sam.T,
        proj_convnext.T,
        proj_clip.T,
        proj_eva.T,
        proj_sam.T,
    )
    gathered = around(own) + around(lax.ppermute(own, "zh", SWAP))
    rows_from = [(y - shift) % 4 for shift in (0,) + SHIFTS]
    place = jnp.stack(
        [zh * 4 + r for r in rows_from] + [(1 - zh) * 4 + r for r in rows_from] + [enc, zh]
    ).astype(jnp.int32)

    hidden, feature, back = forward(place, gathered, acts, cotangent)
    inner = ("x", "core")
    hidden_all = lax.all_gather(hidden, inner, axis=0, tiled=True)

    rows = send_rows(place, gathered)
    rows, hidden, feature = lax.optimization_barrier((rows, hidden, feature))
    rows = expand(lax.all_to_all(rows, inner, split_axis=0, concat_axis=0, tiled=True))

    sums = grads(hidden, feature, acts, cotangent).reshape(4, 2, ROWS, LANES)
    sums = lax.all_to_all(sums, "y", split_axis=0, concat_axis=0, tiled=True)
    other = lax.ppermute(away_sum(place, sums), "zh", SWAP)

    parts = partial_inputs(rows, hidden_all)
    parts = lax.all_to_all(parts, "zl", split_axis=0, concat_axis=0, tiled=True)
    out_v, out_c, out_e, out_s = finish(parts, back)
    wv, wc, we, ws, pv, pc, pe, ps = unpack(place, sums, other, factor)
    outs = (out_c, out_v, out_e, out_s, wc, wv, we, ws, pc, pv, pe, ps)
    return tuple(out.T for out in outs)


def solution(mesh):
    split = Mesh(mesh.devices.reshape(4, 4, 2, 2, 4), ("zl", "x", "core", "zh", "y"))
    seq = ("zh", "y")
    whole = P(seq, None)
    tiled = P(seq, ENC)
    return jax.shard_map(
        body,
        mesh=split,
        in_specs=(whole,) * 5 + (tiled,) * 8,
        out_specs=(tiled,) * 12,
        check_vma=False,
    )
```

time: 253 us -> 198 us (0.78)
  Pallas kernels: 0 us -> 43.1 us
  matrix products: 41.8 us -> 0 us
  local copies, waits for them, and re-layouts: 47.1 us -> 12.3 us
  waiting for transfers between devices: 119 us -> 92.3 us
  starting transfers between devices: 21.2 us -> 35.7 us
  other arithmetic: 8.08 us -> 0 us
    all_gather x2 -> x1, waiting for transfers between devices: 47.4 us -> 0.01 us  [body(): hidden_all = lax.all_gather(hidden, inner, axis=0, tiled=True)]
    pallas_call x0 -> x9, Pallas kernels: none -> 43.1 us  [the longest x1 13.8 us: forward(): pl.pallas_call(forward_kernel, grid_spec=pltpu.PrefetchScalarGridSpec(num...]
    dot_general x11 -> x0, matrix products: 41.8 us -> none  [dot(): lax.dot_general(left, right, (((left_dim,), (right_dim,)), ((), ())), pre...]
    ppermute x2 -> x8, waiting for transfers between devices: 25 us -> 61.2 us  [the longest x1 37.2 us: body(): other = lax.ppermute(away_sum(place, sums), 'zh', SWAP)]
    all_to_all x2 -> x3, waiting for transfers between devices: 47 us -> 31.1 us  [the longest x1 19 us: body(): sums = lax.all_to_all(sums, 'y', split_axis=0, concat_axis=0, tiled=True)]
    ppermute x2 -> x8, starting transfers between devices: 8.4 us -> 21.5 us  [the longest x6 9.34 us: around(): lax.ppermute(block, 'y', [(i, (i + shift) % 4) for i in range(4)])]
    reshape x13 -> x0, local copies, waits for them, and re-layouts: 12.1 us -> none  [the longest x1 4.31 us: unpack(): piece = gathered[:, :, start:start + rows].reshape(4, 2, count, cols, LANES)]
    transpose x13 -> x0, local copies, waits for them, and re-layouts: 9.16 us -> none  [the longest x2 5.52 us: spread(): piece = grad.reshape(cols, 2, 4, count, LANES).transpose(1, 2, 3, 0, 4)]
  transfers between devices with their start and end apart: 6 -> 12, of which waited for: 5 -> 9; matrix products, arithmetic and copies ran while one was open for 20% -> 0% of each run, Pallas kernels for 0% -> 13%
where the time goes in v2:
time: 198 us
  waiting for transfers between devices  92.3 us (47%)
  Pallas kernels  43.1 us (22%)
  starting transfers between devices  35.7 us (18%)
  between operations  14.2 us (7%)
  local copies, waits for them, and re-layouts  12.3 us (6%)
    ppermute x1, waiting for transfers between devices, body(): other = lax.ppermute(away_sum(place, sums), 'zh', SWAP)  37.2 us
    ppermute x6, waiting for transfers between devices, around(): lax.ppermute(block, 'y', [(i, (i + shift) % 4) for i in range(4)])  19.9 us
    all_to_all x1, waiting for transfers between devices, body(): sums = lax.all_to_all(sums, 'y', split_axis=0, concat_axis=0, tiled=True)  19 us
    pallas_call x1, Pallas kernels, forward(): pl.pallas_call(forward_kernel, grid_spec=pltpu.PrefetchScalarGridSpec(num...  13.8 us
    pallas_call x1, Pallas kernels, grads(): pl.pallas_call(grads_kernel, grid=(8,), in_specs=[whole] * 2 + [part(a) f...  13 us
    unnamed x36, local copies, waits for them, and re-layouts  12.3 us
    ppermute x6, starting transfers between devices, around(): lax.ppermute(block, 'y', [(i, (i + shift) % 4) for i in range(4)])  9.34 us
    ppermute x1, starting transfers between devices, body(): gathered = around(own) + around(lax.ppermute(own, 'zh', SWAP))  7.74 us
  transfers between devices with their start and end apart: 12, of which 9 were waited for; matrix products, arithmetic and copies ran while one was open for 0% of the time, Pallas kernels for 13%

profile of v2, /device:TPU:1, one launch (start us, length us, event | category | flops | bytes accessed | tf_op | source)
XLA Modules:
  0.0 197.5 jit_solution(14999595536502548859)
XLA Ops:
  7.2 1.8 pack.1.refs_0_
  9.0 7.7 %collective-permute-start.3 = (bf16[1344,128]{1,0:T(8,128)(2,1)}, bf16[1344,128]{1,0:T(8,128)(2,1)S(1)}, u32[]{:S(2)}, u32[]{:S(2)}) collective-permute-start(bf16[1344,128]{1,0:T(8,128)(2,1)} %pack.1.refs_0_), channel_id=1, source_target_pairs={{0,4},{4,0},{1,5},{5,1},{2,6},{6,2},{3,7},{7,3},{8,12},{12,8},{9,1... | collective-permute-start | bytes 1032200 | tf_op jit(solution)/shard_map/ppermute | solution.py:359
  19.5 1.6 collective-permute-start.2
  21.1 4.1 %collective-permute-done.3.refs_4_ = bf16[1344,128]{1,0:T(8,128)(2,1)S(1)} collective-permute-done((bf16[1344,128]{1,0:T(8,128)(2,1)}, bf16[1344,128]{1,0:T(8,128)(2,1)S(1)}, u32[]{:S(2)}, u32[]{:S(2)}) %collective-permute-start.3) | collective-permute-done | bytes 344096 | tf_op jit(solution)/shard_map/ppermute | solution.py:359
  25.2 1.9 collective-permute-start.4
  30.3 5.2 %collective-permute-done.2.refs_3_ = bf16[1344,128]{1,0:T(8,128)(2,1)S(1)} collective-permute-done((bf16[1344,128]{1,0:T(8,128)(2,1)}, bf16[1344,128]{1,0:T(8,128)(2,1)S(1)}, u32[]{:S(2)}, u32[]{:S(2)}) %collective-permute-start.2) | collective-permute-done | bytes 344096 | tf_op jit(solution)/shard_map/ppermute | solution.py:346
  35.5 7.5 %collective-permute-done.4.refs_5_ = bf16[1344,128]{1,0:T(8,128)(2,1)S(1)} collective-permute-done((bf16[1344,128]{1,0:T(8,128)(2,1)S(1)}, bf16[1344,128]{1,0:T(8,128)(2,1)S(1)}, u32[]{:S(2)}, u32[]{:S(2)}) %collective-permute-start.4) | collective-permute-done | bytes 344096 | tf_op jit(solution)/shard_map/ppermute | solution.py:346
  43.4 6.8 %collective-permute-done.6.refs_7_ = bf16[1344,128]{1,0:T(8,128)(2,1)S(1)} collective-permute-done((bf16[1344,128]{1,0:T(8,128)(2,1)S(1)}, bf16[1344,128]{1,0:T(8,128)(2,1)S(1)}, u32[]{:S(2)}, u32[]{:S(2)}) %collective-permute-start.6) | collective-permute-done | bytes 344096 | tf_op jit(solution)/shard_map/ppermute | solution.py:346
  51.2 13.8 %forward.1 = (bf16[192,1024]{1,0:T(8,128)(2,1)}, bf16[192,1024]{1,0:T(8,128)(2,1)S(1)}, f32[192,1024]{1,0:T(8,128)}) custom-call(s32[10]{0:T(128)S(1)} %stack.43.place.refs_0_, bf16[1344,128]{1,0:T(8,128)(2,1)S(1)} %copy-done.4, bf16[1344,128]{1,0:T(8,128)(2,1)S(1)} %collective-permute-done.refs_1_, bf16[1344,128]{1,0:T(8,128)(2,1)S(1)} %collective-permute-done.1.refs_2_, ...), custom_call_target="tpu_custom_call" | custom-call | tf_op jit(solution)/shard_map/forward/pallas_call | solution.py:111
  69.7 1.9 send_rows.1
  71.6 6.2 %all-to-all-start = ((bf16[8,4,96,128]{3,2,1,0:T(8,128)(2,1)}), bf16[8,4,96,128]{3,2,1,0:T(8,128)(2,1)S(1)}, u32[]{:S(2)}, u32[]{:S(2)}) async-start(bf16[8,4,96,128]{3,2,1,0:T(8,128)(2,1)} %send_rows.1), calls=%async_computation | async-start | bytes 1572864 | tf_op jit(solution)/shard_map/all_to_all | solution.py:371
  78.8 13.0 %grads.1 = bf16[8,1344,128]{2,1,0:T(8,128)(2,1)} custom-call(bf16[192,1024]{1,0:T(8,128)(2,1)} %get-tuple-element.38.hidden, bf16[192,1024]{1,0:T(8,128)(2,1)S(1)} %copy-done.16, bf16[1024,3072]{1,0:T(8,128)(2,1)} %acts_v.1, bf16[1024,1024]{1,0:T(8,128)(2,1)S(1)} %copy-done.1, bf16[1024,1024]{1,0:T(8,128)(2,1)} %acts_e.1, bf16[1024,1024]{1,0:T(8,128)(2,1)} %acts_s.1, ...), custom_call_target="tpu_custom_call" | custom-call | tf_op jit(solution)/shard_map/grads/pallas_call | solution.py:214
  91.8 4.9 %all-to-all-done.rows = bf16[8,4,96,128]{3,2,1,0:T(8,128)(2,1)S(1)} async-done(((bf16[8,4,96,128]{3,2,1,0:T(8,128)(2,1)}), bf16[8,4,96,128]{3,2,1,0:T(8,128)(2,1)S(1)}, u32[]{:S(2)}, u32[]{:S(2)}) %all-to-all-start) | async-done | bytes 786464 | tf_op jit(solution)/shard_map/all_to_all | solution.py:371
  97.6 3.7 %all-to-all-start.2 = ((bf16[4,2,1344,128]{3,2,1,0:T(8,128)(2,1)}), bf16[4,2,1344,128]{3,2,1,0:T(8,128)(2,1)S(1)}, u32[]{:S(2)}, u32[]{:S(2)}) async-start(bf16[4,2,1344,128]{3,2,1,0:T(8,128)(2,1)} %bitcast.31), calls=%async_computation.2 | async-start | bytes 5505024 | tf_op jit(solution)/shard_map/all_to_all | solution.py:374
  101.3 4.6 %expand_rows.1.rows = bf16[4,192,1536]{2,1,0:T(8,128)(2,1)} custom-call(bf16[8,4,96,128]{3,2,1,0:T(8,128)(2,1)} %copy-done.17), custom_call_target="tpu_custom_call" | custom-call | tf_op jit(solution)/shard_map/expand_rows/pallas_call | solution.py:186
  105.9 1.7 copy-done
  107.6 1.9 copy-done.3
  109.5 3.2 %partial_inputs.1 = bf16[4,192,1024]{2,1,0:T(8,128)(2,1)S(1)} custom-call(bf16[4,192,1536]{2,1,0:T(8,128)(2,1)S(1)} %copy-done, bf16[1536,1024]{1,0:T(8,128)(2,1)S(1)} %copy-done.3), custom_call_target="tpu_custom_call" | custom-call | tf_op jit(solution)/shard_map/partial_inputs/pallas_call | solution.py:291
  113.8 19.0 %all-to-all-done.2.parts.refs_1_ = bf16[4,2,1344,128]{3,2,1,0:T(8,128)(2,1)S(1)} async-done(((bf16[4,2,1344,128]{3,2,1,0:T(8,128)(2,1)}), bf16[4,2,1344,128]{3,2,1,0:T(8,128)(2,1)S(1)}, u32[]{:S(2)}, u32[]{:S(2)}) %all-to-all-start.2) | async-done | bytes 2752544 | tf_op jit(solution)/shard_map/all_to_all | solution.py:374
  132.8 4.3 %all-to-all-start.1 = ((bf16[4,192,1024]{2,1,0:T(8,128)(2,1)}), bf16[4,192,1024]{2,1,0:T(8,128)(2,1)}, u32[]{:S(2)}, u32[]{:S(2)}) async-start(bf16[4,192,1024]{2,1,0:T(8,128)(2,1)} %copy-done.2), calls=%async_computation.1 | async-start | bytes 3145728 | tf_op jit(solution)/shard_map/all_to_all | solution.py:378
  138.1 4.4 %collective-permute-start.7 = (bf16[1344,128]{1,0:T(8,128)(2,1)S(1)}, bf16[1344,128]{1,0:T(8,128)(2,1)S(1)}, u32[]{:S(2)}, u32[]{:S(2)}) collective-permute-start(bf16[1344,128]{1,0:T(8,128)(2,1)S(1)} %away_sum.1), channel_id=1, source_target_pairs={{0,4},{4,0},{1,5},{5,1},{2,6},{6,2},{3,7},{7,3},{8,12},{12,8},{9,1... | collective-permute-start | bytes 1032200 | tf_op jit(solution)/shard_map/ppermute | solution.py:375
  142.5 37.2 %collective-permute-done.7.refs_2_ = bf16[1344,128]{1,0:T(8,128)(2,1)S(1)} collective-permute-done((bf16[1344,128]{1,0:T(8,128)(2,1)S(1)}, bf16[1344,128]{1,0:T(8,128)(2,1)S(1)}, u32[]{:S(2)}, u32[]{:S(2)}) %collective-permute-start.7) | collective-permute-done | bytes 344096 | tf_op jit(solution)/shard_map/ppermute | solution.py:375
  181.3 7.1 %all-to-all-done.1.parts = bf16[4,192,1024]{2,1,0:T(8,128)(2,1)} async-done(((bf16[4,192,1024]{2,1,0:T(8,128)(2,1)}), bf16[4,192,1024]{2,1,0:T(8,128)(2,1)}, u32[]{:S(2)}, u32[]{:S(2)}) %all-to-all-start.1) | async-done | bytes 1572896 | tf_op jit(solution)/shard_map/all_to_all | solution.py:378
  188.4 2.3 %finish.1 = (bf16[96,1024]{1,0:T(8,128)(2,1)}, bf16[32,1024]{1,0:T(8,128)(2,1)}, bf16[32,1024]{1,0:T(8,128)(2,1)}, bf16[32,1024]{1,0:T(8,128)(2,1)}) custom-call(bf16[4,192,1024]{2,1,0:T(8,128)(2,1)} %all-to-all-done.1.parts, f32[192,1024]{1,0:T(8,128)S(1)} %copy-done.14), custom_call_target="tpu_custom_call" | custom-call | tf_op jit(solution)/shard_map/finish/pallas_call | solution.py:315
  (47 shorter events, 17.6 us)
Async XLA Ops:
  7.2 98.7 %all-gather.2.cloned.1.call-start = ((), (), s32[]{:S(2)}) async-start(), calls=%async_computation.3 | async-start | bytes 3538944 | tf_op jit(solution)/shard_map/all_gather | solution.py:367
  9.0 16.2 %collective-permute-start.3 = (bf16[1344,128]{1,0:T(8,128)(2,1)}, bf16[1344,128]{1,0:T(8,128)(2,1)S(1)}, u32[]{:S(2)}, u32[]{:S(2)}) collective-permute-start(bf16[1344,128]{1,0:T(8,128)(2,1)} %pack.1.refs_0_), channel_id=1, source_target_pairs={{0,4},{4,0},{1,5},{5,1},{2,6},{6,2},{3,7},{7,3},{8,12},{12,8},{9,1... | collective-permute-start | bytes 1032200 | tf_op jit(solution)/shard_map/ppermute | solution.py:359
  16.8 11.8 %collective-permute-start = (bf16[1344,128]{1,0:T(8,128)(2,1)}, bf16[1344,128]{1,0:T(8,128)(2,1)S(1)}, u32[]{:S(2)}, u32[]{:S(2)}) collective-permute-start(bf16[1344,128]{1,0:T(8,128)(2,1)} %pack.1.refs_0_), channel_id=1, source_target_pairs={{0,1},{1,2},{2,3},{3,0},{4,5},{5,6},{6,7},{7,4},{8,9},{9,10},{10,1... | collective-permute-start | bytes 1032200 | tf_op jit(solution)/shard_map/ppermute | solution.py:346
  18.1 12.2 %collective-permute-start.1 = (bf16[1344,128]{1,0:T(8,128)(2,1)}, bf16[1344,128]{1,0:T(8,128)(2,1)S(1)}, u32[]{:S(2)}, u32[]{:S(2)}) collective-permute-start(bf16[1344,128]{1,0:T(8,128)(2,1)} %pack.1.refs_0_), channel_id=1, source_target_pairs={{0,3},{1,0},{2,1},{3,2},{4,7},{5,4},{6,5},{7,6},{8,11},{9,8},{10,9... | collective-permute-start | bytes 1032200 | tf_op jit(solution)/shard_map/ppermute | solution.py:346
  19.5 16.0 %collective-permute-start.2 = (bf16[1344,128]{1,0:T(8,128)(2,1)}, bf16[1344,128]{1,0:T(8,128)(2,1)S(1)}, u32[]{:S(2)}, u32[]{:S(2)}) collective-permute-start(bf16[1344,128]{1,0:T(8,128)(2,1)} %pack.1.refs_0_), channel_id=1, source_target_pairs={{0,2},{1,3},{2,0},{3,1},{4,6},{5,7},{6,4},{7,5},{8,10},{9,11},{10,... | collective-permute-start | bytes 1032200 | tf_op jit(solution)/shard_map/ppermute | solution.py:346
  25.2 17.7 %collective-permute-start.4 = (bf16[1344,128]{1,0:T(8,128)(2,1)S(1)}, bf16[1344,128]{1,0:T(8,128)(2,1)S(1)}, u32[]{:S(2)}, u32[]{:S(2)}) collective-permute-start(bf16[1344,128]{1,0:T(8,128)(2,1)S(1)} %collective-permute-done.3.refs_4_), channel_id=1, source_target_pairs={{0,1},{1,2},{2,3},{3,0},{4,5},{5,6},{6,7},{7,4},{8,9},{9,10},{10,1... | collective-permute-start | bytes 1032200 | tf_op jit(solution)/shard_map/ppermute | solution.py:346
  27.1 16.3 %collective-permute-start.5 = (bf16[1344,128]{1,0:T(8,128)(2,1)S(1)}, bf16[1344,128]{1,0:T(8,128)(2,1)S(1)}, u32[]{:S(2)}, u32[]{:S(2)}) collective-permute-start(bf16[1344,128]{1,0:T(8,128)(2,1)S(1)} %collective-permute-done.3.refs_4_), channel_id=1, source_target_pairs={{0,3},{1,0},{2,1},{3,2},{4,7},{5,4},{6,5},{7,6},{8,11},{9,8},{10,9... | collective-permute-start | bytes 1032200 | tf_op jit(solution)/shard_map/ppermute | solution.py:346
  28.5 21.7 %collective-permute-start.6 = (bf16[1344,128]{1,0:T(8,128)(2,1)S(1)}, bf16[1344,128]{1,0:T(8,128)(2,1)S(1)}, u32[]{:S(2)}, u32[]{:S(2)}) collective-permute-start(bf16[1344,128]{1,0:T(8,128)(2,1)S(1)} %collective-permute-done.3.refs_4_), channel_id=1, source_target_pairs={{0,2},{1,3},{2,0},{3,1},{4,6},{5,7},{6,4},{7,5},{8,10},{9,11},{10,... | collective-permute-start | bytes 1032200 | tf_op jit(solution)/shard_map/ppermute | solution.py:346
  35.5 29.5 %copy-start.6 = (bf16[1344,128]{1,0:T(8,128)(2,1)}, bf16[1344,128]{1,0:T(8,128)(2,1)S(1)}, u32[]{:S(2)}) copy-start(bf16[1344,128]{1,0:T(8,128)(2,1)S(1)} %collective-permute-done.2.refs_3_) | copy-start | bytes 1032196
  42.9 22.1 %copy-start.8 = (bf16[1344,128]{1,0:T(8,128)(2,1)}, bf16[1344,128]{1,0:T(8,128)(2,1)S(1)}, u32[]{:S(2)}) copy-start(bf16[1344,128]{1,0:T(8,128)(2,1)S(1)} %collective-permute-done.4.refs_5_) | copy-start | bytes 1032196
  43.4 21.6 %copy-start.10 = (bf16[1344,128]{1,0:T(8,128)(2,1)}, bf16[1344,128]{1,0:T(8,128)(2,1)S(1)}, u32[]{:S(2)}) copy-start(bf16[1344,128]{1,0:T(8,128)(2,1)S(1)} %collective-permute-done.5.refs_6_) | copy-start | bytes 1032196
  51.2 13.8 %copy-start.12 = (bf16[1344,128]{1,0:T(8,128)(2,1)}, bf16[1344,128]{1,0:T(8,128)(2,1)S(1)}, u32[]{:S(2)}) copy-start(bf16[1344,128]{1,0:T(8,128)(2,1)S(1)} %collective-permute-done.6.refs_7_) | copy-start | bytes 1032196
  51.2 14.6 %copy-start.5 = (bf16[1344,128]{1,0:T(8,128)(2,1)S(1)}, bf16[1344,128]{1,0:T(8,128)(2,1)}, u32[]{:S(2)}) copy-start(bf16[1344,128]{1,0:T(8,128)(2,1)} %pack.1.refs_0_) | copy-start | bytes 1032196
  65.8 1.0 copy-start.7
  69.7 8.1 %copy-start.1 = (bf16[1024,1024]{1,0:T(8,128)(2,1)S(1)}, bf16[1024,1024]{1,0:T(8,128)(2,1)}, u32[]{:S(2)}) copy-start(bf16[1024,1024]{1,0:T(8,128)(2,1)} %acts_c.1) | copy-start | bytes 6291460
  71.6 25.1 %all-to-all-start = ((bf16[8,4,96,128]{3,2,1,0:T(8,128)(2,1)}), bf16[8,4,96,128]{3,2,1,0:T(8,128)(2,1)S(1)}, u32[]{:S(2)}, u32[]{:S(2)}) async-start(bf16[8,4,96,128]{3,2,1,0:T(8,128)(2,1)} %send_rows.1), calls=%async_computation | async-start | bytes 1572864 | tf_op jit(solution)/shard_map/all_to_all | solution.py:371
  77.8 1.0 copy-start.16
  97.6 35.2 %all-to-all-start.2 = ((bf16[4,2,1344,128]{3,2,1,0:T(8,128)(2,1)}), bf16[4,2,1344,128]{3,2,1,0:T(8,128)(2,1)S(1)}, u32[]{:S(2)}, u32[]{:S(2)}) async-start(bf16[4,2,1344,128]{3,2,1,0:T(8,128)(2,1)} %bitcast.31), calls=%async_computation.2 | async-start | bytes 5505024 | tf_op jit(solution)/shard_map/all_to_all | solution.py:374
  105.9 1.7 copy-start
  107.6 1.9 copy-start.3
  112.6 1.2 copy-start.2
  132.8 55.6 %all-to-all-start.1 = ((bf16[4,192,1024]{2,1,0:T(8,128)(2,1)}), bf16[4,192,1024]{2,1,0:T(8,128)(2,1)}, u32[]{:S(2)}, u32[]{:S(2)}) async-start(bf16[4,192,1024]{2,1,0:T(8,128)(2,1)} %copy-done.2), calls=%async_computation.1 | async-start | bytes 3145728 | tf_op jit(solution)/shard_map/all_to_all | solution.py:378
  137.2 51.3 %copy-start.14 = (f32[192,1024]{1,0:T(8,128)S(1)}, f32[192,1024]{1,0:T(8,128)}, u32[]{:S(2)}) copy-start(f32[192,1024]{1,0:T(8,128)} %get-tuple-element.33.back) | copy-start | bytes 2359300
  138.1 41.6 %collective-permute-start.7 = (bf16[1344,128]{1,0:T(8,128)(2,1)S(1)}, bf16[1344,128]{1,0:T(8,128)(2,1)S(1)}, u32[]{:S(2)}, u32[]{:S(2)}) collective-permute-start(bf16[1344,128]{1,0:T(8,128)(2,1)S(1)} %away_sum.1), channel_id=1, source_target_pairs={{0,4},{4,0},{1,5},{5,1},{2,6},{6,2},{3,7},{7,3},{8,12},{12,8},{9,1... | collective-permute-start | bytes 1032200 | tf_op jit(solution)/shard_map/ppermute | solution.py:375
  (6 other events, 5.5 us)
Sparse Core Ops, SparseCore 0:
  65.9 38.7 all-gather.1

commit v3 on v2

v3 whole, which is shorter than its diff:
```python
import jax
import jax.numpy as jnp
from jax import lax
from jax.experimental import pallas as pl
from jax.experimental.pallas import tpu as pltpu
from jax.sharding import Mesh, PartitionSpec as P

ROOT_HALF = 0.7071067811865476
INV_ROOT_TAU = 0.3989422804014327
LANES = 128
ENC = ("zl", "x", "core")
BF16 = jnp.bfloat16
F32 = jnp.float32
SWAP = [(0, 1), (1, 0)]
SHIFTS = (1, 3, 2)
WIDE = 96
SMALL = 32
COLS = WIDE + 3 * SMALL
SPANS = ((0, 96), (96, 128), (128, 160), (160, 192))
W_ROWS = 3 * WIDE + 3 * SMALL
ROWS = W_ROWS + 5 * COLS
FIRST = 768
TILE = 256
VMEM = 20 * 2**20
MOST = 60 * 2**20


def normal_cdf(values):
    return 0.5 * (1.0 + lax.erf(values * ROOT_HALF))


def slope_of(values):
    return normal_cdf(values) + values * jnp.exp(-0.5 * values * values) * INV_ROOT_TAU


def dot(left, right, left_dim, right_dim):
    return lax.dot_general(
        left, right, (((left_dim,), (right_dim,)), ((), ())), preferred_element_type=F32
    )


def lanes_of(start, width=LANES):
    return pl.ds(pl.multiple_of(start, LANES), width)


def pack_kernel(wv, wc, we, ws, pv, pc, pe, ps, out):
    for j in range(3):
        out[j * WIDE : (j + 1) * WIDE, :] = wv[:, j * LANES : (j + 1) * LANES]
    row = 3 * WIDE
    for ref in (wc, we, ws):
        out[row : row + SMALL, :] = ref[...]
        row += SMALL
    for ref, (low, high) in zip((pv, pc, pe, ps), SPANS):
        for j in range(5):
            at = W_ROWS + j * COLS
            out[at + low : at + high, :] = ref[:, j * LANES : (j + 1) * LANES]


def pack(*shards):
    return pl.pallas_call(
        pack_kernel,
        out_shape=jax.ShapeDtypeStruct((ROWS, LANES), BF16),
        compiler_params=pltpu.CompilerParams(vmem_limit_bytes=MOST),
        name="pack",
    )(*shards)


def forward_kernel(place, *refs):
    gathered = refs[:8]
    acts = refs[8:12]
    cotangent, hidden, feature, back = refs[12:16]
    weights = refs[16:20]
    proj = refs[20]
    held = refs[21:26]
    arrived = refs[26]
    enc = place[8]
    tiles = cotangent.shape[0] // TILE
    copies = []
    for tile in range(tiles):
        at = slice(tile * TILE, (tile + 1) * TILE)
        for i, (source, target) in enumerate(zip((cotangent, *acts), held)):
            copy = pltpu.make_async_copy(source.at[at], target.at[at], arrived.at[tile, i])
            copy.start()
            copies.append(copy)

    for source, ref in enumerate(gathered):
        seq = place[source]
        for j in range(3):
            weights[0][:WIDE, lanes_of(seq * (3 * LANES) + j * LANES)] = ref[
                j * WIDE : (j + 1) * WIDE, :
            ]
        row = 3 * WIDE
        for k in range(1, 4):
            weights[k][:SMALL, lanes_of(seq * LANES)] = ref[row : row + SMALL, :]
            row += SMALL
        for j in range(5):
            at = W_ROWS + j * COLS
            proj[:, lanes_of(seq * (5 * LANES) + j * LANES)] = ref[at : at + COLS, :]
    for k in range(4):
        cols = SPANS[k][1] - SPANS[k][0]
        shape = (cols, weights[k].shape[1])
        row = lax.broadcasted_iota(jnp.int32, shape, 0) + enc * cols
        lane = lax.broadcasted_iota(jnp.int32, shape, 1)
        weights[k][cols:, :] = jnp.where(row == lane, 1.0, 0.0).astype(BF16)

    for tile in range(tiles):
        at = slice(tile * TILE, (tile + 1) * TILE)
        for copy in copies[tile * 5 : tile * 5 + 5]:
            copy.wait()
        back_t = dot(proj[...], held[0][at, :], 1, 1)
        back[:, at] = back_t
        for k in range(4):
            low, high = SPANS[k]
            both = dot(weights[k][...], held[1 + k][at, :], 1, 1)
            pre = both[: high - low]
            cdf = normal_cdf(pre)
            slope = cdf + pre * jnp.exp(-0.5 * pre * pre) * INV_ROOT_TAU
            feature[low:high, at] = (both[high - low :] + pre * cdf).astype(BF16)
            hidden[low:high, at] = (back_t[low:high] * slope).astype(BF16)


def forward(place, gathered, acts, cotangent):
    tokens = cotangent.shape[0]
    vmem = pl.BlockSpec(memory_space=pltpu.VMEM)
    return pl.pallas_call(
        forward_kernel,
        in_specs=[pl.BlockSpec(memory_space=pltpu.SMEM)] + [vmem] * 8
        + [pl.BlockSpec(memory_space=pl.ANY)] * 5,
        out_specs=[vmem] * 3,
        scratch_shapes=[
            pltpu.VMEM((2 * (high - low), a.shape[1]), BF16) for (low, high), a in zip(SPANS, acts)
        ]
        + [pltpu.VMEM((COLS, cotangent.shape[1]), BF16)]
        + [pltpu.VMEM(a.shape, BF16) for a in (cotangent, *acts)]
        + [pltpu.SemaphoreType.DMA((tokens // TILE, 5))],
        out_shape=[
            jax.ShapeDtypeStruct((COLS, tokens), BF16),
            jax.ShapeDtypeStruct((COLS, tokens), BF16),
            jax.ShapeDtypeStruct((COLS, tokens), F32),
        ],
        compiler_params=pltpu.CompilerParams(vmem_limit_bytes=MOST),
        name="forward",
    )(place, *gathered, *acts, cotangent)


def send_kernel(place, *refs):
    out = refs[8]
    for source, ref in enumerate(refs[:8]):
        seq = place[source]
        line = seq // 2
        first = (seq % 2) * 4
        wide = jnp.concatenate([ref[j * WIDE : (j + 1) * WIDE, :] for j in range(3)], axis=1)
        narrow = ref[3 * WIDE : W_ROWS, :]
        for j in range(4):
            out[first + j, line] = jnp.concatenate(
                [wide[:, j * WIDE : (j + 1) * WIDE], narrow[:, j * SMALL : (j + 1) * SMALL]],
                axis=1,
            )


def send_rows(place, gathered):
    return pl.pallas_call(
        send_kernel,
        grid_spec=pltpu.PrefetchScalarGridSpec(
            num_scalar_prefetch=1,
            grid=(1,),
            in_specs=[pl.BlockSpec((W_ROWS, LANES), lambda i, p: (0, 0))] * 8,
            out_specs=pl.BlockSpec((8, 4, WIDE, LANES), lambda i, p: (0, 0, 0, 0)),
        ),
        out_shape=jax.ShapeDtypeStruct((8, 4, WIDE, LANES), BF16),
        compiler_params=pltpu.CompilerParams(vmem_limit_bytes=VMEM),
        name="send_rows",
    )(place, *gathered)


def expand_kernel(rows, out):
    lane = lax.broadcasted_iota(jnp.int32, (WIDE, LANES), 1)
    zero = jnp.zeros((WIDE, LANES), BF16)
    for group in range(4):
        pieces = []
        for j in range(2):
            block = rows[group * 2 + j, 0]
            conv = jnp.where(lane < WIDE, block, zero)
            rest = jnp.where(lane < WIDE, zero, block)
            clip = jnp.concatenate([rest[:SMALL], zero[:SMALL]], axis=1)
            turned = pltpu.roll(rest[SMALL:].astype(F32), SMALL, 1).astype(BF16)
            eva = jnp.concatenate([zero[:SMALL], turned[:SMALL]], axis=1)
            later = pltpu.roll(turned[SMALL:].astype(F32), SMALL, 1).astype(BF16)
            sam = jnp.concatenate([zero[:SMALL], later], axis=1)
            conv = jnp.concatenate([conv, zero], axis=1)
            pieces += [conv, clip, eva, sam]
        both = jnp.concatenate(pieces, axis=0)
        turned = both.astype(F32).T.astype(BF16)
        out[0, :, group * 2 * COLS : (group + 1) * 2 * COLS] = turned[:COLS]


def expand(rows):
    return pl.pallas_call(
        expand_kernel,
        grid=(4,),
        in_specs=[pl.BlockSpec((8, 1, WIDE, LANES), lambda i: (0, i, 0, 0))],
        out_specs=pl.BlockSpec((1, COLS, 8 * COLS), lambda i: (i, 0, 0)),
        out_shape=jax.ShapeDtypeStruct((4, COLS, 8 * COLS), BF16),
        compiler_params=pltpu.CompilerParams(vmem_limit_bytes=VMEM),
        name="expand_rows",
    )(rows)


def grads_kernel(order, hidden, feature, *refs):
    sources = refs[:5]
    outs = refs[5:9]
    held = refs[9:14]
    arrived = refs[14]
    copies = []
    for step in range(4):
        for i, (source, target) in enumerate(zip(sources, held)):
            width = target.shape[2]
            copy = pltpu.make_async_copy(
                source.at[:, lanes_of(order[step] * width, width)],
                target.at[step],
                arrived.at[step, i],
            )
            copy.start()
            copies.append(copy)
    for step, out in enumerate(outs):
        for copy in copies[step * 5 : step * 5 + 5]:
            copy.wait()
        wide = dot(hidden[:WIDE, :], held[0][step], 1, 0)
        for j in range(3):
            out[j * WIDE : (j + 1) * WIDE, :] = wide[:, j * LANES : (j + 1) * LANES].astype(BF16)
        row = 3 * WIDE
        for (low, high), ref in zip(SPANS[1:], held[1:4]):
            out[row : row + SMALL, :] = dot(hidden[low:high, :], ref[step], 1, 0).astype(BF16)
            row += SMALL
        proj = dot(feature[...], held[4][step], 1, 0)
        for j in range(5):
            at = W_ROWS + j * COLS
            out[at : at + COLS, :] = proj[:, j * LANES : (j + 1) * LANES].astype(BF16)


def grads(order, hidden, feature, acts, cotangent):
    arrays = (*acts, cotangent)
    vmem = pl.BlockSpec(memory_space=pltpu.VMEM)
    return pl.pallas_call(
        grads_kernel,
        in_specs=[pl.BlockSpec(memory_space=pltpu.SMEM)]
        + [vmem] * 2
        + [pl.BlockSpec(memory_space=pl.ANY)] * 5,
        out_specs=[vmem] * 4,
        out_shape=[jax.ShapeDtypeStruct((ROWS, LANES), BF16)] * 4,
        scratch_shapes=[pltpu.VMEM((4, a.shape[0], a.shape[1] // 8), BF16) for a in arrays]
        + [pltpu.SemaphoreType.DMA((4, 5))],
        compiler_params=pltpu.CompilerParams(vmem_limit_bytes=MOST),
        name="grads",
    )(order, hidden, feature, *arrays)


def away_kernel(*refs):
    total = refs[0][...].astype(F32)
    for ref in refs[1:4]:
        total += ref[...].astype(F32)
    total = total.astype(BF16)
    refs[4][...] = total[:FIRST]
    refs[5][...] = total[FIRST:]


def away_sum(parts):
    return pl.pallas_call(
        away_kernel,
        out_shape=[
            jax.ShapeDtypeStruct((FIRST, LANES), BF16),
            jax.ShapeDtypeStruct((ROWS - FIRST, LANES), BF16),
        ],
        compiler_params=pltpu.CompilerParams(vmem_limit_bytes=VMEM),
        name="away_sum",
    )(*parts)


def unpack_kernel(factor, *refs):
    parts = refs[:4]
    first, second = refs[4:6]
    wv, wc, we, ws, pv, pc, pe, ps = refs[6:]

    def total(low, high):
        rows = parts[0][low:high].astype(F32)
        for ref in parts[1:]:
            rows += ref[low:high].astype(F32)
        if high <= FIRST:
            away = first[low:high]
        elif low >= FIRST:
            away = second[low - FIRST : high - FIRST]
        else:
            away = jnp.concatenate([first[low:FIRST], second[: high - FIRST]], axis=0)
        return (rows + away.astype(F32)) * factor

    for j in range(3):
        wv[:, j * LANES : (j + 1) * LANES] = total(j * WIDE, (j + 1) * WIDE)
    row = 3 * WIDE
    for ref in (wc, we, ws):
        ref[...] = total(row, row + SMALL)
        row += SMALL
    for j in range(5):
        at = W_ROWS + j * COLS
        for ref, (low, high) in zip((pv, pc, pe, ps), SPANS):
            ref[:, j * LANES : (j + 1) * LANES] = total(at + low, at + high)


def unpack(parts, factor):
    sizes = [(WIDE, 384)] + [(SMALL, 128)] * 3 + [(WIDE, 640)] + [(SMALL, 640)] * 3
    return pl.pallas_call(
        lambda *refs: unpack_kernel(factor, *refs),
        out_shape=[jax.ShapeDtypeStruct(size, F32) for size in sizes],
        compiler_params=pltpu.CompilerParams(vmem_limit_bytes=VMEM),
        name="unpack",
    )(*parts)


def partial_kernel(rows, hidden, out):
    out[0] = dot(rows[0], hidden[...], 1, 0).astype(BF16)


def partial_inputs(rows, hidden):
    depth, tokens = hidden.shape
    return pl.pallas_call(
        partial_kernel,
        grid=(4,),
        in_specs=[
            pl.BlockSpec((1, COLS, depth), lambda i: (i, 0, 0)),
            pl.BlockSpec((depth, tokens), lambda i: (0, 0)),
        ],
        out_specs=pl.BlockSpec((1, COLS, tokens), lambda i: (i, 0, 0)),
        out_shape=jax.ShapeDtypeStruct((4, COLS, tokens), BF16),
        compiler_params=pltpu.CompilerParams(vmem_limit_bytes=VMEM),
        name="partial_inputs",
    )(rows, hidden)


def finish_kernel(parts, back, *outs):
    for (low, high), ref in zip(SPANS, outs):
        total = parts[0, low:high].astype(F32)
        for j in range(1, 4):
            total += parts[j, low:high].astype(F32)
        ref[...] = (back[low:high, :] + total).astype(BF16)


def finish(parts, back):
    tokens = back.shape[1]
    return pl.pallas_call(
        finish_kernel,
        out_shape=[jax.ShapeDtypeStruct((high - low, tokens), BF16) for low, high in SPANS],
        compiler_params=pltpu.CompilerParams(vmem_limit_bytes=VMEM),
        name="finish",
    )(parts, back)


def body(
    acts_clip,
    acts_convnext,
    acts_eva,
    acts_sam,
    cotangent,
    weight_clip,
    weight_convnext,
    weight_eva,
    weight_sam,
    proj_clip,
    proj_convnext,
    proj_eva,
    proj_sam,
):
    acts = (acts_convnext, acts_clip, acts_eva, acts_sam)
    zh = lax.axis_index("zh")
    y = lax.axis_index("y")
    enc = lax.axis_index(ENC)
    factor = float(8 * cotangent.shape[0]) ** (-0.5)

    def turn(block, shift):
        return lax.ppermute(block, "y", [(i, (i + shift) % 4) for i in range(4)])

    def around(block):
        return [block] + [turn(block, shift) for shift in SHIFTS]

    own = pack(
        weight_convnext.T,
        weight_clip.T,
        weight_eva.T,
        weight_sam.T,
        proj_convnext.T,
        proj_clip.T,
        proj_eva.T,
        proj_sam.T,
    )
    gathered = around(own) + around(lax.ppermute(own, "zh", SWAP))
    rows_from = [(y - shift) & 3 for shift in (0,) + SHIFTS]
    place = jnp.stack(
        [zh * 4 + r for r in rows_from] + [(1 - zh) * 4 + r for r in rows_from] + [enc]
    ).astype(jnp.int32)

    hidden, feature, back = forward(place, gathered, acts, cotangent)
    inner = ("x", "core")
    hidden_all = lax.all_gather(hidden, inner, axis=0, tiled=True)

    heads = [(y + shift) & 3 for shift in (0,) + SHIFTS]

    def terms(half, hidden, feature):
        order = jnp.stack([half * 4 + head for head in heads]).astype(jnp.int32)
        return grads(order, hidden, feature, acts, cotangent)

    def turned(blocks):
        return [blocks[0]] + [turn(block, shift) for block, shift in zip(blocks[1:], SHIFTS)]

    away = terms(1 - zh, hidden, feature)
    away, hidden, feature, gathered = lax.optimization_barrier((away, hidden, feature, gathered))
    away = turned(away)
    rows = send_rows(place, gathered)
    rows, hidden, feature = lax.optimization_barrier((rows, hidden, feature))
    rows = lax.all_to_all(rows, inner, split_axis=0, concat_axis=0, tiled=True)
    near = terms(zh, hidden, feature)
    first, second = away_sum(away)
    first = lax.ppermute(first, "zh", SWAP)
    rows, near, first = lax.optimization_barrier((rows, near, first))
    rows = expand(rows)
    sums = turned(near) + [first, lax.ppermute(second, "zh", SWAP)]

    parts = partial_inputs(rows, hidden_all)
    parts = lax.all_to_all(parts, "zl", split_axis=0, concat_axis=0, tiled=True)
    out_v, out_c, out_e, out_s = finish(parts, back)
    wv, wc, we, ws, pv, pc, pe, ps = unpack(sums, factor)
    outs = (out_c, out_v, out_e, out_s, wc, wv, we, ws, pc, pv, pe, ps)
    return tuple(out.T for out in outs)


def solution(mesh):
    split = Mesh(mesh.devices.reshape(4, 4, 2, 2, 4), ("zl", "x", "core", "zh", "y"))
    seq = ("zh", "y")
    whole = P(seq, None)
    tiled = P(seq, ENC)
    return jax.shard_map(
        body,
        mesh=split,
        in_specs=(whole,) * 5 + (tiled,) * 8,
        out_specs=(tiled,) * 12,
        check_vma=False,
    )
```

time: 198 us -> 179 us (0.904)
  waiting for transfers between devices: 92.3 us -> 76.6 us
  local copies, waits for them, and re-layouts: 12.3 us -> 4.45 us
  starting transfers between devices: 35.7 us -> 41.6 us
  Pallas kernels: 43.1 us -> 40.1 us
    all_to_all x2 -> x1, waiting for transfers between devices: 24 us -> 0.01 us  [body(): rows = lax.all_to_all(rows, inner, split_axis=0, concat_axis=0, tiled=True)]
    unnamed x36 -> x46, local copies, waits for them, and re-layouts: 12.3 us -> 3.84 us
    ppermute x7 -> x14, waiting for transfers between devices: 57.1 us -> 65.1 us  [the longest x12 35.1 us: turn(): return lax.ppermute(block, 'y', [(i, (i + shift) % 4) for i in range(4)])]
    ppermute x7 -> x14, starting transfers between devices: 13.7 us -> 19.1 us  [the longest x12 15.4 us: turn(): return lax.ppermute(block, 'y', [(i, (i + shift) % 4) for i in range(4)])]
    all_to_all x1, starting transfers between devices: 4.34 us -> 8.61 us  [body(): parts = lax.all_to_all(parts, 'zl', split_axis=0, concat_axis=0, tiled=True)]
    all_to_all x2 -> x1, starting transfers between devices: 9.83 us -> 6.15 us  [body(): rows = lax.all_to_all(rows, inner, split_axis=0, concat_axis=0, tiled=True)]
    pallas_call x1, Pallas kernels: 4.61 us -> 2.13 us  [expand(): pl.pallas_call(expand_kernel, grid=(4,), in_specs=[pl.BlockSpec((8, 1, WI...]
    pallas_call x4 -> x5, Pallas kernels: 29.3 us -> 30.1 us  [the longest x2 14.7 us: grads(): pl.pallas_call(grads_kernel, in_specs=[pl.BlockSpec(memory_space=pltpu.SM...]
  transfers between devices with their start and end apart: 12 -> 18, of which waited for: 9 -> 10; matrix products, arithmetic and copies ran while one was open for 0% -> 1% of each run, Pallas kernels for 13% -> 11%
where the time goes in v3:
time: 179 us; the launch traced here: 178 us
  waiting for transfers between devices  76.6 us (43%)
  starting transfers between devices  41.6 us (23%)
  Pallas kernels  40.1 us (22%)
  between operations  14.3 us (8%)
  local copies, waits for them, and re-layouts  4.45 us (2%)
    ppermute x12, waiting for transfers between devices, turn(): return lax.ppermute(block, 'y', [(i, (i + shift) % 4) for i in range(4)])  35.1 us
    ppermute x1, waiting for transfers between devices, body(): sums = turned(near) + [first, lax.ppermute(second, 'zh', SWAP)]  28.4 us
    ppermute x12, starting transfers between devices, turn(): return lax.ppermute(block, 'y', [(i, (i + shift) % 4) for i in range(4)])  15.4 us
    pallas_call x2, Pallas kernels, grads(): pl.pallas_call(grads_kernel, in_specs=[pl.BlockSpec(memory_space=pltpu.SM...  14.7 us
    pallas_call x1, Pallas kernels, forward(): pl.pallas_call(forward_kernel, in_specs=[pl.BlockSpec(memory_space=pltpu....  14.3 us
    all_to_all x1, starting transfers between devices, body(): parts = lax.all_to_all(parts, 'zl', split_axis=0, concat_axis=0, tiled=True)  8.61 us
    ppermute x1, starting transfers between devices, body(): gathered = around(own) + around(lax.ppermute(own, 'zh', SWAP))  7.74 us
    all_to_all x1, waiting for transfers between devices, body(): parts = lax.all_to_all(parts, 'zl', split_axis=0, concat_axis=0, tiled=True)  7.41 us
  transfers between devices with their start and end apart: 18, of which 10 were waited for; matrix products, arithmetic and copies ran while one was open for 1% of the time, Pallas kernels for 11%

profile of v3, /device:TPU:1, one launch (start us, length us, event | category | flops | bytes accessed | tf_op | source)
XLA Modules:
  0.0 178.3 jit_solution(16695819873860539245)
XLA Ops:
  7.2 1.8 %pack.1.refs_0_ = bf16[1344,128]{1,0:T(8,128)(2,1)} custom-call(bf16[96,384]{1,0:T(8,128)(2,1)} %bitcast.36, bf16[32,128]{1,0:T(8,128)(2,1)} %bitcast.40, bf16[32,128]{1,0:T(8,128)(2,1)} %bitcast.41, bf16[32,128]{1,0:T(8,128)(2,1)} %bitcast.42, bf16[96,640]{1,0:T(8,128)(2,1)} %bitcast.35, bf16[32,640]{1,0:T(8,128)(2,1)} %bitcast.37, ...), custom_call_target="tpu_custom_call" | custom-call | tf_op jit(solution)/shard_map/pack/pallas_call | solution.py:60
  9.1 7.7 %collective-permute-start.3 = (bf16[1344,128]{1,0:T(8,128)(2,1)}, bf16[1344,128]{1,0:T(8,128)(2,1)S(1)}, u32[]{:S(2)}, u32[]{:S(2)}) collective-permute-start(bf16[1344,128]{1,0:T(8,128)(2,1)} %pack.1.refs_0_), channel_id=1, source_target_pairs={{0,4},{4,0},{1,5},{5,1},{2,6},{6,2},{3,7},{7,3},{8,12},{12,8},{9,1... | collective-permute-start | bytes 1032200 | tf_op jit(solution)/shard_map/ppermute | solution.py:393
  21.2 4.1 %collective-permute-done.3.refs_4_ = bf16[1344,128]{1,0:T(8,128)(2,1)S(1)} collective-permute-done((bf16[1344,128]{1,0:T(8,128)(2,1)}, bf16[1344,128]{1,0:T(8,128)(2,1)S(1)}, u32[]{:S(2)}, u32[]{:S(2)}) %collective-permute-start.3) | collective-permute-done | bytes 344096 | tf_op jit(solution)/shard_map/ppermute | solution.py:393
  25.2 1.9 %collective-permute-start.4 = (bf16[1344,128]{1,0:T(8,128)(2,1)S(1)}, bf16[1344,128]{1,0:T(8,128)(2,1)S(1)}, u32[]{:S(2)}, u32[]{:S(2)}) collective-permute-start(bf16[1344,128]{1,0:T(8,128)(2,1)S(1)} %collective-permute-done.3.refs_4_), channel_id=1, source_target_pairs={{0,1},{1,2},{2,3},{3,0},{4,5},{5,6},{6,7},{7,4},{8,9},{9,10},{10,1... | collective-permute-start | bytes 1032200 | tf_op jit(solution)/shard_map/ppermute | solution.py:378
  28.6 1.6 collective-permute-start.6
  30.8 4.7 %collective-permute-done.2.refs_3_ = bf16[1344,128]{1,0:T(8,128)(2,1)S(1)} collective-permute-done((bf16[1344,128]{1,0:T(8,128)(2,1)}, bf16[1344,128]{1,0:T(8,128)(2,1)S(1)}, u32[]{:S(2)}, u32[]{:S(2)}) %collective-permute-start.2) | collective-permute-done | bytes 344096 | tf_op jit(solution)/shard_map/ppermute | solution.py:378
  35.5 7.5 %collective-permute-done.4.refs_5_ = bf16[1344,128]{1,0:T(8,128)(2,1)S(1)} collective-permute-done((bf16[1344,128]{1,0:T(8,128)(2,1)S(1)}, bf16[1344,128]{1,0:T(8,128)(2,1)S(1)}, u32[]{:S(2)}, u32[]{:S(2)}) %collective-permute-start.4) | collective-permute-done | bytes 344096 | tf_op jit(solution)/shard_map/ppermute | solution.py:378
  43.4 6.8 %collective-permute-done.6.refs_7_ = bf16[1344,128]{1,0:T(8,128)(2,1)S(1)} collective-permute-done((bf16[1344,128]{1,0:T(8,128)(2,1)S(1)}, bf16[1344,128]{1,0:T(8,128)(2,1)S(1)}, u32[]{:S(2)}, u32[]{:S(2)}) %collective-permute-start.6) | collective-permute-done | bytes 344096 | tf_op jit(solution)/shard_map/ppermute | solution.py:378
  51.0 14.3 %forward.1 = (bf16[192,1024]{1,0:T(8,128)(2,1)}, bf16[192,1024]{1,0:T(8,128)(2,1)}, f32[192,1024]{1,0:T(8,128)}) custom-call(s32[9]{0:T(128)} %stack.65.place, bf16[1344,128]{1,0:T(8,128)(2,1)} %pack.1.refs_0_, bf16[1344,128]{1,0:T(8,128)(2,1)} %copy-done.5, bf16[1344,128]{1,0:T(8,128)(2,1)} %copy-done.7, bf16[1344,128]{1,0:T(8,128)(2,1)} %copy-done.9, ...), custom_call_target="tpu_custom_call" | custom-call | tf_op jit(solution)/shard_map/forward/pallas_call | solution.py:125
  66.0 7.4 %grads.2 = (bf16[1344,128]{1,0:T(8,128)(2,1)}, bf16[1344,128]{1,0:T(8,128)(2,1)}, bf16[1344,128]{1,0:T(8,128)(2,1)}, bf16[1344,128]{1,0:T(8,128)(2,1)}) custom-call(s32[4]{0:T(128)} %pad_add_fusion.order, bf16[192,1024]{1,0:T(8,128)(2,1)} %get-tuple-element.77.hidden, bf16[192,1024]{1,0:T(8,128)(2,1)} %get-tuple-element.78.feature, ...), custom_call_target="tpu_custom_call" | custom-call | tf_op jit(solution)/shard_map/grads/pallas_call | solution.py:244
  73.5 1.9 %send_rows.1 = bf16[8,4,96,128]{3,2,1,0:T(8,128)(2,1)} custom-call(s32[9]{0:T(128)S(1)} %copy-done.20, bf16[1344,128]{1,0:T(8,128)(2,1)S(1)} %copy-done.2, bf16[1344,128]{1,0:T(8,128)(2,1)S(1)} %copy-done.6, bf16[1344,128]{1,0:T(8,128)(2,1)S(1)} %copy-done.8, bf16[1344,128]{1,0:T(8,128)(2,1)S(1)} %copy-done.10, bf16[1344,128]{1,0:T(8,128)(2,1)S(1)} %copy-done.4, ...), custom_call_target="tpu_custom_call" | custom-call | tf_op jit(solution)/shard_map/send_rows/pallas_call | solution.py:162
  75.5 6.2 %all-to-all-start = ((bf16[8,4,96,128]{3,2,1,0:T(8,128)(2,1)}), bf16[8,4,96,128]{3,2,1,0:T(8,128)(2,1)S(1)}, u32[]{:S(2)}, u32[]{:S(2)}) async-start(bf16[8,4,96,128]{3,2,1,0:T(8,128)(2,1)} %send_rows.1), calls=%async_computation | async-start | bytes 1572864 | tf_op jit(solution)/shard_map/all_to_all | solution.py:417
  82.5 1.8 %collective-permute-start.8 = (bf16[1344,128]{1,0:T(8,128)(2,1)S(1)}, bf16[1344,128]{1,0:T(8,128)(2,1)S(1)}, u32[]{:S(2)}, u32[]{:S(2)}) collective-permute-start(bf16[1344,128]{1,0:T(8,128)(2,1)S(1)} %copy-done.22), channel_id=1, source_target_pairs={{0,3},{1,0},{2,1},{3,2},{4,7},{5,4},{6,5},{7,6},{8,11},{9,8},{10,9... | collective-permute-start | bytes 1032200 | tf_op jit(solution)/shard_map/ppermute | solution.py:378
  85.0 7.8 %collective-permute-done.7.refs_1_ = bf16[1344,128]{1,0:T(8,128)(2,1)S(1)} collective-permute-done((bf16[1344,128]{1,0:T(8,128)(2,1)}, bf16[1344,128]{1,0:T(8,128)(2,1)S(1)}, u32[]{:S(2)}, u32[]{:S(2)}) %collective-permute-start.7) | collective-permute-done | bytes 344096 | tf_op jit(solution)/shard_map/ppermute | solution.py:378
  92.8 7.9 %collective-permute-done.9.refs_3_ = bf16[1344,128]{1,0:T(8,128)(2,1)S(1)} collective-permute-done((bf16[1344,128]{1,0:T(8,128)(2,1)S(1)}, bf16[1344,128]{1,0:T(8,128)(2,1)S(1)}, u32[]{:S(2)}, u32[]{:S(2)}) %collective-permute-start.9) | collective-permute-done | bytes 344096 | tf_op jit(solution)/shard_map/ppermute | solution.py:378
  101.9 7.3 %grads.3 = (bf16[1344,128]{1,0:T(8,128)(2,1)}, bf16[1344,128]{1,0:T(8,128)(2,1)}, bf16[1344,128]{1,0:T(8,128)(2,1)}, bf16[1344,128]{1,0:T(8,128)(2,1)}) custom-call(s32[4]{0:T(128)} %pad_add_fusion.1.order, bf16[192,1024]{1,0:T(8,128)(2,1)} %get-tuple-element.77.hidden, bf16[192,1024]{1,0:T(8,128)(2,1)} %get-tuple-element.78.feature, ...), custom_call_target="tpu_custom_call" | custom-call | tf_op jit(solution)/shard_map/grads/pallas_call | solution.py:244
  110.8 2.1 %expand_rows.1.rows = bf16[4,192,1536]{2,1,0:T(8,128)(2,1)S(1)} custom-call(bf16[8,4,96,128]{3,2,1,0:T(8,128)(2,1)S(1)} %all-to-all-done.rows), custom_call_target="tpu_custom_call" | custom-call | tf_op jit(solution)/shard_map/expand_rows/pallas_call | solution.py:198
  113.0 1.9 %copy-done.1 = bf16[1536,1024]{1,0:T(8,128)(2,1)S(1)} copy-done((bf16[1536,1024]{1,0:T(8,128)(2,1)S(1)}, bf16[1536,1024]{1,0:T(8,128)(2,1)}, u32[]{:S(2)}) %copy-start.1) | copy-done | bytes 3145752
  114.8 3.2 %partial_inputs.1 = bf16[4,192,1024]{2,1,0:T(8,128)(2,1)S(1)} custom-call(bf16[4,192,1536]{2,1,0:T(8,128)(2,1)S(1)} %expand_rows.1.rows, bf16[1536,1024]{1,0:T(8,128)(2,1)S(1)} %copy-done.1), custom_call_target="tpu_custom_call" | custom-call | tf_op jit(solution)/shard_map/partial_inputs/pallas_call | solution.py:324
  119.2 8.6 %all-to-all-start.1 = ((bf16[4,192,1024]{2,1,0:T(8,128)(2,1)}), bf16[4,192,1024]{2,1,0:T(8,128)(2,1)S(1)}, u32[]{:S(2)}, u32[]{:S(2)}) async-start(bf16[4,192,1024]{2,1,0:T(8,128)(2,1)} %copy-done), calls=%async_computation.1 | async-start | bytes 3145728 | tf_op jit(solution)/shard_map/all_to_all | solution.py:426
  128.3 2.2 %collective-permute-start.12 = (bf16[1344,128]{1,0:T(8,128)(2,1)}, bf16[1344,128]{1,0:T(8,128)(2,1)S(1)}, u32[]{:S(2)}, u32[]{:S(2)}) collective-permute-start(bf16[1344,128]{1,0:T(8,128)(2,1)} %get-tuple-element.96), channel_id=1, source_target_pairs={{0,3},{1,0},{2,1},{3,2},{4,7},{5,4},{6,5},{7,6},{8,11},{9,8},{10,9... | collective-permute-start | bytes 1032200 | tf_op jit(solution)/shard_map/ppermute | solution.py:378
  130.5 3.3 %collective-permute-start.14 = (bf16[576,128]{1,0:T(8,128)(2,1)S(1)}, bf16[576,128]{1,0:T(8,128)(2,1)S(1)}, u32[]{:S(2)}, u32[]{:S(2)}) collective-permute-start(bf16[576,128]{1,0:T(8,128)(2,1)S(1)} %get-tuple-element.99), channel_id=1, source_target_pairs={{0,4},{4,0},{1,5},{5,1},{2,6},{6,2},{3,7},{7,3},{8,12},{12,8},{9,1... | collective-permute-start | bytes 442376 | tf_op jit(solution)/shard_map/ppermute | solution.py:423
  133.8 28.4 %collective-permute-done.14.refs_5_ = bf16[576,128]{1,0:T(8,128)(2,1)S(1)} collective-permute-done((bf16[576,128]{1,0:T(8,128)(2,1)S(1)}, bf16[576,128]{1,0:T(8,128)(2,1)S(1)}, u32[]{:S(2)}, u32[]{:S(2)}) %collective-permute-start.14) | collective-permute-done | bytes 147488 | tf_op jit(solution)/shard_map/ppermute | solution.py:423
  163.2 7.4 %all-to-all-done.1.parts = bf16[4,192,1024]{2,1,0:T(8,128)(2,1)S(1)} async-done(((bf16[4,192,1024]{2,1,0:T(8,128)(2,1)}), bf16[4,192,1024]{2,1,0:T(8,128)(2,1)S(1)}, u32[]{:S(2)}, u32[]{:S(2)}) %all-to-all-start.1) | async-done | bytes 1572896 | tf_op jit(solution)/shard_map/all_to_all | solution.py:426
  (72 shorter events, 16.1 us)
Async XLA Ops:
  7.2 105.8 %all-gather.2.cloned.1.call-start = ((), (), s32[]{:S(2)}) async-start(), calls=%async_computation.2 | async-start | bytes 3538944 | tf_op jit(solution)/shard_map/all_gather | solution.py:401
  9.1 16.2 %collective-permute-start.3 = (bf16[1344,128]{1,0:T(8,128)(2,1)}, bf16[1344,128]{1,0:T(8,128)(2,1)S(1)}, u32[]{:S(2)}, u32[]{:S(2)}) collective-permute-start(bf16[1344,128]{1,0:T(8,128)(2,1)} %pack.1.refs_0_), channel_id=1, source_target_pairs={{0,4},{4,0},{1,5},{5,1},{2,6},{6,2},{3,7},{7,3},{8,12},{12,8},{9,1... | collective-permute-start | bytes 1032200 | tf_op jit(solution)/shard_map/ppermute | solution.py:393
  16.8 11.8 %collective-permute-start = (bf16[1344,128]{1,0:T(8,128)(2,1)}, bf16[1344,128]{1,0:T(8,128)(2,1)S(1)}, u32[]{:S(2)}, u32[]{:S(2)}) collective-permute-start(bf16[1344,128]{1,0:T(8,128)(2,1)} %pack.1.refs_0_), channel_id=1, source_target_pairs={{0,1},{1,2},{2,3},{3,0},{4,5},{5,6},{6,7},{7,4},{8,9},{9,10},{10,1... | collective-permute-start | bytes 1032200 | tf_op jit(solution)/shard_map/ppermute | solution.py:378
  18.1 12.7 %collective-permute-start.1 = (bf16[1344,128]{1,0:T(8,128)(2,1)}, bf16[1344,128]{1,0:T(8,128)(2,1)S(1)}, u32[]{:S(2)}, u32[]{:S(2)}) collective-permute-start(bf16[1344,128]{1,0:T(8,128)(2,1)} %pack.1.refs_0_), channel_id=1, source_target_pairs={{0,3},{1,0},{2,1},{3,2},{4,7},{5,4},{6,5},{7,6},{8,11},{9,8},{10,9... | collective-permute-start | bytes 1032200 | tf_op jit(solution)/shard_map/ppermute | solution.py:378
  19.5 16.0 %collective-permute-start.2 = (bf16[1344,128]{1,0:T(8,128)(2,1)}, bf16[1344,128]{1,0:T(8,128)(2,1)S(1)}, u32[]{:S(2)}, u32[]{:S(2)}) collective-permute-start(bf16[1344,128]{1,0:T(8,128)(2,1)} %pack.1.refs_0_), channel_id=1, source_target_pairs={{0,2},{1,3},{2,0},{3,1},{4,6},{5,7},{6,4},{7,5},{8,10},{9,11},{10,... | collective-permute-start | bytes 1032200 | tf_op jit(solution)/shard_map/ppermute | solution.py:378
  25.2 25.0 %copy-start.3 = (bf16[1344,128]{1,0:T(8,128)(2,1)}, bf16[1344,128]{1,0:T(8,128)(2,1)S(1)}, u32[]{:S(2)}) copy-start(bf16[1344,128]{1,0:T(8,128)(2,1)S(1)} %collective-permute-done.3.refs_4_) | copy-start | bytes 1032196
  25.2 17.7 %collective-permute-start.4 = (bf16[1344,128]{1,0:T(8,128)(2,1)S(1)}, bf16[1344,128]{1,0:T(8,128)(2,1)S(1)}, u32[]{:S(2)}, u32[]{:S(2)}) collective-permute-start(bf16[1344,128]{1,0:T(8,128)(2,1)S(1)} %collective-permute-done.3.refs_4_), channel_id=1, source_target_pairs={{0,1},{1,2},{2,3},{3,0},{4,5},{5,6},{6,7},{7,4},{8,9},{9,10},{10,1... | collective-permute-start | bytes 1032200 | tf_op jit(solution)/shard_map/ppermute | solution.py:378
  27.1 16.3 %collective-permute-start.5 = (bf16[1344,128]{1,0:T(8,128)(2,1)S(1)}, bf16[1344,128]{1,0:T(8,128)(2,1)S(1)}, u32[]{:S(2)}, u32[]{:S(2)}) collective-permute-start(bf16[1344,128]{1,0:T(8,128)(2,1)S(1)} %collective-permute-done.3.refs_4_), channel_id=1, source_target_pairs={{0,3},{1,0},{2,1},{3,2},{4,7},{5,4},{6,5},{7,6},{8,11},{9,8},{10,9... | collective-permute-start | bytes 1032200 | tf_op jit(solution)/shard_map/ppermute | solution.py:378
  28.6 21.7 %copy-start.5 = (bf16[1344,128]{1,0:T(8,128)(2,1)}, bf16[1344,128]{1,0:T(8,128)(2,1)S(1)}, u32[]{:S(2)}) copy-start(bf16[1344,128]{1,0:T(8,128)(2,1)S(1)} %collective-permute-done.refs_1_) | copy-start | bytes 1032196
  28.6 21.7 %collective-permute-start.6 = (bf16[1344,128]{1,0:T(8,128)(2,1)S(1)}, bf16[1344,128]{1,0:T(8,128)(2,1)S(1)}, u32[]{:S(2)}, u32[]{:S(2)}) collective-permute-start(bf16[1344,128]{1,0:T(8,128)(2,1)S(1)} %collective-permute-done.3.refs_4_), channel_id=1, source_target_pairs={{0,2},{1,3},{2,0},{3,1},{4,6},{5,7},{6,4},{7,5},{8,10},{9,11},{10,... | collective-permute-start | bytes 1032200 | tf_op jit(solution)/shard_map/ppermute | solution.py:378
  30.8 19.4 %copy-start.7 = (bf16[1344,128]{1,0:T(8,128)(2,1)}, bf16[1344,128]{1,0:T(8,128)(2,1)S(1)}, u32[]{:S(2)}) copy-start(bf16[1344,128]{1,0:T(8,128)(2,1)S(1)} %collective-permute-done.1.refs_2_) | copy-start | bytes 1032196
  73.5 27.2 %copy-start.19 = (bf16[1344,128]{1,0:T(8,128)(2,1)S(1)}, bf16[1344,128]{1,0:T(8,128)(2,1)}, u32[]{:S(2)}) copy-start(bf16[1344,128]{1,0:T(8,128)(2,1)} %get-tuple-element.83.refs_0_) | copy-start | bytes 1032196
  75.5 35.3 %all-to-all-start = ((bf16[8,4,96,128]{3,2,1,0:T(8,128)(2,1)}), bf16[8,4,96,128]{3,2,1,0:T(8,128)(2,1)S(1)}, u32[]{:S(2)}, u32[]{:S(2)}) async-start(bf16[8,4,96,128]{3,2,1,0:T(8,128)(2,1)} %send_rows.1), calls=%async_computation | async-start | bytes 1572864 | tf_op jit(solution)/shard_map/all_to_all | solution.py:417
  81.6 11.2 %collective-permute-start.7 = (bf16[1344,128]{1,0:T(8,128)(2,1)}, bf16[1344,128]{1,0:T(8,128)(2,1)S(1)}, u32[]{:S(2)}, u32[]{:S(2)}) collective-permute-start(bf16[1344,128]{1,0:T(8,128)(2,1)} %get-tuple-element.84), channel_id=1, source_target_pairs={{0,1},{1,2},{2,3},{3,0},{4,5},{5,6},{6,7},{7,4},{8,9},{9,10},{10,1... | collective-permute-start | bytes 1032200 | tf_op jit(solution)/shard_map/ppermute | solution.py:378
  82.5 10.4 %collective-permute-start.8 = (bf16[1344,128]{1,0:T(8,128)(2,1)S(1)}, bf16[1344,128]{1,0:T(8,128)(2,1)S(1)}, u32[]{:S(2)}, u32[]{:S(2)}) collective-permute-start(bf16[1344,128]{1,0:T(8,128)(2,1)S(1)} %copy-done.22), channel_id=1, source_target_pairs={{0,3},{1,0},{2,1},{3,2},{4,7},{5,4},{6,5},{7,6},{8,11},{9,8},{10,9... | collective-permute-start | bytes 1032200 | tf_op jit(solution)/shard_map/ppermute | solution.py:378
  84.3 16.4 %collective-permute-start.9 = (bf16[1344,128]{1,0:T(8,128)(2,1)S(1)}, bf16[1344,128]{1,0:T(8,128)(2,1)S(1)}, u32[]{:S(2)}, u32[]{:S(2)}) collective-permute-start(bf16[1344,128]{1,0:T(8,128)(2,1)S(1)} %copy-done.21), channel_id=1, source_target_pairs={{0,2},{1,3},{2,0},{3,1},{4,6},{5,7},{6,4},{7,5},{8,10},{9,11},{10,... | collective-permute-start | bytes 1032200 | tf_op jit(solution)/shard_map/ppermute | solution.py:378
  100.9 9.9 %collective-permute-start.10 = (bf16[768,128]{1,0:T(8,128)(2,1)S(1)}, bf16[768,128]{1,0:T(8,128)(2,1)S(1)}, u32[]{:S(2)}, u32[]{:S(2)}) collective-permute-start(bf16[768,128]{1,0:T(8,128)(2,1)S(1)} %get-tuple-element.87), channel_id=1, source_target_pairs={{0,4},{4,0},{1,5},{5,1},{2,6},{6,2},{3,7},{7,3},{8,12},{12,8},{9,1... | collective-permute-start | bytes 589832 | tf_op jit(solution)/shard_map/ppermute | solution.py:420
  119.2 43.0 %copy-start.18 = (bf16[1344,128]{1,0:T(8,128)(2,1)S(1)}, bf16[1344,128]{1,0:T(8,128)(2,1)}, u32[]{:S(2)}) copy-start(bf16[1344,128]{1,0:T(8,128)(2,1)} %get-tuple-element.94.refs_0_) | copy-start | bytes 1032196
  119.2 51.4 %copy-start.17 = (f32[192,1024]{1,0:T(8,128)S(1)}, f32[192,1024]{1,0:T(8,128)}, u32[]{:S(2)}) copy-start(f32[192,1024]{1,0:T(8,128)} %get-tuple-element.89.back) | copy-start | bytes 2359300
  119.2 51.4 %all-to-all-start.1 = ((bf16[4,192,1024]{2,1,0:T(8,128)(2,1)}), bf16[4,192,1024]{2,1,0:T(8,128)(2,1)S(1)}, u32[]{:S(2)}, u32[]{:S(2)}) async-start(bf16[4,192,1024]{2,1,0:T(8,128)(2,1)} %copy-done), calls=%async_computation.1 | async-start | bytes 3145728 | tf_op jit(solution)/shard_map/all_to_all | solution.py:426
  127.8 34.4 %collective-permute-start.11 = (bf16[1344,128]{1,0:T(8,128)(2,1)}, bf16[1344,128]{1,0:T(8,128)(2,1)S(1)}, u32[]{:S(2)}, u32[]{:S(2)}) collective-permute-start(bf16[1344,128]{1,0:T(8,128)(2,1)} %get-tuple-element.95), channel_id=1, source_target_pairs={{0,1},{1,2},{2,3},{3,0},{4,5},{5,6},{6,7},{7,4},{8,9},{9,10},{10,1... | collective-permute-start | bytes 1032200 | tf_op jit(solution)/shard_map/ppermute | solution.py:378
  128.3 34.0 %collective-permute-start.12 = (bf16[1344,128]{1,0:T(8,128)(2,1)}, bf16[1344,128]{1,0:T(8,128)(2,1)S(1)}, u32[]{:S(2)}, u32[]{:S(2)}) collective-permute-start(bf16[1344,128]{1,0:T(8,128)(2,1)} %get-tuple-element.96), channel_id=1, source_target_pairs={{0,3},{1,0},{2,1},{3,2},{4,7},{5,4},{6,5},{7,6},{8,11},{9,8},{10,9... | collective-permute-start | bytes 1032200 | tf_op jit(solution)/shard_map/ppermute | solution.py:378
  130.5 31.7 %collective-permute-start.13 = (bf16[1344,128]{1,0:T(8,128)(2,1)}, bf16[1344,128]{1,0:T(8,128)(2,1)S(1)}, u32[]{:S(2)}, u32[]{:S(2)}) collective-permute-start(bf16[1344,128]{1,0:T(8,128)(2,1)} %get-tuple-element.97), channel_id=1, source_target_pairs={{0,2},{1,3},{2,0},{3,1},{4,6},{5,7},{6,4},{7,5},{8,10},{9,11},{10,... | collective-permute-start | bytes 1032200 | tf_op jit(solution)/shard_map/ppermute | solution.py:378
  130.5 31.7 %collective-permute-start.14 = (bf16[576,128]{1,0:T(8,128)(2,1)S(1)}, bf16[576,128]{1,0:T(8,128)(2,1)S(1)}, u32[]{:S(2)}, u32[]{:S(2)}) collective-permute-start(bf16[576,128]{1,0:T(8,128)(2,1)S(1)} %get-tuple-element.99), channel_id=1, source_target_pairs={{0,4},{4,0},{1,5},{5,1},{2,6},{6,2},{3,7},{7,3},{8,12},{12,8},{9,1... | collective-permute-start | bytes 442376 | tf_op jit(solution)/shard_map/ppermute | solution.py:423
  (17 other events, 120.2 us)
Sparse Core Ops, SparseCore 0:
  65.4 40.6 all-gather.1

commit v4 on v3

--- a/solution.py
+++ b/solution.py
@@ -19,7 +19,6 @@
 SPANS = ((0, 96), (96, 128), (128, 160), (160, 192))
 W_ROWS = 3 * WIDE + 3 * SMALL
 ROWS = W_ROWS + 5 * COLS
-FIRST = 768
 TILE = 256
 VMEM = 20 * 2**20
 MOST = 60 * 2**20
@@ -173,13 +172,13 @@
     )(place, *gathered)
 
 
-def expand_kernel(rows, out):
+def expand_kernel(order, rows, out):
     lane = lax.broadcasted_iota(jnp.int32, (WIDE, LANES), 1)
     zero = jnp.zeros((WIDE, LANES), BF16)
     for group in range(4):
         pieces = []
         for j in range(2):
-            block = rows[group * 2 + j, 0]
+            block = rows[order[4 + group * 2 + j], 0]
             conv = jnp.where(lane < WIDE, block, zero)
             rest = jnp.where(lane < WIDE, zero, block)
             clip = jnp.concatenate([rest[:SMALL], zero[:SMALL]], axis=1)
@@ -194,16 +193,19 @@
         out[0, :, group * 2 * COLS : (group + 1) * 2 * COLS] = turned[:COLS]
 
 
-def expand(rows):
+def expand(order, rows):
     return pl.pallas_call(
         expand_kernel,
-        grid=(4,),
-        in_specs=[pl.BlockSpec((8, 1, WIDE, LANES), lambda i: (0, i, 0, 0))],
-        out_specs=pl.BlockSpec((1, COLS, 8 * COLS), lambda i: (i, 0, 0)),
+        grid_spec=pltpu.PrefetchScalarGridSpec(
+            num_scalar_prefetch=1,
+            grid=(4,),
+            in_specs=[pl.BlockSpec((8, 1, WIDE, LANES), lambda i, p: (0, p[i], 0, 0))],
+            out_specs=pl.BlockSpec((1, COLS, 8 * COLS), lambda i, p: (i, 0, 0)),
+        ),
         out_shape=jax.ShapeDtypeStruct((4, COLS, 8 * COLS), BF16),
         compiler_params=pltpu.CompilerParams(vmem_limit_bytes=VMEM),
         name="expand_rows",
-    )(rows)
+    )(order, rows)
 
 
 def grads_kernel(order, hidden, feature, *refs):
@@ -259,39 +261,27 @@
     total = refs[0][...].astype(F32)
     for ref in refs[1:4]:
         total += ref[...].astype(F32)
-    total = total.astype(BF16)
-    refs[4][...] = total[:FIRST]
-    refs[5][...] = total[FIRST:]
+    refs[4][...] = total.astype(BF16)
 
 
 def away_sum(parts):
     return pl.pallas_call(
         away_kernel,
-        out_shape=[
-            jax.ShapeDtypeStruct((FIRST, LANES), BF16),
-            jax.ShapeDtypeStruct((ROWS - FIRST, LANES), BF16),
-        ],
+        out_shape=jax.ShapeDtypeStruct((ROWS, LANES), BF16),
         compiler_params=pltpu.CompilerParams(vmem_limit_bytes=VMEM),
         name="away_sum",
     )(*parts)
 
 
 def unpack_kernel(factor, *refs):
-    parts = refs[:4]
-    first, second = refs[4:6]
-    wv, wc, we, ws, pv, pc, pe, ps = refs[6:]
+    parts = refs[:5]
+    wv, wc, we, ws, pv, pc, pe, ps = refs[5:]
 
     def total(low, high):
         rows = parts[0][low:high].astype(F32)
         for ref in parts[1:]:
             rows += ref[low:high].astype(F32)
-        if high <= FIRST:
-            away = first[low:high]
-        elif low >= FIRST:
-            away = second[low - FIRST : high - FIRST]
-        else:
-            away = jnp.concatenate([first[low:FIRST], second[: high - FIRST]], axis=0)
-        return (rows + away.astype(F32)) * factor
+        return rows * factor
 
     for j in range(3):
         wv[:, j * LANES : (j + 1) * LANES] = total(j * WIDE, (j + 1) * WIDE)
@@ -315,32 +305,43 @@
     )(*parts)
 
 
-def partial_kernel(rows, hidden, out):
-    out[0] = dot(rows[0], hidden[...], 1, 0).astype(BF16)
+def partial_kernel(rows, *refs):
+    outs, whole = refs[8:12], refs[12]
+
+    @pl.when(pl.program_id(0) == 0)
+    def _():
+        for j, ref in enumerate(refs[:8]):
+            whole[j * COLS : (j + 1) * COLS, :] = ref[...]
+
+    part = dot(rows[0], whole[...], 1, 0).astype(BF16)
+    for step, out in enumerate(outs):
+
+        @pl.when(pl.program_id(0) == step)
+        def _(out=out):
+            out[...] = part
 
 
 def partial_inputs(rows, hidden):
-    depth, tokens = hidden.shape
+    tokens = hidden[0].shape[1]
+    block = pl.BlockSpec((COLS, tokens), lambda i: (0, 0))
     return pl.pallas_call(
         partial_kernel,
         grid=(4,),
-        in_specs=[
-            pl.BlockSpec((1, COLS, depth), lambda i: (i, 0, 0)),
-            pl.BlockSpec((depth, tokens), lambda i: (0, 0)),
-        ],
-        out_specs=pl.BlockSpec((1, COLS, tokens), lambda i: (i, 0, 0)),
-        out_shape=jax.ShapeDtypeStruct((4, COLS, tokens), BF16),
+        in_specs=[pl.BlockSpec((1, COLS, 8 * COLS), lambda i: (i, 0, 0))] + [block] * 8,
+        out_specs=[block] * 4,
+        out_shape=[jax.ShapeDtypeStruct((COLS, tokens), BF16)] * 4,
+        scratch_shapes=[pltpu.VMEM((8 * COLS, tokens), BF16)],
         compiler_params=pltpu.CompilerParams(vmem_limit_bytes=VMEM),
         name="partial_inputs",
-    )(rows, hidden)
-
-
-def finish_kernel(parts, back, *outs):
-    for (low, high), ref in zip(SPANS, outs):
-        total = parts[0, low:high].astype(F32)
-        for j in range(1, 4):
-            total += parts[j, low:high].astype(F32)
-        ref[...] = (back[low:high, :] + total).astype(BF16)
+    )(rows, *hidden)
+
+
+def finish_kernel(back, *refs):
+    for (low, high), out in zip(SPANS, refs[4:]):
+        total = refs[0][low:high].astype(F32)
+        for ref in refs[1:4]:
+            total += ref[low:high].astype(F32)
+        out[...] = (back[low:high, :] + total).astype(BF16)
 
 
 def finish(parts, back):
@@ -350,7 +351,7 @@
         out_shape=[jax.ShapeDtypeStruct((high - low, tokens), BF16) for low, high in SPANS],
         compiler_params=pltpu.CompilerParams(vmem_limit_bytes=VMEM),
         name="finish",
-    )(parts, back)
+    )(back, *parts)
 
 
 def body(
@@ -374,11 +375,14 @@
     enc = lax.axis_index(ENC)
     factor = float(8 * cotangent.shape[0]) ** (-0.5)
 
-    def turn(block, shift):
-        return lax.ppermute(block, "y", [(i, (i + shift) % 4) for i in range(4)])
-
-    def around(block):
-        return [block] + [turn(block, shift) for shift in SHIFTS]
+    def turn(block, shift, axis="y"):
+        return lax.ppermute(block, axis, [(i, (i + shift) % 4) for i in range(4)])
+
+    def around(block, axis="y"):
+        return [block] + [turn(block, shift, axis) for shift in SHIFTS]
+
+    def turned(blocks, axis="y"):
+        return [blocks[0]] + [turn(b, shift, axis) for b, shift in zip(blocks[1:], SHIFTS)]
 
     own = pack(
         weight_convnext.T,
@@ -396,34 +400,33 @@
         [zh * 4 + r for r in rows_from] + [(1 - zh) * 4 + r for r in rows_from] + [enc]
     ).astype(jnp.int32)
 
+    heads = [(y + shift) & 3 for shift in (0,) + SHIFTS]
+    order_away = jnp.stack([(1 - zh) * 4 + head for head in heads]).astype(jnp.int32)
+    order_near = jnp.stack([zh * 4 + head for head in heads]).astype(jnp.int32)
+    zl = lax.axis_index("zl")
+    core = lax.axis_index("core")
+    x_from = [((lax.axis_index("x") - shift) & 3) * 2 for shift in (0,) + SHIFTS]
+    order_rows = jnp.stack(
+        [(zl + shift) & 3 for shift in (0,) + SHIFTS]
+        + [x + core for x in x_from]
+        + [x + 1 - core for x in x_from]
+    ).astype(jnp.int32)
+
+    rows = send_rows(place, gathered)
+    rows, gathered = lax.optimization_barrier((rows, gathered))
+    rows = lax.all_to_all(rows, ("x", "core"), split_axis=0, concat_axis=0, tiled=True)
+
     hidden, feature, back = forward(place, gathered, acts, cotangent)
-    inner = ("x", "core")
-    hidden_all = lax.all_gather(hidden, inner, axis=0, tiled=True)
-
-    heads = [(y + shift) & 3 for shift in (0,) + SHIFTS]
-
-    def terms(half, hidden, feature):
-        order = jnp.stack([half * 4 + head for head in heads]).astype(jnp.int32)
-        return grads(order, hidden, feature, acts, cotangent)
-
-    def turned(blocks):
-        return [blocks[0]] + [turn(block, shift) for block, shift in zip(blocks[1:], SHIFTS)]
-
-    away = terms(1 - zh, hidden, feature)
-    away, hidden, feature, gathered = lax.optimization_barrier((away, hidden, feature, gathered))
-    away = turned(away)
-    rows = send_rows(place, gathered)
-    rows, hidden, feature = lax.optimization_barrier((rows, hidden, feature))
-    rows = lax.all_to_all(rows, inner, split_axis=0, concat_axis=0, tiled=True)
-    near = terms(zh, hidden, feature)
-    first, second = away_sum(away)
-    first = lax.ppermute(first, "zh", SWAP)
-    rows, near, first = lax.optimization_barrier((rows, near, first))
-    rows = expand(rows)
-    sums = turned(near) + [first, lax.ppermute(second, "zh", SWAP)]
-
-    parts = partial_inputs(rows, hidden_all)
-    parts = lax.all_to_all(parts, "zl", split_axis=0, concat_axis=0, tiled=True)
+    hidden_all = around(hidden, "x")
+    hidden_all = hidden_all + [lax.ppermute(block, "core", SWAP) for block in hidden_all]
+
+    away = turned(grads(order_away, hidden, feature, acts, cotangent))
+    other = lax.ppermute(away_sum(away), "zh", SWAP)
+
+    parts = partial_inputs(expand(order_rows, rows), hidden_all)
+    parts, hidden, feature = lax.optimization_barrier((parts, hidden, feature))
+    sums = turned(grads(order_near, hidden, feature, acts, cotangent)) + [other]
+    parts = turned(parts, "zl")
     out_v, out_c, out_e, out_s = finish(parts, back)
     wv, wc, we, ws, pv, pc, pe, ps = unpack(sums, factor)
     outs = (out_c, out_v, out_e, out_s, wc, wv, we, ws, pc, pv, pe, ps)

time: 179 us -> 160 us (0.89)
  waiting for transfers between devices: 76.6 us -> 62.1 us
  between operations: 14.3 us -> 0.86 us
  Pallas kernels: 40.1 us -> 44.7 us
  starting transfers between devices: 41.6 us -> 44.3 us
  local copies, waits for them, and re-layouts: 4.45 us -> 6.4 us
    ppermute x14 -> x23, starting transfers between devices: 19.1 us -> 29.9 us  [the longest x18 26.8 us: turn(): return lax.ppermute(block, axis, [(i, (i + shift) % 4) for i in range(4)])]
    all_to_all x2 -> x1, starting transfers between devices: 14.8 us -> 6.7 us  [body(): lax.all_to_all(rows, ('x', 'core'), split_axis=0, concat_axis=0, tiled=True)]
    all_to_all x2 -> x1, waiting for transfers between devices: 7.42 us -> 0.01 us  [body(): lax.all_to_all(rows, ('x', 'core'), split_axis=0, concat_axis=0, tiled=True)]
    ppermute x14 -> x23, waiting for transfers between devices: 65.1 us -> 58 us  [the longest x18 58 us: turn(): return lax.ppermute(block, axis, [(i, (i + shift) % 4) for i in range(4)])]
    pallas_call x2, Pallas kernels: 2.3 us -> 4.69 us  [the longest x1 2.71 us: expand(): pl.pallas_call(expand_kernel, grid_spec=pltpu.PrefetchScalarGridSpec(num_...]
    unnamed x46 -> x38, local copies, waits for them, and re-layouts: 3.84 us -> 6.22 us
  transfers between devices with their start and end apart: 18 -> 25, of which waited for: 10 -> 10; matrix products, arithmetic and copies ran while one was open for 1% -> 1% of each run, Pallas kernels for 11% -> 16%
where the time goes in v4:
time: 160 us
  waiting for transfers between devices  62.1 us (39%)
  Pallas kernels  44.7 us (28%)
  starting transfers between devices  44.3 us (28%)
  local copies, waits for them, and re-layouts  6.4 us (4%)
    ppermute x18, waiting for transfers between devices, turn(): return lax.ppermute(block, axis, [(i, (i + shift) % 4) for i in range(4)])  58 us
    ppermute x18, starting transfers between devices, turn(): return lax.ppermute(block, axis, [(i, (i + shift) % 4) for i in range(4)])  26.8 us
    pallas_call x2, Pallas kernels, grads(): pl.pallas_call(grads_kernel, in_specs=[pl.BlockSpec(memory_space=pltpu.SM...  14.7 us
    pallas_call x1, Pallas kernels, forward(): pl.pallas_call(forward_kernel, in_specs=[pl.BlockSpec(memory_space=pltpu....  14.3 us
    ppermute x1, starting transfers between devices, body(): gathered = around(own) + around(lax.ppermute(own, 'zh', SWAP))  7.74 us
    all_to_all x1, starting transfers between devices, body(): lax.all_to_all(rows, ('x', 'core'), split_axis=0, concat_axis=0, tiled=True)  6.7 us
    unnamed x38, local copies, waits for them, and re-layouts  6.22 us
    pallas_call x1, Pallas kernels, partial_inputs(): pl.pallas_call(partial_kernel, grid=(4,), in_specs=[pl.BlockSpec((1, COLS...  4.6 us
  transfers between devices with their start and end apart: 25, of which 10 were waited for; matrix products, arithmetic and copies ran while one was open for 1% of the time, Pallas kernels for 16%

profile of v4, /device:TPU:1, one launch (start us, length us, event | category | flops | bytes accessed | tf_op | source)
XLA Modules:
  0.0 159.6 jit_solution(3199759328737803924)
XLA Ops:
  2.5 7.7 %collective-permute-start.3 = (bf16[1344,128]{1,0:T(8,128)(2,1)}, bf16[1344,128]{1,0:T(8,128)(2,1)S(1)}, u32[]{:S(2)}, u32[]{:S(2)}) collective-permute-start(bf16[1344,128]{1,0:T(8,128)(2,1)} %pack.1.refs_0_), channel_id=1, source_target_pairs={{0,4},{4,0},{1,5},{5,1},{2,6},{6,2},{3,7},{7,3},{8,12},{12,8},{9,1... | collective-permute-start | bytes 1032200 | tf_op jit(solution)/shard_map/ppermute | solution.py:397
  14.6 4.1 %collective-permute-done.3.refs_4_ = bf16[1344,128]{1,0:T(8,128)(2,1)S(1)} collective-permute-done((bf16[1344,128]{1,0:T(8,128)(2,1)}, bf16[1344,128]{1,0:T(8,128)(2,1)S(1)}, u32[]{:S(2)}, u32[]{:S(2)}) %collective-permute-start.3) | collective-permute-done | bytes 344096 | tf_op jit(solution)/shard_map/ppermute | solution.py:397
  18.6 1.9 %collective-permute-start.4 = (bf16[1344,128]{1,0:T(8,128)(2,1)S(1)}, bf16[1344,128]{1,0:T(8,128)(2,1)S(1)}, u32[]{:S(2)}, u32[]{:S(2)}) collective-permute-start(bf16[1344,128]{1,0:T(8,128)(2,1)S(1)} %collective-permute-done.3.refs_4_), channel_id=1, source_target_pairs={{0,1},{1,2},{2,3},{3,0},{4,5},{5,6},{6,7},{7,4},{8,9},{9,10},{10,1... | collective-permute-start | bytes 1032200 | tf_op jit(solution)/shard_map/ppermute | solution.py:379
  23.7 5.2 %collective-permute-done.2.refs_3_ = bf16[1344,128]{1,0:T(8,128)(2,1)S(1)} collective-permute-done((bf16[1344,128]{1,0:T(8,128)(2,1)}, bf16[1344,128]{1,0:T(8,128)(2,1)S(1)}, u32[]{:S(2)}, u32[]{:S(2)}) %collective-permute-start.2) | collective-permute-done | bytes 344096 | tf_op jit(solution)/shard_map/ppermute | solution.py:379
  28.9 7.5 %collective-permute-done.4.refs_5_ = bf16[1344,128]{1,0:T(8,128)(2,1)S(1)} collective-permute-done((bf16[1344,128]{1,0:T(8,128)(2,1)S(1)}, bf16[1344,128]{1,0:T(8,128)(2,1)S(1)}, u32[]{:S(2)}, u32[]{:S(2)}) %collective-permute-start.4) | collective-permute-done | bytes 344096 | tf_op jit(solution)/shard_map/ppermute | solution.py:379
  36.8 6.8 %collective-permute-done.6.refs_7_ = bf16[1344,128]{1,0:T(8,128)(2,1)S(1)} collective-permute-done((bf16[1344,128]{1,0:T(8,128)(2,1)S(1)}, bf16[1344,128]{1,0:T(8,128)(2,1)S(1)}, u32[]{:S(2)}, u32[]{:S(2)}) %collective-permute-start.6) | collective-permute-done | bytes 344096 | tf_op jit(solution)/shard_map/ppermute | solution.py:379
  44.6 1.9 %send_rows.1 = bf16[8,4,96,128]{3,2,1,0:T(8,128)(2,1)} custom-call(s32[9]{0:T(128)S(1)} %stack.104.place, bf16[1344,128]{1,0:T(8,128)(2,1)S(1)} %copy-done.1, bf16[1344,128]{1,0:T(8,128)(2,1)S(1)} %collective-permute-done.refs_1_, bf16[1344,128]{1,0:T(8,128)(2,1)S(1)} %collective-permute-done.1.refs_2_, ...), custom_call_target="tpu_custom_call" | custom-call | tf_op jit(solution)/shard_map/send_rows/pallas_call | solution.py:161
  46.6 14.3 %forward.1 = (bf16[192,1024]{1,0:T(8,128)(2,1)}, bf16[192,1024]{1,0:T(8,128)(2,1)}, f32[192,1024]{1,0:T(8,128)}) custom-call(s32[9]{0:T(128)} %copy-done.14, bf16[1344,128]{1,0:T(8,128)(2,1)} %pack.1.refs_0_, bf16[1344,128]{1,0:T(8,128)(2,1)} %copy-done.3, bf16[1344,128]{1,0:T(8,128)(2,1)} %copy-done.4, bf16[1344,128]{1,0:T(8,128)(2,1)} %copy-done.5, ...), custom_call_target="tpu_custom_call" | custom-call | tf_op jit(solution)/shard_map/forward/pallas_call | solution.py:124
  65.7 7.3 %grads.3 = (bf16[1344,128]{1,0:T(8,128)(2,1)}, bf16[1344,128]{1,0:T(8,128)(2,1)}, bf16[1344,128]{1,0:T(8,128)(2,1)}, bf16[1344,128]{1,0:T(8,128)(2,1)}) custom-call(s32[4]{0:T(128)} %pad_add_fusion.1.order, bf16[192,1024]{1,0:T(8,128)(2,1)} %get-tuple-element.78.refs_0_.hidden, bf16[192,1024]{1,0:T(8,128)(2,1)} %get-tuple-element.79.feature, ...), custom_call_target="tpu_custom_call" | custom-call | tf_op jit(solution)/shard_map/grads/pallas_call | solution.py:246
  73.7 2.1 %collective-permute-start.21 = (bf16[1344,128]{1,0:T(8,128)(2,1)}, bf16[1344,128]{1,0:T(8,128)(2,1)}, u32[]{:S(2)}, u32[]{:S(2)}) collective-permute-start(bf16[1344,128]{1,0:T(8,128)(2,1)} %get-tuple-element.86), channel_id=1, source_target_pairs={{0,3},{1,0},{2,1},{3,2},{4,7},{5,4},{6,5},{7,6},{8,11},{9,8},{10,9... | collective-permute-start | bytes 1032200 | tf_op jit(solution)/shard_map/ppermute | solution.py:379
  75.8 6.7 %all-to-all-start = ((bf16[8,4,96,128]{3,2,1,0:T(8,128)(2,1)}), bf16[8,4,96,128]{3,2,1,0:T(8,128)(2,1)S(1)}, u32[]{:S(2)}, u32[]{:S(2)}) async-start(bf16[8,4,96,128]{3,2,1,0:T(8,128)(2,1)} %send_rows.1), calls=%async_computation | async-start | bytes 1572864 | tf_op jit(solution)/shard_map/all_to_all | solution.py:417
  83.2 2.5 %collective-permute-start.10 = (bf16[192,1024]{1,0:T(8,128)(2,1)S(1)}, bf16[192,1024]{1,0:T(8,128)(2,1)S(1)}, u32[]{:S(2)}, u32[]{:S(2)}) collective-permute-start(bf16[192,1024]{1,0:T(8,128)(2,1)S(1)} %copy-done), channel_id=1, source_target_pairs={{0,8},{8,0},{1,9},{9,1},{2,10},{10,2},{3,11},{11,3},{4,12},{12,4},... | collective-permute-start | bytes 1179656 | tf_op jit(solution)/shard_map/ppermute | solution.py:421
  87.1 10.3 %collective-permute-done.22.refs_3_ = bf16[1344,128]{1,0:T(8,128)(2,1)} collective-permute-done((bf16[1344,128]{1,0:T(8,128)(2,1)}, bf16[1344,128]{1,0:T(8,128)(2,1)}, u32[]{:S(2)}, u32[]{:S(2)}) %collective-permute-start.22) | collective-permute-done | bytes 344096 | tf_op jit(solution)/shard_map/ppermute | solution.py:379
  99.4 2.0 %away_sum.1 = bf16[1344,128]{1,0:T(8,128)(2,1)} custom-call(bf16[1344,128]{1,0:T(8,128)(2,1)S(1)} %copy-done.10, bf16[1344,128]{1,0:T(8,128)(2,1)S(1)} %copy-done.12, bf16[1344,128]{1,0:T(8,128)(2,1)} %collective-permute-done.21.refs_2_, bf16[1344,128]{1,0:T(8,128)(2,1)} %collective-permute-done.22.refs_3_), custom_call_target="tpu_custom_call" | custom-call | tf_op jit(solution)/shard_map/away_sum/pallas_call | solution.py:268
  101.3 2.7 %expand_rows.1.rows = bf16[4,192,1536]{2,1,0:T(8,128)(2,1)S(1)} custom-call(s32[12]{0:T(128)S(1)} %stack.117.order, bf16[8,4,96,128]{3,2,1,0:T(8,128)(2,1)S(1)} %all-to-all-done.rows), custom_call_target="tpu_custom_call" | custom-call | tf_op jit(solution)/shard_map/expand_rows/pallas_call | solution.py:197
  104.1 4.6 %partial_inputs.1 = (bf16[192,1024]{1,0:T(8,128)(2,1)S(1)}, bf16[192,1024]{1,0:T(8,128)(2,1)S(1)}, bf16[192,1024]{1,0:T(8,128)(2,1)S(1)}, bf16[192,1024]{1,0:T(8,128)(2,1)S(1)}) custom-call(bf16[4,192,1536]{2,1,0:T(8,128)(2,1)S(1)} %expand_rows.1.rows, bf16[192,1024]{1,0:T(8,128)(2,1)S(1)} %copy-done, bf16[192,1024]{1,0:T(8,128)(2,1)S(1)} %collective-permute-done.7.refs_1_, ...), custom_call_target="tpu_custom_call" | custom-call | tf_op jit(solution)/shard_map/partial_inputs/pallas_call | solution.py:327
  110.3 7.4 %grads.2 = (bf16[1344,128]{1,0:T(8,128)(2,1)}, bf16[1344,128]{1,0:T(8,128)(2,1)}, bf16[1344,128]{1,0:T(8,128)(2,1)}, bf16[1344,128]{1,0:T(8,128)(2,1)}) custom-call(s32[4]{0:T(128)} %pad_add_fusion.order, bf16[192,1024]{1,0:T(8,128)(2,1)} %get-tuple-element.78.refs_0_.hidden, bf16[192,1024]{1,0:T(8,128)(2,1)} %get-tuple-element.79.feature, ...), custom_call_target="tpu_custom_call" | custom-call | tf_op jit(solution)/shard_map/grads/pallas_call | solution.py:246
  117.7 5.7 %collective-permute-start.14 = (bf16[192,1024]{1,0:T(8,128)(2,1)S(1)}, bf16[192,1024]{1,0:T(8,128)(2,1)S(1)}, u32[]{:S(2)}, u32[]{:S(2)}) collective-permute-start(bf16[192,1024]{1,0:T(8,128)(2,1)S(1)} %copy-done.18), channel_id=1, source_target_pairs={{0,64},{64,128},{128,192},{192,0},{1,65},{65,129},{129,193},{193,1... | collective-permute-start | bytes 1179656 | tf_op jit(solution)/shard_map/ppermute | solution.py:379
  125.5 2.6 %collective-permute-start.18 = (bf16[1344,128]{1,0:T(8,128)(2,1)}, bf16[1344,128]{1,0:T(8,128)(2,1)S(1)}, u32[]{:S(2)}, u32[]{:S(2)}) collective-permute-start(bf16[1344,128]{1,0:T(8,128)(2,1)} %get-tuple-element.82), channel_id=1, source_target_pairs={{0,3},{1,0},{2,1},{3,2},{4,7},{5,4},{6,5},{7,6},{8,11},{9,8},{10,9... | collective-permute-start | bytes 1032200 | tf_op jit(solution)/shard_map/ppermute | solution.py:379
  128.1 5.6 %collective-permute-done.18.refs_2_ = bf16[1344,128]{1,0:T(8,128)(2,1)S(1)} collective-permute-done((bf16[1344,128]{1,0:T(8,128)(2,1)}, bf16[1344,128]{1,0:T(8,128)(2,1)S(1)}, u32[]{:S(2)}, u32[]{:S(2)}) %collective-permute-start.18) | collective-permute-done | bytes 344096 | tf_op jit(solution)/shard_map/ppermute | solution.py:379
  133.7 2.7 %collective-permute-done.19.refs_3_ = bf16[1344,128]{1,0:T(8,128)(2,1)S(1)} collective-permute-done((bf16[1344,128]{1,0:T(8,128)(2,1)}, bf16[1344,128]{1,0:T(8,128)(2,1)S(1)}, u32[]{:S(2)}, u32[]{:S(2)}) %collective-permute-start.19) | collective-permute-done | bytes 344096 | tf_op jit(solution)/shard_map/ppermute | solution.py:379
  137.4 1.9 %unpack.1 = (f32[96,384]{1,0:T(8,128)}, f32[32,128]{1,0:T(8,128)}, f32[32,128]{1,0:T(8,128)}, f32[32,128]{1,0:T(8,128)}, f32[96,640]{1,0:T(8,128)}, /*index=5*/f...) custom-call(bf16[1344,128]{1,0:T(8,128)(2,1)S(1)} %copy-done.13, ...), custom_call_target="tpu_custom_call" | custom-call | tf_op jit(solution)/shard_map/unpack/pallas_call | solution.py:300
  139.3 2.5 %collective-permute-done.15.refs_2_ = bf16[192,1024]{1,0:T(8,128)(2,1)S(1)} collective-permute-done((bf16[192,1024]{1,0:T(8,128)(2,1)S(1)}, bf16[192,1024]{1,0:T(8,128)(2,1)S(1)}, u32[]{:S(2)}, u32[]{:S(2)}) %collective-permute-start.15) | collective-permute-done | bytes 393248 | tf_op jit(solution)/shard_map/ppermute | solution.py:379
  141.8 16.9 %collective-permute-done.16.refs_3_ = bf16[192,1024]{1,0:T(8,128)(2,1)S(1)} collective-permute-done((bf16[192,1024]{1,0:T(8,128)(2,1)S(1)}, bf16[192,1024]{1,0:T(8,128)(2,1)S(1)}, u32[]{:S(2)}, u32[]{:S(2)}) %collective-permute-start.16) | collective-permute-done | bytes 393248 | tf_op jit(solution)/shard_map/ppermute | solution.py:379
  (78 shorter events, 25.8 us)
Async XLA Ops:
  2.5 16.2 %collective-permute-start.3 = (bf16[1344,128]{1,0:T(8,128)(2,1)}, bf16[1344,128]{1,0:T(8,128)(2,1)S(1)}, u32[]{:S(2)}, u32[]{:S(2)}) collective-permute-start(bf16[1344,128]{1,0:T(8,128)(2,1)} %pack.1.refs_0_), channel_id=1, source_target_pairs={{0,4},{4,0},{1,5},{5,1},{2,6},{6,2},{3,7},{7,3},{8,12},{12,8},{9,1... | collective-permute-start | bytes 1032200 | tf_op jit(solution)/shard_map/ppermute | solution.py:397
  10.2 11.8 %collective-permute-start = (bf16[1344,128]{1,0:T(8,128)(2,1)}, bf16[1344,128]{1,0:T(8,128)(2,1)S(1)}, u32[]{:S(2)}, u32[]{:S(2)}) collective-permute-start(bf16[1344,128]{1,0:T(8,128)(2,1)} %pack.1.refs_0_), channel_id=1, source_target_pairs={{0,1},{1,2},{2,3},{3,0},{4,5},{5,6},{6,7},{7,4},{8,9},{9,10},{10,1... | collective-permute-start | bytes 1032200 | tf_op jit(solution)/shard_map/ppermute | solution.py:379
  11.5 12.2 %collective-permute-start.1 = (bf16[1344,128]{1,0:T(8,128)(2,1)}, bf16[1344,128]{1,0:T(8,128)(2,1)S(1)}, u32[]{:S(2)}, u32[]{:S(2)}) collective-permute-start(bf16[1344,128]{1,0:T(8,128)(2,1)} %pack.1.refs_0_), channel_id=1, source_target_pairs={{0,3},{1,0},{2,1},{3,2},{4,7},{5,4},{6,5},{7,6},{8,11},{9,8},{10,9... | collective-permute-start | bytes 1032200 | tf_op jit(solution)/shard_map/ppermute | solution.py:379
  12.9 16.0 %collective-permute-start.2 = (bf16[1344,128]{1,0:T(8,128)(2,1)}, bf16[1344,128]{1,0:T(8,128)(2,1)S(1)}, u32[]{:S(2)}, u32[]{:S(2)}) collective-permute-start(bf16[1344,128]{1,0:T(8,128)(2,1)} %pack.1.refs_0_), channel_id=1, source_target_pairs={{0,2},{1,3},{2,0},{3,1},{4,6},{5,7},{6,4},{7,5},{8,10},{9,11},{10,... | collective-permute-start | bytes 1032200 | tf_op jit(solution)/shard_map/ppermute | solution.py:379
  18.6 17.7 %collective-permute-start.4 = (bf16[1344,128]{1,0:T(8,128)(2,1)S(1)}, bf16[1344,128]{1,0:T(8,128)(2,1)S(1)}, u32[]{:S(2)}, u32[]{:S(2)}) collective-permute-start(bf16[1344,128]{1,0:T(8,128)(2,1)S(1)} %collective-permute-done.3.refs_4_), channel_id=1, source_target_pairs={{0,1},{1,2},{2,3},{3,0},{4,5},{5,6},{6,7},{7,4},{8,9},{9,10},{10,1... | collective-permute-start | bytes 1032200 | tf_op jit(solution)/shard_map/ppermute | solution.py:379
  20.5 16.3 %collective-permute-start.5 = (bf16[1344,128]{1,0:T(8,128)(2,1)S(1)}, bf16[1344,128]{1,0:T(8,128)(2,1)S(1)}, u32[]{:S(2)}, u32[]{:S(2)}) collective-permute-start(bf16[1344,128]{1,0:T(8,128)(2,1)S(1)} %collective-permute-done.3.refs_4_), channel_id=1, source_target_pairs={{0,3},{1,0},{2,1},{3,2},{4,7},{5,4},{6,5},{7,6},{8,11},{9,8},{10,9... | collective-permute-start | bytes 1032200 | tf_op jit(solution)/shard_map/ppermute | solution.py:379
  22.0 21.7 %collective-permute-start.6 = (bf16[1344,128]{1,0:T(8,128)(2,1)S(1)}, bf16[1344,128]{1,0:T(8,128)(2,1)S(1)}, u32[]{:S(2)}, u32[]{:S(2)}) collective-permute-start(bf16[1344,128]{1,0:T(8,128)(2,1)S(1)} %collective-permute-done.3.refs_4_), channel_id=1, source_target_pairs={{0,2},{1,3},{2,0},{3,1},{4,6},{5,7},{6,4},{7,5},{8,10},{9,11},{10,... | collective-permute-start | bytes 1032200 | tf_op jit(solution)/shard_map/ppermute | solution.py:379
  60.8 24.9 %collective-permute-start.7 = (bf16[192,1024]{1,0:T(8,128)(2,1)}, bf16[192,1024]{1,0:T(8,128)(2,1)S(1)}, u32[]{:S(2)}, u32[]{:S(2)}) collective-permute-start(bf16[192,1024]{1,0:T(8,128)(2,1)} %get-tuple-element.78.refs_0_.hidden), channel_id=1, source_target_pairs={{0,16},{16,32},{32,48},{48,0},{1,17},{17,33},{33,49},{49,1},{2,18}... | collective-permute-start | bytes 1179656 | tf_op jit(solution)/shard_map/ppermute | solution.py:379
  62.1 23.7 %collective-permute-start.8 = (bf16[192,1024]{1,0:T(8,128)(2,1)}, bf16[192,1024]{1,0:T(8,128)(2,1)S(1)}, u32[]{:S(2)}, u32[]{:S(2)}) collective-permute-start(bf16[192,1024]{1,0:T(8,128)(2,1)} %get-tuple-element.78.refs_0_.hidden), channel_id=1, source_target_pairs={{0,48},{16,0},{32,16},{48,32},{1,49},{17,1},{33,17},{49,33},{2,50}... | collective-permute-start | bytes 1179656 | tf_op jit(solution)/shard_map/ppermute | solution.py:379
  63.7 22.6 %collective-permute-start.9 = (bf16[192,1024]{1,0:T(8,128)(2,1)}, bf16[192,1024]{1,0:T(8,128)(2,1)S(1)}, u32[]{:S(2)}, u32[]{:S(2)}) collective-permute-start(bf16[192,1024]{1,0:T(8,128)(2,1)} %get-tuple-element.78.refs_0_.hidden), channel_id=1, source_target_pairs={{0,32},{16,48},{32,0},{48,16},{1,33},{17,49},{33,1},{49,17},{2,34}... | collective-permute-start | bytes 1179656 | tf_op jit(solution)/shard_map/ppermute | solution.py:379
  73.0 9.5 %collective-permute-start.20 = (bf16[1344,128]{1,0:T(8,128)(2,1)}, bf16[1344,128]{1,0:T(8,128)(2,1)S(1)}, u32[]{:S(2)}, u32[]{:S(2)}) collective-permute-start(bf16[1344,128]{1,0:T(8,128)(2,1)} %get-tuple-element.85), channel_id=1, source_target_pairs={{0,1},{1,2},{2,3},{3,0},{4,5},{5,6},{6,7},{7,4},{8,9},{9,10},{10,1... | collective-permute-start | bytes 1032200 | tf_op jit(solution)/shard_map/ppermute | solution.py:379
  73.7 12.7 %collective-permute-start.21 = (bf16[1344,128]{1,0:T(8,128)(2,1)}, bf16[1344,128]{1,0:T(8,128)(2,1)}, u32[]{:S(2)}, u32[]{:S(2)}) collective-permute-start(bf16[1344,128]{1,0:T(8,128)(2,1)} %get-tuple-element.86), channel_id=1, source_target_pairs={{0,3},{1,0},{2,1},{3,2},{4,7},{5,4},{6,5},{7,6},{8,11},{9,8},{10,9... | collective-permute-start | bytes 1032200 | tf_op jit(solution)/shard_map/ppermute | solution.py:379
  75.8 25.6 %all-to-all-start = ((bf16[8,4,96,128]{3,2,1,0:T(8,128)(2,1)}), bf16[8,4,96,128]{3,2,1,0:T(8,128)(2,1)S(1)}, u32[]{:S(2)}, u32[]{:S(2)}) async-start(bf16[8,4,96,128]{3,2,1,0:T(8,128)(2,1)} %send_rows.1), calls=%async_computation | async-start | bytes 1572864 | tf_op jit(solution)/shard_map/all_to_all | solution.py:417
  83.2 20.8 %collective-permute-start.10 = (bf16[192,1024]{1,0:T(8,128)(2,1)S(1)}, bf16[192,1024]{1,0:T(8,128)(2,1)S(1)}, u32[]{:S(2)}, u32[]{:S(2)}) collective-permute-start(bf16[192,1024]{1,0:T(8,128)(2,1)S(1)} %copy-done), channel_id=1, source_target_pairs={{0,8},{8,0},{1,9},{9,1},{2,10},{10,2},{3,11},{11,3},{4,12},{12,4},... | collective-permute-start | bytes 1179656 | tf_op jit(solution)/shard_map/ppermute | solution.py:421
  85.8 18.3 %collective-permute-start.11 = (bf16[192,1024]{1,0:T(8,128)(2,1)S(1)}, bf16[192,1024]{1,0:T(8,128)(2,1)S(1)}, u32[]{:S(2)}, u32[]{:S(2)}) collective-permute-start(bf16[192,1024]{1,0:T(8,128)(2,1)S(1)} %collective-permute-done.7.refs_1_), channel_id=1, source_target_pairs={{0,8},{8,0},{1,9},{9,1},{2,10},{10,2},{3,11},{11,3},{4,12},{12,4},... | collective-permute-start | bytes 1179656 | tf_op jit(solution)/shard_map/ppermute | solution.py:421
  85.8 18.2 %collective-permute-start.12 = (bf16[192,1024]{1,0:T(8,128)(2,1)S(1)}, bf16[192,1024]{1,0:T(8,128)(2,1)S(1)}, u32[]{:S(2)}, u32[]{:S(2)}) collective-permute-start(bf16[192,1024]{1,0:T(8,128)(2,1)S(1)} %collective-permute-done.8.refs_2_), channel_id=1, source_target_pairs={{0,8},{8,0},{1,9},{9,1},{2,10},{10,2},{3,11},{11,3},{4,12},{12,4},... | collective-permute-start | bytes 1179656 | tf_op jit(solution)/shard_map/ppermute | solution.py:421
  86.3 17.8 %collective-permute-start.13 = (bf16[192,1024]{1,0:T(8,128)(2,1)S(1)}, bf16[192,1024]{1,0:T(8,128)(2,1)}, u32[]{:S(2)}, u32[]{:S(2)}) collective-permute-start(bf16[192,1024]{1,0:T(8,128)(2,1)S(1)} %collective-permute-done.9.refs_3_), channel_id=1, source_target_pairs={{0,8},{8,0},{1,9},{9,1},{2,10},{10,2},{3,11},{11,3},{4,12},{12,4},... | collective-permute-start | bytes 1179656 | tf_op jit(solution)/shard_map/ppermute | solution.py:421
  86.4 11.0 %collective-permute-start.22 = (bf16[1344,128]{1,0:T(8,128)(2,1)}, bf16[1344,128]{1,0:T(8,128)(2,1)}, u32[]{:S(2)}, u32[]{:S(2)}) collective-permute-start(bf16[1344,128]{1,0:T(8,128)(2,1)} %get-tuple-element.87), channel_id=1, source_target_pairs={{0,2},{1,3},{2,0},{3,1},{4,6},{5,7},{6,4},{7,5},{8,10},{9,11},{10,... | collective-permute-start | bytes 1032200 | tf_op jit(solution)/shard_map/ppermute | solution.py:379
  101.3 24.1 %collective-permute-start.23 = (bf16[1344,128]{1,0:T(8,128)(2,1)}, bf16[1344,128]{1,0:T(8,128)(2,1)}, u32[]{:S(2)}, u32[]{:S(2)}) collective-permute-start(bf16[1344,128]{1,0:T(8,128)(2,1)} %away_sum.1), channel_id=1, source_target_pairs={{0,4},{4,0},{1,5},{5,1},{2,6},{6,2},{3,7},{7,3},{8,12},{12,8},{9,1... | collective-permute-start | bytes 1032200 | tf_op jit(solution)/shard_map/ppermute | solution.py:424
  117.6 10.4 %collective-permute-start.17 = (bf16[1344,128]{1,0:T(8,128)(2,1)}, bf16[1344,128]{1,0:T(8,128)(2,1)S(1)}, u32[]{:S(2)}, u32[]{:S(2)}) collective-permute-start(bf16[1344,128]{1,0:T(8,128)(2,1)} %get-tuple-element.81), channel_id=1, source_target_pairs={{0,1},{1,2},{2,3},{3,0},{4,5},{5,6},{6,7},{7,4},{8,9},{9,10},{10,1... | collective-permute-start | bytes 1032200 | tf_op jit(solution)/shard_map/ppermute | solution.py:379
  117.7 21.6 %collective-permute-start.14 = (bf16[192,1024]{1,0:T(8,128)(2,1)S(1)}, bf16[192,1024]{1,0:T(8,128)(2,1)S(1)}, u32[]{:S(2)}, u32[]{:S(2)}) collective-permute-start(bf16[192,1024]{1,0:T(8,128)(2,1)S(1)} %copy-done.18), channel_id=1, source_target_pairs={{0,64},{64,128},{128,192},{192,0},{1,65},{65,129},{129,193},{193,1... | collective-permute-start | bytes 1179656 | tf_op jit(solution)/shard_map/ppermute | solution.py:379
  123.5 18.4 %collective-permute-start.15 = (bf16[192,1024]{1,0:T(8,128)(2,1)S(1)}, bf16[192,1024]{1,0:T(8,128)(2,1)S(1)}, u32[]{:S(2)}, u32[]{:S(2)}) collective-permute-start(bf16[192,1024]{1,0:T(8,128)(2,1)S(1)} %copy-done.16), channel_id=1, source_target_pairs={{0,192},{64,0},{128,64},{192,128},{1,193},{65,1},{129,65},{193,129... | collective-permute-start | bytes 1179656 | tf_op jit(solution)/shard_map/ppermute | solution.py:379
  124.0 34.8 %collective-permute-start.16 = (bf16[192,1024]{1,0:T(8,128)(2,1)S(1)}, bf16[192,1024]{1,0:T(8,128)(2,1)S(1)}, u32[]{:S(2)}, u32[]{:S(2)}) collective-permute-start(bf16[192,1024]{1,0:T(8,128)(2,1)S(1)} %get-tuple-element.73), channel_id=1, source_target_pairs={{0,128},{64,192},{128,0},{192,64},{1,129},{65,193},{129,1},{193,65... | collective-permute-start | bytes 1179656 | tf_op jit(solution)/shard_map/ppermute | solution.py:379
  128.1 8.3 %collective-permute-start.19 = (bf16[1344,128]{1,0:T(8,128)(2,1)}, bf16[1344,128]{1,0:T(8,128)(2,1)S(1)}, u32[]{:S(2)}, u32[]{:S(2)}) collective-permute-start(bf16[1344,128]{1,0:T(8,128)(2,1)} %get-tuple-element.83), channel_id=1, source_target_pairs={{0,2},{1,3},{2,0},{3,1},{4,6},{5,7},{6,4},{7,5},{8,10},{9,11},{10,... | collective-permute-start | bytes 1032200 | tf_op jit(solution)/shard_map/ppermute | solution.py:379
  (20 other events, 238.8 us)

commit v5 on v4

--- a/solution.py
+++ b/solution.py
@@ -167,7 +167,7 @@
             out_specs=pl.BlockSpec((8, 4, WIDE, LANES), lambda i, p: (0, 0, 0, 0)),
         ),
         out_shape=jax.ShapeDtypeStruct((8, 4, WIDE, LANES), BF16),
-        compiler_params=pltpu.CompilerParams(vmem_limit_bytes=VMEM),
+        compiler_params=pltpu.CompilerParams(vmem_limit_bytes=MOST),
         name="send_rows",
     )(place, *gathered)
 
@@ -268,7 +268,7 @@
     return pl.pallas_call(
         away_kernel,
         out_shape=jax.ShapeDtypeStruct((ROWS, LANES), BF16),
-        compiler_params=pltpu.CompilerParams(vmem_limit_bytes=VMEM),
+        compiler_params=pltpu.CompilerParams(vmem_limit_bytes=MOST),
         name="away_sum",
     )(*parts)
 
@@ -401,7 +401,7 @@
     ).astype(jnp.int32)
 
     heads = [(y + shift) & 3 for shift in (0,) + SHIFTS]
-    order_away = jnp.stack([(1 - zh) * 4 + head for head in heads]).astype(jnp.int32)
+    order_away = ((1 - zh) * 4 + jnp.arange(4)).astype(jnp.int32)
     order_near = jnp.stack([zh * 4 + head for head in heads]).astype(jnp.int32)
     zl = lax.axis_index("zl")
     core = lax.axis_index("core")
@@ -420,8 +420,9 @@
     hidden_all = around(hidden, "x")
     hidden_all = hidden_all + [lax.ppermute(block, "core", SWAP) for block in hidden_all]
 
-    away = turned(grads(order_away, hidden, feature, acts, cotangent))
-    other = lax.ppermute(away_sum(away), "zh", SWAP)
+    away = jnp.stack(grads(order_away, hidden, feature, acts, cotangent))
+    away = lax.all_to_all(away, "y", split_axis=0, concat_axis=0, tiled=True)
+    other = lax.ppermute(away_sum([away[j] for j in range(4)]), "zh", SWAP)
 
     parts = partial_inputs(expand(order_rows, rows), hidden_all)
     parts, hidden, feature = lax.optimization_barrier((parts, hidden, feature))

time: 160 us -> 170 us (1.062)
  starting transfers between devices: 44.3 us -> 48.9 us
  waiting for transfers between devices: 62.1 us -> 65.8 us
  other arithmetic: 1.18 us -> 3.71 us
  local copies, waits for them, and re-layouts: 6.4 us -> 3.89 us
    unnamed x38 -> x22, local copies, waits for them, and re-layouts: 6.22 us -> 0.77 us
    ppermute x18 -> x15, starting transfers between devices: 26.8 us -> 21.6 us  [turn(): return lax.ppermute(block, axis, [(i, (i + shift) % 4) for i in range(4)])]
    all_to_all x0 -> x1, starting transfers between devices: none -> 4.49 us  [body(): away = lax.all_to_all(away, 'y', split_axis=0, concat_axis=0, tiled=True)]
    ppermute x1, starting transfers between devices: 0.01 us -> 4.4 us  [body(): other = lax.ppermute(away_sum([away[j] for j in range(4)]), 'zh', SWAP)]
    ppermute x18 -> x15, waiting for transfers between devices: 58 us -> 61.8 us  [turn(): return lax.ppermute(block, axis, [(i, (i + shift) % 4) for i in range(4)])]
    squeeze x0 -> x1, local copies, waits for them, and re-layouts: none -> 2.43 us  [body(): other = lax.ppermute(away_sum([away[j] for j in range(4)]), 'zh', SWAP)]
    another operation x1, other arithmetic: 0.59 us -> 2.61 us  [body(): away = jnp.stack(grads(order_away, hidden, feature, acts, cotangent))]
  transfers between devices with their start and end apart: 25 -> 23, of which waited for: 10 -> 9; matrix products, arithmetic and copies ran while one was open for 1% -> 4% of each run, Pallas kernels for 16% -> 24%
where the time goes in v5:
time: 170 us; the launch traced here: 169 us
  waiting for transfers between devices  65.8 us (39%)
  starting transfers between devices  48.9 us (29%)
  Pallas kernels  46.3 us (27%)
  local copies, waits for them, and re-layouts  3.89 us (2%)
  other arithmetic  3.71 us (2%)
    ppermute x15, waiting for transfers between devices, turn(): return lax.ppermute(block, axis, [(i, (i + shift) % 4) for i in range(4)])  61.8 us
    ppermute x15, starting transfers between devices, turn(): return lax.ppermute(block, axis, [(i, (i + shift) % 4) for i in range(4)])  21.6 us
    pallas_call x2, Pallas kernels, grads(): pl.pallas_call(grads_kernel, in_specs=[pl.BlockSpec(memory_space=pltpu.SM...  14.5 us
    pallas_call x1, Pallas kernels, forward(): pl.pallas_call(forward_kernel, in_specs=[pl.BlockSpec(memory_space=pltpu....  14.3 us
    ppermute x1, starting transfers between devices, body(): gathered = around(own) + around(lax.ppermute(own, 'zh', SWAP))  7.74 us
    all_to_all x1, starting transfers between devices, body(): lax.all_to_all(rows, ('x', 'core'), split_axis=0, concat_axis=0, tiled=True)  6.16 us
    pallas_call x1, Pallas kernels, partial_inputs(): pl.pallas_call(partial_kernel, grid=(4,), in_specs=[pl.BlockSpec((1, COLS...  5.65 us
    all_to_all x1, starting transfers between devices, body(): away = lax.all_to_all(away, 'y', split_axis=0, concat_axis=0, tiled=True)  4.49 us
  transfers between devices with their start and end apart: 23, of which 9 were waited for; matrix products, arithmetic and copies ran while one was open for 4% of the time, Pallas kernels for 24%

profile of v5, /device:TPU:1, one launch (start us, length us, event | category | flops | bytes accessed | tf_op | source)
XLA Modules:
  0.0 169.4 jit_solution(1246473303073065213)
XLA Ops:
  0.6 1.8 %pack.1.refs_0_ = bf16[1344,128]{1,0:T(8,128)(2,1)} custom-call(bf16[96,384]{1,0:T(8,128)(2,1)} %bitcast.61, bf16[32,128]{1,0:T(8,128)(2,1)} %bitcast.65, bf16[32,128]{1,0:T(8,128)(2,1)} %bitcast.66, bf16[32,128]{1,0:T(8,128)(2,1)} %bitcast.67, bf16[96,640]{1,0:T(8,128)(2,1)} %bitcast.60, bf16[32,640]{1,0:T(8,128)(2,1)} %bitcast.62, ...), custom_call_target="tpu_custom_call" | custom-call | tf_op jit(solution)/shard_map/pack/pallas_call | solution.py:59
  2.5 7.7 %collective-permute-start.3 = (bf16[1344,128]{1,0:T(8,128)(2,1)}, bf16[1344,128]{1,0:T(8,128)(2,1)S(1)}, u32[]{:S(2)}, u32[]{:S(2)}) collective-permute-start(bf16[1344,128]{1,0:T(8,128)(2,1)} %pack.1.refs_0_), channel_id=1, source_target_pairs={{0,4},{4,0},{1,5},{5,1},{2,6},{6,2},{3,7},{7,3},{8,12},{12,8},{9,1... | collective-permute-start | bytes 1032200 | tf_op jit(solution)/shard_map/ppermute | solution.py:397
  14.6 4.1 %collective-permute-done.3.refs_4_ = bf16[1344,128]{1,0:T(8,128)(2,1)S(1)} collective-permute-done((bf16[1344,128]{1,0:T(8,128)(2,1)}, bf16[1344,128]{1,0:T(8,128)(2,1)S(1)}, u32[]{:S(2)}, u32[]{:S(2)}) %collective-permute-start.3) | collective-permute-done | bytes 344096 | tf_op jit(solution)/shard_map/ppermute | solution.py:397
  18.7 1.9 %collective-permute-start.4 = (bf16[1344,128]{1,0:T(8,128)(2,1)S(1)}, bf16[1344,128]{1,0:T(8,128)(2,1)S(1)}, u32[]{:S(2)}, u32[]{:S(2)}) collective-permute-start(bf16[1344,128]{1,0:T(8,128)(2,1)S(1)} %collective-permute-done.3.refs_4_), channel_id=1, source_target_pairs={{0,1},{1,2},{2,3},{3,0},{4,5},{5,6},{6,7},{7,4},{8,9},{9,10},{10,1... | collective-permute-start | bytes 1032200 | tf_op jit(solution)/shard_map/ppermute | solution.py:379
  24.2 4.7 %collective-permute-done.2.refs_3_ = bf16[1344,128]{1,0:T(8,128)(2,1)S(1)} collective-permute-done((bf16[1344,128]{1,0:T(8,128)(2,1)}, bf16[1344,128]{1,0:T(8,128)(2,1)S(1)}, u32[]{:S(2)}, u32[]{:S(2)}) %collective-permute-start.2) | collective-permute-done | bytes 344096 | tf_op jit(solution)/shard_map/ppermute | solution.py:379
  28.9 7.5 %collective-permute-done.4.refs_5_ = bf16[1344,128]{1,0:T(8,128)(2,1)S(1)} collective-permute-done((bf16[1344,128]{1,0:T(8,128)(2,1)S(1)}, bf16[1344,128]{1,0:T(8,128)(2,1)S(1)}, u32[]{:S(2)}, u32[]{:S(2)}) %collective-permute-start.4) | collective-permute-done | bytes 344096 | tf_op jit(solution)/shard_map/ppermute | solution.py:379
  36.8 6.8 %collective-permute-done.6.refs_7_ = bf16[1344,128]{1,0:T(8,128)(2,1)S(1)} collective-permute-done((bf16[1344,128]{1,0:T(8,128)(2,1)S(1)}, bf16[1344,128]{1,0:T(8,128)(2,1)S(1)}, u32[]{:S(2)}, u32[]{:S(2)}) %collective-permute-start.6) | collective-permute-done | bytes 344096 | tf_op jit(solution)/shard_map/ppermute | solution.py:379
  44.4 3.2 %send_rows.1 = bf16[8,4,96,128]{3,2,1,0:T(8,128)(2,1)} custom-call(s32[9]{0:T(128)} %stack.106.place, bf16[1344,128]{1,0:T(8,128)(2,1)} %pack.1.refs_0_, bf16[1344,128]{1,0:T(8,128)(2,1)} %copy-done.4, bf16[1344,128]{1,0:T(8,128)(2,1)} %copy-done.5, bf16[1344,128]{1,0:T(8,128)(2,1)} %copy-done.6, bf16[1344,128]{1,0:T(8,128)(2,1)} %copy-done.3, ...), custom_call_target="tpu_custom_call" | custom-call | tf_op jit(solution)/shard_map/send_rows/pallas_call | solution.py:161
  47.7 6.2 %all-to-all-start = ((bf16[8,4,96,128]{3,2,1,0:T(8,128)(2,1)}), bf16[8,4,96,128]{3,2,1,0:T(8,128)(2,1)S(1)}, u32[]{:S(2)}, u32[]{:S(2)}) async-start(bf16[8,4,96,128]{3,2,1,0:T(8,128)(2,1)} %send_rows.1), calls=%async_computation | async-start | bytes 1572864 | tf_op jit(solution)/shard_map/all_to_all | solution.py:417
  54.4 14.3 %forward.1 = (bf16[192,1024]{1,0:T(8,128)(2,1)}, bf16[192,1024]{1,0:T(8,128)(2,1)}, f32[192,1024]{1,0:T(8,128)}) custom-call(s32[9]{0:T(128)} %stack.106.place, bf16[1344,128]{1,0:T(8,128)(2,1)} %pack.1.refs_0_, bf16[1344,128]{1,0:T(8,128)(2,1)} %copy-done.4, bf16[1344,128]{1,0:T(8,128)(2,1)} %copy-done.5, bf16[1344,128]{1,0:T(8,128)(2,1)} %copy-done.6, ...), custom_call_target="tpu_custom_call" | custom-call | tf_op jit(solution)/shard_map/forward/pallas_call | solution.py:124
  68.6 7.3 %grads.3 = (bf16[1344,128]{1,0:T(8,128)(2,1)}, bf16[1344,128]{1,0:T(8,128)(2,1)}, bf16[1344,128]{1,0:T(8,128)(2,1)}, bf16[1344,128]{1,0:T(8,128)(2,1)}) custom-call(s32[4]{0:T(128)} %iota_add_fusion.order, bf16[192,1024]{1,0:T(8,128)(2,1)} %get-tuple-element.78.refs_0_.hidden, bf16[192,1024]{1,0:T(8,128)(2,1)} %get-tuple-element.79.feature, ...), custom_call_target="tpu_custom_call" | custom-call | tf_op jit(solution)/shard_map/grads/pallas_call | solution.py:246
  75.9 2.6 %pad_maximum_fusion = bf16[4,1344,128]{2,1,0:T(8,128)(2,1)} fusion(bf16[1,1344,128]{2,1,0:T(8,128)(2,1)} %bitcast.59, bf16[1,1344,128]{2,1,0:T(8,128)(2,1)} %bitcast.58, bf16[1,1344,128]{2,1,0:T(8,128)(2,1)} %bitcast.57, bf16[1,1344,128]{2,1,0:T(8,128)(2,1)} %bitcast.56), kind=kLoop, calls=%fused_computation | loop fusion | flops 2064384 | bytes 2752512 | tf_op jit(solution)/shard_map/stack | solution.py:423
  78.5 4.5 %all-to-all-start.1 = ((bf16[4,1344,128]{2,1,0:T(8,128)(2,1)}), bf16[4,1344,128]{2,1,0:T(8,128)(2,1)}, u32[]{:S(2)}, u32[]{:S(2)}) async-start(bf16[4,1344,128]{2,1,0:T(8,128)(2,1)} %pad_maximum_fusion), calls=%async_computation.1 | async-start | bytes 2752512 | tf_op jit(solution)/shard_map/all_to_all | solution.py:424
  88.6 6.4 %collective-permute-done.7.refs_1_ = bf16[192,1024]{1,0:T(8,128)(2,1)S(1)} collective-permute-done((bf16[192,1024]{1,0:T(8,128)(2,1)S(1)}, bf16[192,1024]{1,0:T(8,128)(2,1)S(1)}, u32[]{:S(2)}, u32[]{:S(2)}) %collective-permute-start.7) | collective-permute-done | bytes 393248 | tf_op jit(solution)/shard_map/ppermute | solution.py:379
  97.1 7.1 %collective-permute-done.9.refs_3_ = bf16[192,1024]{1,0:T(8,128)(2,1)S(1)} collective-permute-done((bf16[192,1024]{1,0:T(8,128)(2,1)S(1)}, bf16[192,1024]{1,0:T(8,128)(2,1)S(1)}, u32[]{:S(2)}, u32[]{:S(2)}) %collective-permute-start.9) | collective-permute-done | bytes 393248 | tf_op jit(solution)/shard_map/ppermute | solution.py:379
  106.0 2.7 %expand_rows.1.rows = bf16[4,192,1536]{2,1,0:T(8,128)(2,1)S(1)} custom-call(s32[12]{0:T(128)S(1)} %stack.119.order, bf16[8,4,96,128]{3,2,1,0:T(8,128)(2,1)S(1)} %all-to-all-done.rows), custom_call_target="tpu_custom_call" | custom-call | tf_op jit(solution)/shard_map/expand_rows/pallas_call | solution.py:197
  108.8 5.7 %partial_inputs.1 = (bf16[192,1024]{1,0:T(8,128)(2,1)S(1)}, bf16[192,1024]{1,0:T(8,128)(2,1)}, bf16[192,1024]{1,0:T(8,128)(2,1)}, bf16[192,1024]{1,0:T(8,128)(2,1)}) custom-call(bf16[4,192,1536]{2,1,0:T(8,128)(2,1)S(1)} %expand_rows.1.rows, bf16[192,1024]{1,0:T(8,128)(2,1)S(1)} %copy-done, bf16[192,1024]{1,0:T(8,128)(2,1)S(1)} %collective-permute-done.7.refs_1_, ...), custom_call_target="tpu_custom_call" | custom-call | tf_op jit(solution)/shard_map/partial_inputs/pallas_call | solution.py:327
  115.6 2.2 %collective-permute-start.15 = (bf16[192,1024]{1,0:T(8,128)(2,1)}, bf16[192,1024]{1,0:T(8,128)(2,1)S(1)}, u32[]{:S(2)}, u32[]{:S(2)}) collective-permute-start(bf16[192,1024]{1,0:T(8,128)(2,1)} %get-tuple-element.72), channel_id=1, source_target_pairs={{0,192},{64,0},{128,64},{192,128},{1,193},{65,1},{129,65},{193,129... | collective-permute-start | bytes 1179656 | tf_op jit(solution)/shard_map/ppermute | solution.py:379
  117.8 7.3 %grads.2 = (bf16[1344,128]{1,0:T(8,128)(2,1)}, bf16[1344,128]{1,0:T(8,128)(2,1)}, bf16[1344,128]{1,0:T(8,128)(2,1)}, bf16[1344,128]{1,0:T(8,128)(2,1)}) custom-call(s32[4]{0:T(128)} %pad_add_fusion.order, bf16[192,1024]{1,0:T(8,128)(2,1)} %get-tuple-element.78.refs_0_.hidden, bf16[192,1024]{1,0:T(8,128)(2,1)} %get-tuple-element.79.feature, ...), custom_call_target="tpu_custom_call" | custom-call | tf_op jit(solution)/shard_map/grads/pallas_call | solution.py:246
  127.8 2.4 %slice_bitcast_fusion = (bf16[1344,128]{1,0:T(8,128)(2,1)}, bf16[1344,128]{1,0:T(8,128)(2,1)}, bf16[1344,128]{1,0:T(8,128)(2,1)}, bf16[1344,128]{1,0:T(8,128)(2,1)}) fusion(bf16[4,1344,128]{2,1,0:T(8,128)(2,1)} %all-to-all-done.1), kind=kLoop, calls=%fused_computation.1 | loop fusion | bytes 2752512 | tf_op jit(solution)/shard_map/squeeze | solution.py:425
  130.3 2.3 %away_sum.1 = bf16[1344,128]{1,0:T(8,128)(2,1)} custom-call(bf16[1344,128]{1,0:T(8,128)(2,1)} %get-tuple-element.99.refs_0_, bf16[1344,128]{1,0:T(8,128)(2,1)} %get-tuple-element.98.refs_1_, bf16[1344,128]{1,0:T(8,128)(2,1)} %get-tuple-element.97.refs_2_, bf16[1344,128]{1,0:T(8,128)(2,1)} %get-tuple-element.96.refs_3_), custom_call_target="tpu_custom_call" | custom-call | tf_op jit(solution)/shard_map/away_sum/pallas_call | solution.py:268
  132.6 1.7 %collective-permute-start.19 = (bf16[1344,128]{1,0:T(8,128)(2,1)S(1)}, bf16[1344,128]{1,0:T(8,128)(2,1)S(1)}, u32[]{:S(2)}, u32[]{:S(2)}) collective-permute-start(bf16[1344,128]{1,0:T(8,128)(2,1)S(1)} %copy-done.10), channel_id=1, source_target_pairs={{0,2},{1,3},{2,0},{3,1},{4,6},{5,7},{6,4},{7,5},{8,10},{9,11},{10,... | collective-permute-start | bytes 1032200 | tf_op jit(solution)/shard_map/ppermute | solution.py:379
  134.6 4.4 %collective-permute-start.20 = (bf16[1344,128]{1,0:T(8,128)(2,1)}, bf16[1344,128]{1,0:T(8,128)(2,1)S(1)}, u32[]{:S(2)}, u32[]{:S(2)}) collective-permute-start(bf16[1344,128]{1,0:T(8,128)(2,1)} %away_sum.1), channel_id=1, source_target_pairs={{0,4},{4,0},{1,5},{5,1},{2,6},{6,2},{3,7},{7,3},{8,12},{12,8},{9,1... | collective-permute-start | bytes 1032200 | tf_op jit(solution)/shard_map/ppermute | solution.py:425
  139.0 28.5 %collective-permute-done.16.refs_3_ = bf16[192,1024]{1,0:T(8,128)(2,1)S(1)} collective-permute-done((bf16[192,1024]{1,0:T(8,128)(2,1)}, bf16[192,1024]{1,0:T(8,128)(2,1)S(1)}, u32[]{:S(2)}, u32[]{:S(2)}) %collective-permute-start.16) | collective-permute-done | bytes 393248 | tf_op jit(solution)/shard_map/ppermute | solution.py:379
  (60 shorter events, 25.5 us)
Async XLA Ops:
  2.5 16.2 %collective-permute-start.3 = (bf16[1344,128]{1,0:T(8,128)(2,1)}, bf16[1344,128]{1,0:T(8,128)(2,1)S(1)}, u32[]{:S(2)}, u32[]{:S(2)}) collective-permute-start(bf16[1344,128]{1,0:T(8,128)(2,1)} %pack.1.refs_0_), channel_id=1, source_target_pairs={{0,4},{4,0},{1,5},{5,1},{2,6},{6,2},{3,7},{7,3},{8,12},{12,8},{9,1... | collective-permute-start | bytes 1032200 | tf_op jit(solution)/shard_map/ppermute | solution.py:397
  10.2 11.8 %collective-permute-start = (bf16[1344,128]{1,0:T(8,128)(2,1)}, bf16[1344,128]{1,0:T(8,128)(2,1)S(1)}, u32[]{:S(2)}, u32[]{:S(2)}) collective-permute-start(bf16[1344,128]{1,0:T(8,128)(2,1)} %pack.1.refs_0_), channel_id=1, source_target_pairs={{0,1},{1,2},{2,3},{3,0},{4,5},{5,6},{6,7},{7,4},{8,9},{9,10},{10,1... | collective-permute-start | bytes 1032200 | tf_op jit(solution)/shard_map/ppermute | solution.py:379
  11.5 12.7 %collective-permute-start.1 = (bf16[1344,128]{1,0:T(8,128)(2,1)}, bf16[1344,128]{1,0:T(8,128)(2,1)S(1)}, u32[]{:S(2)}, u32[]{:S(2)}) collective-permute-start(bf16[1344,128]{1,0:T(8,128)(2,1)} %pack.1.refs_0_), channel_id=1, source_target_pairs={{0,3},{1,0},{2,1},{3,2},{4,7},{5,4},{6,5},{7,6},{8,11},{9,8},{10,9... | collective-permute-start | bytes 1032200 | tf_op jit(solution)/shard_map/ppermute | solution.py:379
  13.0 16.0 %collective-permute-start.2 = (bf16[1344,128]{1,0:T(8,128)(2,1)}, bf16[1344,128]{1,0:T(8,128)(2,1)S(1)}, u32[]{:S(2)}, u32[]{:S(2)}) collective-permute-start(bf16[1344,128]{1,0:T(8,128)(2,1)} %pack.1.refs_0_), channel_id=1, source_target_pairs={{0,2},{1,3},{2,0},{3,1},{4,6},{5,7},{6,4},{7,5},{8,10},{9,11},{10,... | collective-permute-start | bytes 1032200 | tf_op jit(solution)/shard_map/ppermute | solution.py:379
  18.7 17.7 %collective-permute-start.4 = (bf16[1344,128]{1,0:T(8,128)(2,1)S(1)}, bf16[1344,128]{1,0:T(8,128)(2,1)S(1)}, u32[]{:S(2)}, u32[]{:S(2)}) collective-permute-start(bf16[1344,128]{1,0:T(8,128)(2,1)S(1)} %collective-permute-done.3.refs_4_), channel_id=1, source_target_pairs={{0,1},{1,2},{2,3},{3,0},{4,5},{5,6},{6,7},{7,4},{8,9},{9,10},{10,1... | collective-permute-start | bytes 1032200 | tf_op jit(solution)/shard_map/ppermute | solution.py:379
  20.5 16.3 %collective-permute-start.5 = (bf16[1344,128]{1,0:T(8,128)(2,1)S(1)}, bf16[1344,128]{1,0:T(8,128)(2,1)S(1)}, u32[]{:S(2)}, u32[]{:S(2)}) collective-permute-start(bf16[1344,128]{1,0:T(8,128)(2,1)S(1)} %collective-permute-done.3.refs_4_), channel_id=1, source_target_pairs={{0,3},{1,0},{2,1},{3,2},{4,7},{5,4},{6,5},{7,6},{8,11},{9,8},{10,9... | collective-permute-start | bytes 1032200 | tf_op jit(solution)/shard_map/ppermute | solution.py:379
  22.0 21.7 %collective-permute-start.6 = (bf16[1344,128]{1,0:T(8,128)(2,1)S(1)}, bf16[1344,128]{1,0:T(8,128)(2,1)S(1)}, u32[]{:S(2)}, u32[]{:S(2)}) collective-permute-start(bf16[1344,128]{1,0:T(8,128)(2,1)S(1)} %collective-permute-done.3.refs_4_), channel_id=1, source_target_pairs={{0,2},{1,3},{2,0},{3,1},{4,6},{5,7},{6,4},{7,5},{8,10},{9,11},{10,... | collective-permute-start | bytes 1032200 | tf_op jit(solution)/shard_map/ppermute | solution.py:379
  47.7 30.8 %all-to-all-start = ((bf16[8,4,96,128]{3,2,1,0:T(8,128)(2,1)}), bf16[8,4,96,128]{3,2,1,0:T(8,128)(2,1)S(1)}, u32[]{:S(2)}, u32[]{:S(2)}) async-start(bf16[8,4,96,128]{3,2,1,0:T(8,128)(2,1)} %send_rows.1), calls=%async_computation | async-start | bytes 1572864 | tf_op jit(solution)/shard_map/all_to_all | solution.py:417
  78.5 49.3 %all-to-all-start.1 = ((bf16[4,1344,128]{2,1,0:T(8,128)(2,1)}), bf16[4,1344,128]{2,1,0:T(8,128)(2,1)}, u32[]{:S(2)}, u32[]{:S(2)}) async-start(bf16[4,1344,128]{2,1,0:T(8,128)(2,1)} %pad_maximum_fusion), calls=%async_computation.1 | async-start | bytes 2752512 | tf_op jit(solution)/shard_map/all_to_all | solution.py:424
  83.0 12.0 %collective-permute-start.7 = (bf16[192,1024]{1,0:T(8,128)(2,1)S(1)}, bf16[192,1024]{1,0:T(8,128)(2,1)S(1)}, u32[]{:S(2)}, u32[]{:S(2)}) collective-permute-start(bf16[192,1024]{1,0:T(8,128)(2,1)S(1)} %copy-done), channel_id=1, source_target_pairs={{0,16},{16,32},{32,48},{48,0},{1,17},{17,33},{33,49},{49,1},{2,18}... | collective-permute-start | bytes 1179656 | tf_op jit(solution)/shard_map/ppermute | solution.py:379
  84.5 11.4 %collective-permute-start.8 = (bf16[192,1024]{1,0:T(8,128)(2,1)S(1)}, bf16[192,1024]{1,0:T(8,128)(2,1)S(1)}, u32[]{:S(2)}, u32[]{:S(2)}) collective-permute-start(bf16[192,1024]{1,0:T(8,128)(2,1)S(1)} %copy-done), channel_id=1, source_target_pairs={{0,48},{16,0},{32,16},{48,32},{1,49},{17,1},{33,17},{49,33},{2,50}... | collective-permute-start | bytes 1179656 | tf_op jit(solution)/shard_map/ppermute | solution.py:379
  85.8 18.4 %collective-permute-start.9 = (bf16[192,1024]{1,0:T(8,128)(2,1)S(1)}, bf16[192,1024]{1,0:T(8,128)(2,1)S(1)}, u32[]{:S(2)}, u32[]{:S(2)}) collective-permute-start(bf16[192,1024]{1,0:T(8,128)(2,1)S(1)} %copy-done), channel_id=1, source_target_pairs={{0,32},{16,48},{32,0},{48,16},{1,33},{17,49},{33,1},{49,17},{2,34}... | collective-permute-start | bytes 1179656 | tf_op jit(solution)/shard_map/ppermute | solution.py:379
  87.5 21.3 %collective-permute-start.10 = (bf16[192,1024]{1,0:T(8,128)(2,1)S(1)}, bf16[192,1024]{1,0:T(8,128)(2,1)S(1)}, u32[]{:S(2)}, u32[]{:S(2)}) collective-permute-start(bf16[192,1024]{1,0:T(8,128)(2,1)S(1)} %copy-done), channel_id=1, source_target_pairs={{0,8},{8,0},{1,9},{9,1},{2,10},{10,2},{3,11},{11,3},{4,12},{12,4},... | collective-permute-start | bytes 1179656 | tf_op jit(solution)/shard_map/ppermute | solution.py:421
  95.0 13.7 %collective-permute-start.11 = (bf16[192,1024]{1,0:T(8,128)(2,1)S(1)}, bf16[192,1024]{1,0:T(8,128)(2,1)S(1)}, u32[]{:S(2)}, u32[]{:S(2)}) collective-permute-start(bf16[192,1024]{1,0:T(8,128)(2,1)S(1)} %collective-permute-done.7.refs_1_), channel_id=1, source_target_pairs={{0,8},{8,0},{1,9},{9,1},{2,10},{10,2},{3,11},{11,3},{4,12},{12,4},... | collective-permute-start | bytes 1179656 | tf_op jit(solution)/shard_map/ppermute | solution.py:421
  95.8 12.9 %collective-permute-start.12 = (bf16[192,1024]{1,0:T(8,128)(2,1)S(1)}, bf16[192,1024]{1,0:T(8,128)(2,1)S(1)}, u32[]{:S(2)}, u32[]{:S(2)}) collective-permute-start(bf16[192,1024]{1,0:T(8,128)(2,1)S(1)} %collective-permute-done.8.refs_2_), channel_id=1, source_target_pairs={{0,8},{8,0},{1,9},{9,1},{2,10},{10,2},{3,11},{11,3},{4,12},{12,4},... | collective-permute-start | bytes 1179656 | tf_op jit(solution)/shard_map/ppermute | solution.py:421
  104.2 4.6 %collective-permute-start.13 = (bf16[192,1024]{1,0:T(8,128)(2,1)S(1)}, bf16[192,1024]{1,0:T(8,128)(2,1)}, u32[]{:S(2)}, u32[]{:S(2)}) collective-permute-start(bf16[192,1024]{1,0:T(8,128)(2,1)S(1)} %collective-permute-done.9.refs_3_), channel_id=1, source_target_pairs={{0,8},{8,0},{1,9},{9,1},{2,10},{10,2},{3,11},{11,3},{4,12},{12,4},... | collective-permute-start | bytes 1179656 | tf_op jit(solution)/shard_map/ppermute | solution.py:421
  114.5 18.1 %collective-permute-start.14 = (bf16[192,1024]{1,0:T(8,128)(2,1)}, bf16[192,1024]{1,0:T(8,128)(2,1)S(1)}, u32[]{:S(2)}, u32[]{:S(2)}) collective-permute-start(bf16[192,1024]{1,0:T(8,128)(2,1)} %get-tuple-element.71), channel_id=1, source_target_pairs={{0,64},{64,128},{128,192},{192,0},{1,65},{65,129},{129,193},{193,1... | collective-permute-start | bytes 1179656 | tf_op jit(solution)/shard_map/ppermute | solution.py:379
  115.6 19.1 %collective-permute-start.15 = (bf16[192,1024]{1,0:T(8,128)(2,1)}, bf16[192,1024]{1,0:T(8,128)(2,1)S(1)}, u32[]{:S(2)}, u32[]{:S(2)}) collective-permute-start(bf16[192,1024]{1,0:T(8,128)(2,1)} %get-tuple-element.72), channel_id=1, source_target_pairs={{0,192},{64,0},{128,64},{192,128},{1,193},{65,1},{129,65},{193,129... | collective-permute-start | bytes 1179656 | tf_op jit(solution)/shard_map/ppermute | solution.py:379
  117.7 49.8 %collective-permute-start.16 = (bf16[192,1024]{1,0:T(8,128)(2,1)}, bf16[192,1024]{1,0:T(8,128)(2,1)S(1)}, u32[]{:S(2)}, u32[]{:S(2)}) collective-permute-start(bf16[192,1024]{1,0:T(8,128)(2,1)} %get-tuple-element.73), channel_id=1, source_target_pairs={{0,128},{64,192},{128,0},{192,64},{1,129},{65,193},{129,1},{193,65... | collective-permute-start | bytes 1179656 | tf_op jit(solution)/shard_map/ppermute | solution.py:379
  125.1 43.3 %collective-permute-start.17 = (bf16[1344,128]{1,0:T(8,128)(2,1)}, bf16[1344,128]{1,0:T(8,128)(2,1)S(1)}, u32[]{:S(2)}, u32[]{:S(2)}) collective-permute-start(bf16[1344,128]{1,0:T(8,128)(2,1)} %get-tuple-element.81), channel_id=1, source_target_pairs={{0,1},{1,2},{2,3},{3,0},{4,5},{5,6},{6,7},{7,4},{8,9},{9,10},{10,1... | collective-permute-start | bytes 1032200 | tf_op jit(solution)/shard_map/ppermute | solution.py:379
  126.5 41.9 %collective-permute-start.18 = (bf16[1344,128]{1,0:T(8,128)(2,1)}, bf16[1344,128]{1,0:T(8,128)(2,1)S(1)}, u32[]{:S(2)}, u32[]{:S(2)}) collective-permute-start(bf16[1344,128]{1,0:T(8,128)(2,1)} %get-tuple-element.82), channel_id=1, source_target_pairs={{0,3},{1,0},{2,1},{3,2},{4,7},{5,4},{6,5},{7,6},{8,11},{9,8},{10,9... | collective-permute-start | bytes 1032200 | tf_op jit(solution)/shard_map/ppermute | solution.py:379
  130.3 37.3 %copy-start.1 = (f32[192,1024]{1,0:T(8,128)S(1)}, f32[192,1024]{1,0:T(8,128)}, u32[]{:S(2)}) copy-start(f32[192,1024]{1,0:T(8,128)} %get-tuple-element.62.back) | copy-start | bytes 2359300
  132.6 35.9 %collective-permute-start.19 = (bf16[1344,128]{1,0:T(8,128)(2,1)S(1)}, bf16[1344,128]{1,0:T(8,128)(2,1)S(1)}, u32[]{:S(2)}, u32[]{:S(2)}) collective-permute-start(bf16[1344,128]{1,0:T(8,128)(2,1)S(1)} %copy-done.10), channel_id=1, source_target_pairs={{0,2},{1,3},{2,0},{3,1},{4,6},{5,7},{6,4},{7,5},{8,10},{9,11},{10,... | collective-permute-start | bytes 1032200 | tf_op jit(solution)/shard_map/ppermute | solution.py:379
  134.6 33.8 %collective-permute-start.20 = (bf16[1344,128]{1,0:T(8,128)(2,1)}, bf16[1344,128]{1,0:T(8,128)(2,1)S(1)}, u32[]{:S(2)}, u32[]{:S(2)}) collective-permute-start(bf16[1344,128]{1,0:T(8,128)(2,1)} %away_sum.1), channel_id=1, source_target_pairs={{0,4},{4,0},{1,5},{5,1},{2,6},{6,2},{3,7},{7,3},{8,12},{12,8},{9,1... | collective-permute-start | bytes 1032200 | tf_op jit(solution)/shard_map/ppermute | solution.py:425
  (10 other events, 138.5 us)
